TPU v7x, 512 devices: a whole 4x4x16 slice. The times are simulated.
512 devices in a mesh: dp: 16 (over x, y), expert: 32 (over z, core).
Axes of the slice: x: 4, y: 4, z: 16, core: 2. Of those that a mesh axis runs over, the one named last changes fastest.
Arguments:
- tokens: bfloat16 [512, 196, 1280], P(('dp', 'expert')), may hold values from -40 to 40
- router: bfloat16 [1280, 32], replicated, may hold values from -2 to 2
- w_in: bfloat16 [32, 1280, 5120], P('expert', None, 'dp'), may hold values from -0.15625 to 0.15625
- w_out: bfloat16 [32, 5120, 1280], P('expert', 'dp'), may hold values from -0.078125 to 0.078125
- cotangent: bfloat16 [512, 196, 1280], P(('dp', 'expert')), may hold values from -6 to 6
Outputs:
- grad_tokens: bfloat16 [512, 196, 1280], P(('dp', 'expert'))
- grad_router: float32 [1280, 32], replicated
- grad_w_in: bfloat16 [32, 1280, 5120], P('expert', None, 'dp')
- grad_w_out: bfloat16 [32, 5120, 1280], P('expert', 'dp')
All inputs are finite; a program needn't handle non-finite values.
Results may differ from a plain program's by a relative error of at most 0.022.
Values may be sent and summed in bfloat16 or wider, within the bound.
No kernel may reach another device: no remote copies, remote signals or barrier semaphores. Data moves between devices by JAX's collectives and lax.ppermute only.
A program may use at most 64 MiB of HBM per device.

v0:
```python
import jax
import jax.numpy as jnp
from jax import lax
from jax.sharding import PartitionSpec as P


def gelu_slope(x):
    cdf = 0.5 * (1.0 + jax.scipy.special.erf(x * 0.7071067811865476))
    return cdf + x * jnp.exp(-0.5 * x * x) * 0.3989422804014327


def local(tokens, router, w_in, w_out, cotangent):
    logits = jnp.einsum("btd,ds->bts", tokens, router, preferred_element_type=jnp.float32)
    dispatch = jax.nn.softmax(logits, axis=1)
    combine = jax.nn.softmax(logits, axis=2)
    dispatch_bf = dispatch.astype(jnp.bfloat16)
    combine_bf = combine.astype(jnp.bfloat16)
    slot_in = jnp.einsum(
        "bts,btd->bsd", dispatch_bf, tokens, preferred_element_type=jnp.float32
    ).astype(jnp.bfloat16)
    expert_in = lax.all_to_all(slot_in, "expert", split_axis=1, concat_axis=0, tiled=True)
    all_in = lax.all_gather(expert_in, "dp", axis=0, tiled=True)
    pre = jnp.einsum("bed,edh->beh", all_in, w_in, preferred_element_type=jnp.float32)
    hidden = jax.nn.gelu(pre, approximate=False).astype(jnp.bfloat16)
    rows = hidden
    slot_part = lax.psum_scatter(
        jnp.einsum("beh,ehd->bed", rows, w_out, preferred_element_type=jnp.float32).astype(
            jnp.bfloat16
        ),
        "dp",
        scatter_dimension=0,
        tiled=True,
    )
    slot_out = lax.all_to_all(slot_part, "expert", split_axis=0, concat_axis=1, tiled=True)
    g_comb = jnp.einsum("btd,bsd->bts", cotangent, slot_out, preferred_element_type=jnp.float32)
    g_clog = combine * (g_comb - jnp.sum(combine * g_comb, axis=2, keepdims=True))
    g_late = jnp.einsum(
        "bts,btd->bsd", combine_bf, cotangent, preferred_element_type=jnp.float32
    ).astype(jnp.bfloat16)
    g_sout = lax.all_to_all(g_late, "expert", split_axis=1, concat_axis=0, tiled=True)
    g_sall = lax.all_gather(g_sout, "dp", axis=0, tiled=True)
    g_hid = jnp.einsum("bed,ehd->beh", g_sall, w_out, preferred_element_type=jnp.float32)
    g_pre = (g_hid * gelu_slope(pre)).astype(jnp.bfloat16)
    grad_w_out = jnp.einsum(
        "beh,bed->ehd", hidden, g_sall, preferred_element_type=jnp.float32
    ).astype(jnp.bfloat16)
    grad_w_in = jnp.einsum(
        "bed,beh->edh", all_in, g_pre, preferred_element_type=jnp.float32
    ).astype(jnp.bfloat16)
    rows = g_pre
    g_slot_part = lax.psum_scatter(
        jnp.einsum("beh,edh->bed", rows, w_in, preferred_element_type=jnp.float32).astype(
            jnp.bfloat16
        ),
        "dp",
        scatter_dimension=0,
        tiled=True,
    )
    g_slot = lax.all_to_all(g_slot_part, "expert", split_axis=0, concat_axis=1, tiled=True)
    g_disp = jnp.einsum("btd,bsd->bts", tokens, g_slot, preferred_element_type=jnp.float32)
    g_dlog = dispatch * (g_disp - jnp.sum(dispatch * g_disp, axis=1, keepdims=True))
    g_logits = (g_dlog + g_clog).astype(jnp.bfloat16)
    grad_tokens = jnp.einsum(
        "bts,bsd->btd", dispatch_bf, g_slot, preferred_element_type=jnp.float32
    )
    grad_tokens = grad_tokens + jnp.einsum(
        "bts,ds->btd", g_logits, router, preferred_element_type=jnp.float32
    )
    router_term = jnp.einsum("btd,bts->ds", tokens, g_logits, preferred_element_type=jnp.float32)
    grad_router = lax.psum(router_term, ("dp", "expert"))
    return (grad_tokens.astype(jnp.bfloat16), grad_router, grad_w_in, grad_w_out)


def solution(mesh):
    placed = (
        P(("dp", "expert"), None, None),
        P(),
        P("expert", None, "dp"),
        P("expert", "dp", None),
        P(("dp", "expert"), None, None),
    )
    return jax.shard_map(
        local,
        mesh=mesh,
        in_specs=placed,
        out_specs=(
            P(("dp", "expert"), None, None),
            P(),
            P("expert", None, "dp"),
            P("expert", "dp", None),
        ),
        check_vma=False,
    )
```

profile of v0, /device:TPU:1, one launch (start us, length us, event | category | flops | bytes accessed | tf_op | source)
XLA Modules:
  0.0 820.4 jit_solution(10235485146663449798)
XLA Ops:
  7.2 0.0 all-gather.7.cloned.1.call-start
  7.2 1.6 fusion.73
  8.8 0.2 fusion.64
  9.0 1.3 fusion.7
  10.3 0.2 copy.37
  10.4 0.5 broadcast.36
  11.0 1.1 reduce.13
  12.1 30.3 %all_to_all.42 = bf16[32,2,640]{2,1,0:T(2,128)(2,1)S(1)} all-to-all(bf16[32,2,640]{2,1,0:T(2,128)(2,1)S(1)} %reshape.157), channel_id=1, replica_groups=mesh['dp'=16,'expert'=32] {'expert'}, dimensions={0} | all-to-all | bytes 163840 | tf_op jit(solution)/shard_map/all_to_all | solution.py:21
  42.4 0.1 reshape.158
  42.4 0.6 copy.16
  43.1 0.0 all-gather.7.cloned.1.call-update
  43.1 0.0 all-gather.5.cloned.1.call-start
  43.2 0.2 fusion.6
  43.4 0.1 copy.38
  43.5 1.1 reduce.12
  44.6 18.0 %all_to_all.43 = bf16[32,2,640]{2,1,0:T(2,128)(2,1)S(1)} all-to-all(bf16[32,2,640]{2,1,0:T(2,128)(2,1)S(1)} %reshape.155), channel_id=1, replica_groups=mesh['dp'=16,'expert'=32] {'expert'}, dimensions={0} | all-to-all | bytes 163840 | tf_op jit(solution)/shard_map/all_to_all | solution.py:40
  62.7 0.1 reshape.156
  62.8 0.6 copy.14
  63.4 0.0 all-gather.5.cloned.1.call-update
  63.4 0.0 reduce-scatter.5.cloned.1.call-start
  63.5 29.8 %all-gather.7.cloned.1.call-done = bf16[1,512,1280]{2,1,0:T(8,128)(2,1)} async-done(((bf16[1,32,1280]{2,1,0:T(8,128)(2,1)}), bf16[1,512,1280]{2,1,0:T(8,128)(2,1)}) %all-gather.7.cloned.1.call-update) | async-done | bytes 1310736 | tf_op jit(solution)/shard_map/all_gather | solution.py:22
  93.3 4.0 fusion.39
  97.2 2.0 fusion.1
  99.2 0.0 reduce-scatter.3.cloned.1.call-start
  99.3 55.8 %all-gather.5.cloned.1.call-done = bf16[1,512,1280]{2,1,0:T(8,128)(2,1)} async-done(((bf16[1,32,1280]{2,1,0:T(8,128)(2,1)}), bf16[1,512,1280]{2,1,0:T(8,128)(2,1)}) %all-gather.5.cloned.1.call-update) | async-done | bytes 1310736 | tf_op jit(solution)/shard_map/all_gather | solution.py:41
  155.1 2.2 fusion.26
  157.3 2.0 fusion
  159.3 87.3 %reduce-scatter.5.cloned.1.call-done = bf16[32,1,1280]{2,0,1:T(8,128)(2,1)} async-done(((bf16[512,1,1280]{2,0,1:T(8,128)(2,1)}), bf16[32,1,1280]{2,0,1:T(8,128)(2,1)}) %reduce-scatter.5.cloned.1.call-update) | async-done | bytes 81936 | tf_op jit(solution)/shard_map/reduce_scatter | solution.py:26
  246.5 1.5 reduce.15
  248.1 0.7 reshape.161
  248.7 14.6 %all-to-all-start.3 = ((bf16[32,2,640]{2,1,0:T(2,128)(2,1)}), bf16[32,2,640]{2,1,0:T(2,128)(2,1)S(1)}, u32[]{:S(2)}, u32[]{:S(2)}) async-start(bf16[32,2,640]{2,1,0:T(2,128)(2,1)} %reshape.161), calls=%async_computation.5 | async-start | bytes 163840 | tf_op jit(solution)/shard_map/all_to_all | solution.py:34
  263.3 2.9 fusion.2
  266.2 72.2 %reduce-scatter.3.cloned.1.call-done = bf16[32,1,1280]{2,0,1:T(8,128)(2,1)} async-done(((bf16[512,1,1280]{2,0,1:T(8,128)(2,1)}), bf16[32,1,1280]{2,0,1:T(8,128)(2,1)}) %reduce-scatter.3.cloned.1.call-update) | async-done | bytes 81936 | tf_op jit(solution)/shard_map/reduce_scatter | solution.py:51
  338.4 1.5 reduce.14
  340.0 0.7 reshape.159
  340.7 14.6 %all-to-all-start.2 = ((bf16[32,2,640]{2,1,0:T(2,128)(2,1)}), bf16[32,2,640]{2,1,0:T(2,128)(2,1)S(1)}, u32[]{:S(2)}, u32[]{:S(2)}) async-start(bf16[32,2,640]{2,1,0:T(2,128)(2,1)} %reshape.159), calls=%async_computation.3 | async-start | bytes 163840 | tf_op jit(solution)/shard_map/all_to_all | solution.py:59
  355.3 0.0 all-reduce.2.cloned.1.call-start
  355.3 1.5 fusion.3
  356.8 0.1 reshape.162
  356.9 0.2 convolution_bitcast_fusion.1
  357.1 11.9 %all-to-all-done.2 = bf16[32,2,640]{2,1,0:T(2,128)(2,1)S(1)} async-done(((bf16[32,2,640]{2,1,0:T(2,128)(2,1)}), bf16[32,2,640]{2,1,0:T(2,128)(2,1)S(1)}, u32[]{:S(2)}, u32[]{:S(2)}) %all-to-all-start.2) | async-done | bytes 81952 | tf_op jit(solution)/shard_map/all_to_all | solution.py:59
  369.0 0.1 reshape.160
  369.0 0.4 fusion.59
  369.5 0.4 multiply_reduce_fusion.1
  369.9 0.9 convolution_bitcast_fusion
  370.8 1.2 fusion.5
  372.0 440.3 %all-reduce.2.cloned.1.call-done = f32[1280,32]{0,1:T(8,128)} async-done(((f32[1280,32]{0,1:T(8,128)}), f32[1280,32]{0,1:T(8,128)}) %all-reduce.2.cloned.1.call-update) | async-done | bytes 163856 | tf_op jit(solution)/shard_map/psum | solution.py:70
  812.3 1.6 copy.42
  (18 shorter events, 0.1 us)
Async XLA Ops:
  7.2 86.1 %copy-start = (bf16[1,1280,320]{1,2,0:T(8,128)(2,1)S(1)}, bf16[1,1280,320]{1,2,0:T(8,128)(2,1)}, u32[]{:S(2)}) copy-start(bf16[1,1280,320]{1,2,0:T(8,128)(2,1)} %param.7) | copy-start | bytes 2457604
  7.2 36.0 %copy-start.2 = (bf16[1,196,1280]{2,1,0:T(8,128)(2,1)S(1)}, bf16[1,196,1280]{2,1,0:T(8,128)(2,1)}, u32[]{:S(2)}) copy-start(bf16[1,196,1280]{2,1,0:T(8,128)(2,1)} %param.9) | copy-start | bytes 1505284
  7.2 86.1 %all-gather.7.cloned.1.call-start = ((), (), s32[]{:S(2)}) async-start(), calls=%async_computation.10 | async-start | bytes 1392640 | tf_op jit(solution)/shard_map/all_gather | solution.py:22
  43.1 112.0 %all-gather.5.cloned.1.call-start = ((), (), s32[]{:S(2)}) async-start(), calls=%async_computation.9 | async-start | bytes 1392640 | tf_op jit(solution)/shard_map/all_gather | solution.py:41
  63.4 33.8 %copy-start.5 = (bf16[1,320,1280]{2,1,0:T(8,128)(2,1)S(1)}, bf16[1,320,1280]{2,1,0:T(8,128)(2,1)}, u32[]{:S(2)}) copy-start(bf16[1,320,1280]{2,1,0:T(8,128)(2,1)} %param.8) | copy-start | bytes 2457604
  63.4 183.1 %reduce-scatter.5.cloned.1.call-start = ((), (), s32[]{:S(2)}) async-start(), calls=%async_computation.7 | async-start | bytes 1392640 | tf_op jit(solution)/shard_map/reduce_scatter | solution.py:26
  99.2 239.2 %reduce-scatter.3.cloned.1.call-start = ((), (), s32[]{:S(2)}) async-start(), calls=%async_computation.6 | async-start | bytes 1392640 | tf_op jit(solution)/shard_map/reduce_scatter | solution.py:51
  248.7 91.9 %all-to-all-start.3 = ((bf16[32,2,640]{2,1,0:T(2,128)(2,1)}), bf16[32,2,640]{2,1,0:T(2,128)(2,1)S(1)}, u32[]{:S(2)}, u32[]{:S(2)}) async-start(bf16[32,2,640]{2,1,0:T(2,128)(2,1)} %reshape.161), calls=%async_computation.5 | async-start | bytes 163840 | tf_op jit(solution)/shard_map/all_to_all | solution.py:34
  263.3 92.0 %copy-start.3 = (bf16[1,512,1280]{2,1,0:T(8,128)(2,1)S(1)}, bf16[1,512,1280]{2,1,0:T(8,128)(2,1)}, u32[]{:S(2)}) copy-start(bf16[1,512,1280]{2,1,0:T(8,128)(2,1)} %all-gather.7.cloned.1.call-done) | copy-start | bytes 3932164
  340.7 28.3 %all-to-all-start.2 = ((bf16[32,2,640]{2,1,0:T(2,128)(2,1)}), bf16[32,2,640]{2,1,0:T(2,128)(2,1)S(1)}, u32[]{:S(2)}, u32[]{:S(2)}) async-start(bf16[32,2,640]{2,1,0:T(2,128)(2,1)} %reshape.159), calls=%async_computation.3 | async-start | bytes 163840 | tf_op jit(solution)/shard_map/all_to_all | solution.py:59
  355.3 457.0 %all-reduce.2.cloned.1.call-start = ((), (), s32[]{:S(2)}) async-start(), calls=%async_computation.8 | async-start | bytes 327680 | tf_op jit(solution)/shard_map/psum | solution.py:70
  356.8 12.6 %copy-start.1 = (bf16[1,196,1280]{2,1,0:T(8,128)(2,1)S(1)}, bf16[1,196,1280]{2,1,0:T(8,128)(2,1)}, u32[]{:S(2)}) copy-start(bf16[1,196,1280]{2,1,0:T(8,128)(2,1)} %param.5) | copy-start | bytes 1505284
  369.0 1.8 copy-start.4
Sparse Core Ops, SparseCore 0:
  43.2 50.0 all-gather.6
  96.9 58.1 all-gather.4
  159.2 87.3 reduce-scatter.4
  250.5 87.9 reduce-scatter.2
  371.0 441.3 all-reduce.1
where the time goes:
time: 821 us; the launch traced here: 820 us
  waiting for transfers between devices  697 us (85%)
  blocking collectives  48.3 us (6%)
  starting transfers between devices  29.4 us (4%)
  matrix products  20.7 us (3%)
  between operations  13.9 us (2%)
    psum x1, waiting for transfers between devices, local(): grad_router = lax.psum(router_term, ('dp', 'expert'))  440 us
    reduce_scatter x1, waiting for transfers between devices, local(): lax.psum_scatter(jnp.einsum('beh,ehd->bed', rows, w_out, preferred_elemen...  87.3 us
    reduce_scatter x1, waiting for transfers between devices, local(): lax.psum_scatter(jnp.einsum('beh,edh->bed', rows, w_in, preferred_element...  72.2 us
    all_gather x1, waiting for transfers between devices, local(): g_sall = lax.all_gather(g_sout, 'dp', axis=0, tiled=True)  55.8 us
    all_to_all x1, blocking collectives, local(): lax.all_to_all(slot_in, 'expert', split_axis=1, concat_axis=0, tiled=True)  30.3 us
    all_gather x1, waiting for transfers between devices, local(): all_in = lax.all_gather(expert_in, 'dp', axis=0, tiled=True)  29.8 us
    all_to_all x1, blocking collectives, local(): lax.all_to_all(g_late, 'expert', split_axis=1, concat_axis=0, tiled=True)  18 us
  transfers between devices with their start and end apart: 7, of which 6 were waited for; matrix products, arithmetic and copies ran while one was open for 3% of the time, Pallas kernels for 0%

commit v1 on v0

v1 whole, which is shorter than its diff:
```python
import jax
import jax.numpy as jnp
from jax import lax
from jax.sharding import PartitionSpec as P

BF = jnp.bfloat16
F32 = jnp.float32


def gelu_slope(x):
    cdf = 0.5 * (1.0 + jax.scipy.special.erf(x * 0.7071067811865476))
    return cdf + x * jnp.exp(-0.5 * x * x) * 0.3989422804014327


def dot(spec, a, b):
    return jnp.einsum(spec, a, b, preferred_element_type=F32)


def swap(x, axis):
    return lax.all_to_all(x, axis, split_axis=0, concat_axis=0, tiled=True)


def local(tokens, router, w_in, w_out, cotangent):
    n_dp, n_ex = lax.axis_size("dp"), lax.axis_size("expert")
    tok, cot = tokens[0], cotangent[0]
    win, wout = w_in[0], w_out[0]
    d = tok.shape[1]

    logits = dot("td,ds->ts", tok, router)
    dispatch = jax.nn.softmax(logits, axis=0)
    combine = jax.nn.softmax(logits, axis=1)
    dispatch_bf = dispatch.astype(BF)
    combine_bf = combine.astype(BF)
    slot_in = dot("ts,td->sd", dispatch_bf, tok).astype(BF)
    g_late = dot("ts,td->sd", combine_bf, cot).astype(BF)

    rows = swap(jnp.concatenate([slot_in, g_late], axis=1), "expert")
    rows = rows.reshape(n_ex, 2, d).transpose(1, 0, 2).reshape(2 * n_ex, d)
    every = swap(jnp.broadcast_to(rows[None], (n_dp, 2 * n_ex, d)), "dp")
    every = every.reshape(n_dp, 2, n_ex, d)
    all_in = every[:, 0].reshape(n_dp * n_ex, d)
    g_sall = every[:, 1].reshape(n_dp * n_ex, d)

    pre = dot("bd,dh->bh", all_in, win)
    hidden = jax.nn.gelu(pre, approximate=False).astype(BF)
    g_hid = dot("bd,hd->bh", g_sall, wout)
    g_pre = (g_hid * gelu_slope(pre)).astype(BF)
    slot_part = dot("bh,hd->bd", hidden, wout).astype(BF)
    g_slot_part = dot("bh,dh->bd", g_pre, win).astype(BF)
    grad_w_out = dot("bh,bd->hd", hidden, g_sall).astype(BF)
    grad_w_in = dot("bd,bh->dh", all_in, g_pre).astype(BF)

    terms = jnp.concatenate(
        [slot_part.reshape(n_dp, n_ex, d), g_slot_part.reshape(n_dp, n_ex, d)], axis=1
    )
    terms = swap(terms, "dp")
    sums = jnp.sum(terms.astype(F32), axis=0).astype(BF)
    sums = sums.reshape(2, n_ex, d).transpose(1, 0, 2).reshape(n_ex, 2 * d)
    back = swap(sums, "expert")
    slot_out, g_slot = back[:, :d], back[:, d:]

    g_comb = dot("td,sd->ts", cot, slot_out)
    g_clog = combine * (g_comb - jnp.sum(combine * g_comb, axis=1, keepdims=True))
    g_disp = dot("td,sd->ts", tok, g_slot)
    g_dlog = dispatch * (g_disp - jnp.sum(dispatch * g_disp, axis=0, keepdims=True))
    g_logits = (g_dlog + g_clog).astype(BF)

    term = dot("ts,td->sd", g_logits, tok)
    row = jnp.sum(swap(term, "expert"), axis=0, keepdims=True)
    row = jnp.sum(swap(jnp.broadcast_to(row, (n_dp, d)), "dp"), axis=0, keepdims=True)
    grad_router = swap(jnp.broadcast_to(row, (n_ex, d)), "expert").T

    grad_tokens = dot("ts,sd->td", dispatch_bf, g_slot) + dot("ts,ds->td", g_logits, router)
    return (grad_tokens.astype(BF)[None], grad_router, grad_w_in[None], grad_w_out[None])


def solution(mesh):
    placed = (
        P(("dp", "expert"), None, None),
        P(),
        P("expert", None, "dp"),
        P("expert", "dp", None),
        P(("dp", "expert"), None, None),
    )
    return jax.shard_map(
        local,
        mesh=mesh,
        in_specs=placed,
        out_specs=(
            P(("dp", "expert"), None, None),
            P(),
            P("expert", None, "dp"),
            P("expert", "dp", None),
        ),
        check_vma=False,
    )
```

time: 821 us -> 207 us (0.25)
  waiting for transfers between devices: 697 us -> 12.6 us
  blocking collectives: 48.3 us -> 164 us
  starting transfers between devices: 29.4 us -> 6.55 us
  between operations: 13.9 us -> 0.98 us
    psum x1 -> x0, waiting for transfers between devices: 440 us -> none  [local(): grad_router = lax.psum(router_term, ('dp', 'expert'))]
    reduce_scatter x2 -> x0, waiting for transfers between devices: 159 us -> none  [the longest x1 87.3 us: local(): lax.psum_scatter(jnp.einsum('beh,ehd->bed', rows, w_out, preferred_elemen...]
    all_to_all x2 -> x6, blocking collectives: 48.3 us -> 164 us  [swap(): return lax.all_to_all(x, axis, split_axis=0, concat_axis=0, tiled=True)]
    all_gather x2 -> x0, waiting for transfers between devices: 85.6 us -> none  [the longest x1 55.8 us: local(): g_sall = lax.all_gather(g_sout, 'dp', axis=0, tiled=True)]
    all_to_all x2 -> x1, starting transfers between devices: 29.2 us -> 6.55 us  [swap(): return lax.all_to_all(x, axis, split_axis=0, concat_axis=0, tiled=True)]
  transfers between devices with their start and end apart: 7 -> 1, of which waited for: 6 -> 1; matrix products, arithmetic and copies ran while one was open for 3% -> 2% of each run, Pallas kernels for 0% -> 0%
where the time goes in v1:
time: 207 us
  blocking collectives  164 us (79%)
  matrix products  13.2 us (6%)
  waiting for transfers between devices  12.6 us (6%)
  starting transfers between devices  6.55 us (3%)
  other arithmetic  4.95 us (2%)
  local copies, waits for them, and re-layouts  4.33 us (2%)
    all_to_all x6, blocking collectives, swap(): return lax.all_to_all(x, axis, split_axis=0, concat_axis=0, tiled=True)  164 us
    dot_general x14, matrix products, dot(): return jnp.einsum(spec, a, b, preferred_element_type=F32)  13.2 us
    all_to_all x1, waiting for transfers between devices, swap(): return lax.all_to_all(x, axis, split_axis=0, concat_axis=0, tiled=True)  12.6 us
    all_to_all x1, starting transfers between devices, swap(): return lax.all_to_all(x, axis, split_axis=0, concat_axis=0, tiled=True)  6.55 us
  transfers between devices with their start and end apart: 1, of which 1 were waited for; matrix products, arithmetic and copies ran while one was open for 2% of the time, Pallas kernels for 0%

profile of v1, /device:TPU:1, one launch (start us, length us, event | category | flops | bytes accessed | tf_op | source)
XLA Modules:
  0.0 206.5 jit_solution(8577334486461936741)
XLA Ops:
  0.6 0.0 copy-start
  0.6 0.0 copy-start.6
  0.7 1.5 fusion.45
  2.2 0.2 fusion.36
  2.4 1.3 convolution_convert_fusion.5
  3.7 0.2 convolution_convert_fusion.4
  3.9 0.5 broadcast.31
  4.5 0.7 reduce.4
  5.2 33.7 %all_to_all.56 = bf16[32,2,1280]{2,1,0:T(2,128)(2,1)S(1)} all-to-all(bf16[32,2,1280]{2,1,0:T(2,128)(2,1)S(1)} %reshape.57), channel_id=1, replica_groups=mesh['dp'=16,'expert'=32] {'expert'}, dimensions={0} | all-to-all | bytes 327680 | tf_op jit(solution)/shard_map/all_to_all | solution.py:20
  38.9 0.1 reshape.58
  39.0 0.9 reduce.3
  40.1 0.2 broadcast_in_dim.15
  40.3 38.4 %all_to_all.57 = bf16[16,64,1280]{2,1,0:T(8,128)(2,1)S(1)} all-to-all(bf16[16,64,1280]{2,1,0:T(8,128)(2,1)S(1)} %broadcast_in_dim.15), channel_id=1, replica_groups=mesh['dp'=16,'expert'=32] {'dp'}, dimensions={0} | all-to-all | bytes 5242880 | tf_op jit(solution)/shard_map/all_to_all | solution.py:20
  78.7 0.2 fusion.46
  78.9 0.0 copy-start.13
  78.9 2.2 %fusion.12 = (bf16[512,320]{0,1:T(8,128)(2,1)S(1)}, f32[512,320]{0,1:T(8,128)S(1)}) fusion(bf16[512,1280]{1,0:T(8,128)(2,1)S(1)} %bitcast.73, bf16[1,1280,320]{1,2,0:T(8,128)(2,1)S(1)} %copy-done), kind=kOutput, calls=%fused_computation.26 | convolution fusion | flops 430080000 | bytes 3112960 | tf_op jit(solution)/shard_map/bd,dh->bh/dot_general | solution.py:16
  81.2 0.0 copy-start.10
  81.2 0.7 fusion.4
  81.9 0.0 copy-start.8
  81.9 0.9 convolution_convert_fusion
  82.8 0.9 convolution_convert_fusion.1
  83.7 0.2 pad_maximum_fusion
  83.9 33.1 %all_to_all.58 = bf16[16,64,1280]{2,1,0:T(8,128)(2,1)S(1)} all-to-all(bf16[16,64,1280]{2,1,0:T(8,128)(2,1)S(1)} %pad_maximum_fusion), channel_id=1, replica_groups=mesh['dp'=16,'expert'=32] {'dp'}, dimensions={0} | all-to-all | bytes 5242880 | tf_op jit(solution)/shard_map/all_to_all | solution.py:20
  117.0 1.1 reduce_sum.68
  118.1 1.1 copy.28
  119.2 0.0 copy-start.7
  119.2 0.1 all_to_all.48
  119.3 1.7 reduce.5
  121.1 27.4 %all_to_all.59 = bf16[32,2,1280]{2,1,0:T(2,128)(2,1)S(1)} all-to-all(bf16[32,2,1280]{2,1,0:T(2,128)(2,1)S(1)} %reshape.59), channel_id=1, replica_groups=mesh['dp'=16,'expert'=32] {'expert'}, dimensions={0} | all-to-all | bytes 327680 | tf_op jit(solution)/shard_map/all_to_all | solution.py:20
  148.5 0.1 reshape.60
  148.7 0.2 convolution_bitcast_fusion.1
  148.9 0.0 copy-done.5
  148.9 0.4 multiply_reduce_fusion.1
  149.4 0.0 copy-start.11
  149.4 0.3 convolution_bitcast_fusion
  149.6 0.2 copy.30
  149.8 21.7 %all_to_all.60 = f32[32,1,1280]{2,1,0:T(1,128)S(1)} all-to-all(f32[32,1,1280]{2,1,0:T(1,128)S(1)} %copy.30), channel_id=1, replica_groups=mesh['dp'=16,'expert'=32] {'expert'}, dimensions={0} | all-to-all | bytes 327680 | tf_op jit(solution)/shard_map/all_to_all | solution.py:20
  171.5 0.1 reduce_sum.71
  171.7 9.6 %all_to_all.61 = f32[16,1,1280]{2,1,0:T(1,128)S(1)} all-to-all(f32[16,1,1280]{2,1,0:T(1,128)S(1)} %broadcast_in_dim.17), channel_id=1, replica_groups=mesh['dp'=16,'expert'=32] {'dp'}, dimensions={0} | all-to-all | bytes 163840 | tf_op jit(solution)/shard_map/all_to_all | solution.py:20
  181.3 0.1 reduce_sum.72
  181.3 0.8 broadcast_in_dim.18
  182.1 6.6 %all-to-all-start.6 = ((f32[32,1,1280]{2,1,0:T(1,128)}), f32[32,1,1280]{2,1,0:T(1,128)S(1)}, u32[]{:S(2)}, u32[]{:S(2)}) async-start(f32[32,1,1280]{2,1,0:T(1,128)} %broadcast_in_dim.18), calls=%async_computation.6 | async-start | bytes 327680 | tf_op jit(solution)/shard_map/all_to_all | solution.py:20
  188.7 1.5 fusion
  190.2 1.5 fusion.1
  191.7 0.4 fusion.33
  192.1 1.2 fusion.3
  193.3 12.6 %all-to-all-done.6 = f32[32,1,1280]{2,1,0:T(1,128)S(1)} async-done(((f32[32,1,1280]{2,1,0:T(1,128)}), f32[32,1,1280]{2,1,0:T(1,128)S(1)}, u32[]{:S(2)}, u32[]{:S(2)}) %all-to-all-start.6) | async-done | bytes 163872 | tf_op jit(solution)/shard_map/all_to_all | solution.py:20
  205.9 0.7 copy.37
  (27 shorter events, 0.3 us)
Async XLA Ops:
  0.6 78.3 %copy-start = (bf16[1,1280,320]{1,2,0:T(8,128)(2,1)S(1)}, bf16[1,1280,320]{1,2,0:T(8,128)(2,1)}, u32[]{:S(2)}) copy-start(bf16[1,1280,320]{1,2,0:T(8,128)(2,1)} %param.7) | copy-start | bytes 2457604
  0.6 3.1 %copy-start.6 = (bf16[1,196,1280]{2,1,0:T(8,128)(2,1)S(1)}, bf16[1,196,1280]{2,1,0:T(8,128)(2,1)}, u32[]{:S(2)}) copy-start(bf16[1,196,1280]{2,1,0:T(8,128)(2,1)} %param.9) | copy-start | bytes 1505284
  78.9 2.3 %copy-start.1 = (bf16[16,1,32,1280]{3,2,1,0:T(8,128)(2,1)}, bf16[16,1,32,1280]{3,2,1,0:T(8,128)(2,1)S(1)}, u32[]{:S(2)}) copy-start(bf16[16,1,32,1280]{3,2,1,0:T(8,128)(2,1)S(1)} %get-tuple-element.10) | copy-start | bytes 3932164
  78.9 2.3 %copy-start.3 = (bf16[16,1,32,1280]{3,2,1,0:T(8,128)(2,1)}, bf16[16,1,32,1280]{3,2,1,0:T(8,128)(2,1)S(1)}, u32[]{:S(2)}) copy-start(bf16[16,1,32,1280]{3,2,1,0:T(8,128)(2,1)S(1)} %get-tuple-element.11) | copy-start | bytes 3932164
  78.9 2.3 %copy-start.13 = (bf16[1,320,1280]{2,1,0:T(8,128)(2,1)S(1)}, bf16[1,320,1280]{2,1,0:T(8,128)(2,1)}, u32[]{:S(2)}) copy-start(bf16[1,320,1280]{2,1,0:T(8,128)(2,1)} %param.8) | copy-start | bytes 2457604
  81.2 1.7 copy-start.10
  81.9 1.8 copy-start.8
  119.2 29.5 %copy-start.7 = (bf16[1,196,1280]{2,1,0:T(8,128)(2,1)S(1)}, bf16[1,196,1280]{2,1,0:T(8,128)(2,1)}, u32[]{:S(2)}) copy-start(bf16[1,196,1280]{2,1,0:T(8,128)(2,1)} %param.9) | copy-start | bytes 1505284
  119.3 29.6 %copy-start.5 = (bf16[1,196,1280]{2,1,0:T(8,128)(2,1)S(1)}, bf16[1,196,1280]{2,1,0:T(8,128)(2,1)}, u32[]{:S(2)}) copy-start(bf16[1,196,1280]{2,1,0:T(8,128)(2,1)} %param.5) | copy-start | bytes 1505284
  149.3 39.3 %copy-start.4 = (bf16[16,1,32,1280]{3,2,1,0:T(8,128)(2,1)S(1)}, bf16[16,1,32,1280]{3,2,1,0:T(8,128)(2,1)}, u32[]{:S(2)}) copy-start(bf16[16,1,32,1280]{3,2,1,0:T(8,128)(2,1)} %copy-done.3) | copy-start | bytes 3932164
  149.4 39.3 %copy-start.11 = (bf16[512,320]{0,1:T(8,128)(2,1)S(1)}, bf16[512,320]{0,1:T(8,128)(2,1)}, u32[]{:S(2)}) copy-start(bf16[512,320]{0,1:T(8,128)(2,1)} %copy-done.10) | copy-start | bytes 983044
  182.1 23.8 %all-to-all-start.6 = ((f32[32,1,1280]{2,1,0:T(1,128)}), f32[32,1,1280]{2,1,0:T(1,128)S(1)}, u32[]{:S(2)}, u32[]{:S(2)}) async-start(f32[32,1,1280]{2,1,0:T(1,128)} %broadcast_in_dim.18), calls=%async_computation.6 | async-start | bytes 327680 | tf_op jit(solution)/shard_map/all_to_all | solution.py:20
  188.7 1.5 copy-start.2
  188.7 1.5 copy-start.9
  190.2 1.9 copy-start.12

commit v2 on v1

v2 whole, which is shorter than its diff:
```python
import jax
import jax.numpy as jnp
import numpy as np
from jax import lax
from jax.sharding import Mesh, PartitionSpec as P

BF = jnp.bfloat16
F32 = jnp.float32
PLANE = ("x", "yh", "yl")
CHIPS = ("x", "yh", "yl", "core")
TURN = [(0, 0), (1, 2), (2, 1), (3, 3)]
OTHER = [(0, 1), (1, 0)]


def gelu_slope(x):
    cdf = 0.5 * (1.0 + jax.scipy.special.erf(x * 0.7071067811865476))
    return cdf + x * jnp.exp(-0.5 * x * x) * 0.3989422804014327


def dot(spec, a, b):
    return jnp.einsum(spec, a, b, preferred_element_type=F32)


def swap(x, axis):
    return lax.all_to_all(x, axis, split_axis=0, concat_axis=0, tiled=True)


def local(tokens, router, w_in, w_out, cotangent):
    n_z = lax.axis_size("z")
    n_plane = lax.axis_size(PLANE)
    n_chips = lax.axis_size(CHIPS)
    tok, cot = tokens[0], cotangent[0]
    d = tok.shape[1]
    hid = w_out.shape[1]

    held = jnp.concatenate([w_in[0].T, w_out[0]], axis=0)
    mine = lax.ppermute(held, ("yl", "core"), TURN)
    other = lax.ppermute(mine, "core", OTHER)

    logits = dot("td,ds->ts", tok, router)
    dispatch = jax.nn.softmax(logits, axis=0)
    combine = jax.nn.softmax(logits, axis=1)
    dispatch_bf = dispatch.astype(BF)
    combine_bf = combine.astype(BF)
    slot_in = dot("ts,td->sd", dispatch_bf, tok).astype(BF)
    g_late = dot("ts,td->sd", combine_bf, cot).astype(BF)

    rows = jnp.stack([slot_in.reshape(n_z, 2, d), g_late.reshape(n_z, 2, d)], axis=2)
    rows = swap(rows.reshape(n_z, 4, d), "z").reshape(n_z, 2, 2, d)
    rows = rows.transpose(1, 2, 0, 3).reshape(1, 2, 2 * n_z, d)
    every = jnp.broadcast_to(rows, (n_plane // 2, 2, 2 * n_z, d)).reshape(n_plane, 2 * n_z, d)
    every = swap(every, PLANE).reshape(n_plane, 2, n_z, d)
    all_in = every[:, 0].reshape(n_plane * n_z, d)
    g_sall = every[:, 1].reshape(n_plane * n_z, d)

    slot_part, g_slot_part, kept = 0.0, 0.0, []
    for block in (mine, other):
        win, wout = block[:hid], block[hid:]
        pre = dot("bd,hd->bh", all_in, win)
        hidden = jax.nn.gelu(pre, approximate=False).astype(BF)
        g_pre = (dot("bd,hd->bh", g_sall, wout) * gelu_slope(pre)).astype(BF)
        slot_part = slot_part + dot("bh,hd->bd", hidden, wout)
        g_slot_part = g_slot_part + dot("bh,hd->bd", g_pre, win)
        kept.append((hidden, g_pre))

    terms = jnp.concatenate(
        [
            slot_part.astype(BF).reshape(n_plane, n_z, d),
            g_slot_part.astype(BF).reshape(n_plane, n_z, d),
        ],
        axis=1,
    )
    terms = swap(terms, PLANE).reshape(n_plane // 2, 2, 2, n_z, d)
    sums = jnp.sum(terms.astype(F32), axis=0).astype(BF)
    sums = sums.transpose(2, 0, 1, 3).reshape(n_z, 4, d)
    back = swap(sums, "z").reshape(n_z, 2, 2, d)
    slot_out, g_slot = back[:, :, 0].reshape(2 * n_z, d), back[:, :, 1].reshape(2 * n_z, d)

    grads = []
    for hidden, g_pre in kept:
        grads.append(
            jnp.concatenate([dot("bh,bd->hd", g_pre, all_in), dot("bh,bd->hd", hidden, g_sall)], axis=0)
        )
    theirs = lax.ppermute(grads[1].astype(BF), "core", OTHER)
    whole = (grads[0] + theirs.astype(F32)).astype(BF)
    whole = lax.ppermute(whole, ("yl", "core"), TURN)
    grad_w_in, grad_w_out = whole[:hid].T, whole[hid:]

    g_comb = dot("td,sd->ts", cot, slot_out)
    g_clog = combine * (g_comb - jnp.sum(combine * g_comb, axis=1, keepdims=True))
    g_disp = dot("td,sd->ts", tok, g_slot)
    g_dlog = dispatch * (g_disp - jnp.sum(dispatch * g_disp, axis=0, keepdims=True))
    g_logits = (g_dlog + g_clog).astype(BF)

    term = dot("ts,td->sd", g_logits, tok)
    row = jnp.sum(swap(term, CHIPS), axis=0, keepdims=True)
    row = jnp.sum(swap(jnp.broadcast_to(row, (n_z, d)), "z"), axis=0, keepdims=True)
    grad_router = swap(jnp.broadcast_to(row, (n_chips, d)), CHIPS).T

    grad_tokens = dot("ts,sd->td", dispatch_bf, g_slot) + dot("ts,ds->td", g_logits, router)
    return (grad_tokens.astype(BF)[None], grad_router, grad_w_in[None], grad_w_out[None])


def solution(mesh):
    fine = Mesh(np.asarray(mesh.devices).reshape(4, 2, 2, 16, 2), ("x", "yh", "yl", "z", "core"))
    images = P(("x", "yh", "yl", "z", "core"), None, None)
    first = P(("z", "core"), None, ("x", "yh", "yl"))
    second = P(("z", "core"), ("x", "yh", "yl"), None)
    return jax.shard_map(
        local,
        mesh=fine,
        in_specs=(images, P(), first, second, images),
        out_specs=(images, P(), first, second),
        check_vma=False,
    )
```

time: 207 us -> 202 us (0.976); the launches traced: 207 us -> 199 us
  blocking collectives: 164 us -> 19.2 us
  starting transfers between devices: 6.55 us -> 73.8 us
  waiting for transfers between devices: 12.6 us -> 62.5 us
  matrix products: 13.2 us -> 24.6 us
  local copies, waits for them, and re-layouts: 4.33 us -> 10.2 us
  other arithmetic: 4.95 us -> 7.3 us
    all_to_all x6 -> x1, blocking collectives: 164 us -> 19.2 us  [swap(): return lax.all_to_all(x, axis, split_axis=0, concat_axis=0, tiled=True)]
    all_to_all x1 -> x6, starting transfers between devices: 6.55 us -> 58 us  [swap(): return lax.all_to_all(x, axis, split_axis=0, concat_axis=0, tiled=True)]
    all_to_all x1 -> x6, waiting for transfers between devices: 12.6 us -> 61.1 us  [swap(): return lax.all_to_all(x, axis, split_axis=0, concat_axis=0, tiled=True)]
    ppermute x0 -> x4, starting transfers between devices: none -> 15.8 us  [the longest x1 5.64 us: local(): theirs = lax.ppermute(grads[1].astype(BF), 'core', OTHER)]
    dot_general x14 -> x20, matrix products: 13.2 us -> 24.6 us  [dot(): return jnp.einsum(spec, a, b, preferred_element_type=F32)]
    broadcast_in_dim x3 -> x4, local copies, waits for them, and re-layouts: 1.04 us -> 5.3 us  [the longest x1 2.66 us: local(): grad_w_out[None]]
    concatenate x1 -> x3, other arithmetic: 0.19 us -> 3.78 us  [the longest x1 1.28 us: local(): held = jnp.concatenate([w_in[0].T, w_out[0]], axis=0)]
    all_to_all x4 -> x0, other arithmetic: 3.34 us -> none  [swap(): return lax.all_to_all(x, axis, split_axis=0, concat_axis=0, tiled=True)]
  transfers between devices with their start and end apart: 1 -> 10, of which waited for: 1 -> 7; matrix products, arithmetic and copies ran while one was open for 2% -> 14% of each run, Pallas kernels for 0% -> 0%
where the time goes in v2:
time: 202 us; the launch traced here: 199 us
  starting transfers between devices  73.8 us (37%)
  waiting for transfers between devices  62.5 us (31%)
  matrix products  24.6 us (12%)
  blocking collectives  19.2 us (10%)
  local copies, waits for them, and re-layouts  10.2 us (5%)
  other arithmetic  7.3 us (4%)
    all_to_all x6, waiting for transfers between devices, swap(): return lax.all_to_all(x, axis, split_axis=0, concat_axis=0, tiled=True)  61.1 us
    all_to_all x6, starting transfers between devices, swap(): return lax.all_to_all(x, axis, split_axis=0, concat_axis=0, tiled=True)  58 us
    dot_general x20, matrix products, dot(): return jnp.einsum(spec, a, b, preferred_element_type=F32)  24.6 us
    all_to_all x1, blocking collectives, swap(): return lax.all_to_all(x, axis, split_axis=0, concat_axis=0, tiled=True)  19.2 us
    ppermute x1, starting transfers between devices, local(): theirs = lax.ppermute(grads[1].astype(BF), 'core', OTHER)  5.64 us
  transfers between devices with their start and end apart: 10, of which 7 were waited for; matrix products, arithmetic and copies ran while one was open for 14% of the time, Pallas kernels for 0%

profile of v2, /device:TPU:1, one launch (start us, length us, event | category | flops | bytes accessed | tf_op | source)
XLA Modules:
  0.0 198.6 jit_solution(3114410920757066778)
XLA Ops:
  0.7 1.0 copy-done
  1.7 1.4 fusion.70
  3.2 1.2 convolution_convert_fusion.2
  4.9 0.8 copy.43
  5.7 15.7 %all-to-all-start = ((bf16[16,4,1280]{2,1,0:T(4,128)(2,1)}), bf16[16,4,1280]{2,1,0:T(4,128)(2,1)S(1)}, u32[]{:S(2)}, u32[]{:S(2)}) async-start(bf16[16,4,1280]{2,1,0:T(4,128)(2,1)} %copy.43), calls=%async_computation | async-start | bytes 327680 | tf_op jit(solution)/shard_map/all_to_all | solution.py:25
  21.4 1.3 pad_maximum_fusion
  22.7 4.0 %collective-permute-start = (bf16[640,1280]{1,0:T(8,128)(2,1)}, bf16[640,1280]{1,0:T(8,128)(2,1)}, u32[]{:S(2)}, u32[]{:S(2)}) collective-permute-start(bf16[640,1280]{1,0:T(8,128)(2,1)} %pad_maximum_fusion), channel_id=1, source_target_pairs={{0,0},{1,32},{32,1},{33,33},{2,2},{3,34},{34,3},{35,35},{4,4},{5,3... | collective-permute-start | bytes 4915208 | tf_op jit(solution)/shard_map/ppermute | solution.py:37
  26.8 6.9 %all-to-all-done = bf16[16,4,1280]{2,1,0:T(4,128)(2,1)S(1)} async-done(((bf16[16,4,1280]{2,1,0:T(4,128)(2,1)}), bf16[16,4,1280]{2,1,0:T(4,128)(2,1)S(1)}, u32[]{:S(2)}, u32[]{:S(2)}) %all-to-all-start) | async-done | bytes 163872 | tf_op jit(solution)/shard_map/all_to_all | solution.py:25
  33.7 1.2 broadcast_in_dim.15
  34.9 9.6 %all-to-all-start.1 = ((bf16[16,32,1280]{2,1,0:T(8,128)(2,1)}), bf16[16,32,1280]{2,1,0:T(8,128)(2,1)S(1)}, u32[]{:S(2)}, u32[]{:S(2)}) async-start(bf16[16,32,1280]{2,1,0:T(8,128)(2,1)} %bitcast.84), calls=%async_computation.1 | async-start | bytes 2621440 | tf_op jit(solution)/shard_map/all_to_all | solution.py:25
  44.4 1.4 collective-permute-done
  45.9 2.3 %collective-permute-start.1 = (bf16[640,1280]{1,0:T(8,128)(2,1)}, bf16[640,1280]{1,0:T(8,128)(2,1)}, u32[]{:S(2)}, u32[]{:S(2)}) collective-permute-start(bf16[640,1280]{1,0:T(8,128)(2,1)} %collective-permute-done), channel_id=1, source_target_pairs={{0,1},{1,0},{2,3},{3,2},{4,5},{5,4},{6,7},{7,6},{8,9},{9,8},{10,11... | collective-permute-start | bytes 4915208 | tf_op jit(solution)/shard_map/ppermute | solution.py:38
  48.2 14.0 %all-to-all-done.1 = bf16[16,32,1280]{2,1,0:T(8,128)(2,1)S(1)} async-done(((bf16[16,32,1280]{2,1,0:T(8,128)(2,1)}), bf16[16,32,1280]{2,1,0:T(8,128)(2,1)S(1)}, u32[]{:S(2)}, u32[]{:S(2)}) %all-to-all-start.1) | async-done | bytes 1310752 | tf_op jit(solution)/shard_map/all_to_all | solution.py:25
  62.3 1.6 fusion.17
  63.8 1.7 fusion.5
  65.6 1.7 fusion.15
  67.2 2.2 %fusion.13 = f32[256,1280]{1,0:T(8,128)S(1)} fusion(bf16[640,1280]{1,0:T(8,128)(2,1)} %collective-permute-done, f32[256,320]{0,1:T(8,128)S(1)} %fusion.17), kind=kOutput, calls=%fused_computation.31 | convolution fusion | flops 215040000 | bytes 2457600 | tf_op jit(solution)/shard_map/bh,hd->bd/dot_general | solution.py:21
  69.5 1.6 fusion.10
  71.1 1.0 convolution_convert_fusion
  72.1 1.6 fusion.6
  73.7 0.4 convolution_convert_fusion.1
  74.1 1.3 pad_maximum_fusion.1
  75.4 5.6 %collective-permute-start.2 = (bf16[640,1280]{1,0:T(8,128)(2,1)}, bf16[640,1280]{1,0:T(8,128)(2,1)}, u32[]{:S(2)}, u32[]{:S(2)}) collective-permute-start(bf16[640,1280]{1,0:T(8,128)(2,1)} %pad_maximum_fusion.1), channel_id=1, source_target_pairs={{0,1},{1,0},{2,3},{3,2},{4,5},{5,4},{6,7},{7,6},{8,9},{9,8},{10,11... | collective-permute-start | bytes 4915208 | tf_op jit(solution)/shard_map/ppermute | solution.py:84
  81.0 1.7 fusion.2
  82.7 2.3 %fusion.1 = bf16[256,1280]{1,0:T(8,128)(2,1)S(1)} fusion(f32[256,1280]{1,0:T(8,128)S(1)} %fusion.13, bf16[640,1280]{1,0:T(8,128)(2,1)} %collective-permute-done.1, f32[256,320]{0,1:T(8,128)S(1)} %fusion.10), kind=kOutput, calls=%fused_computation.7 | convolution fusion | flops 215695360 | bytes 3112960 | tf_op jit(solution)/shard_map/bh,hd->bd/dot_general | solution.py:21
  85.0 1.2 pad_maximum_fusion.2
  86.2 3.7 %all-to-all-start.2 = ((bf16[16,32,1280]{2,1,0:T(8,128)(2,1)}), bf16[16,32,1280]{2,1,0:T(8,128)(2,1)S(1)}, u32[]{:S(2)}, u32[]{:S(2)}) async-start(bf16[16,32,1280]{2,1,0:T(8,128)(2,1)} %pad_maximum_fusion.2), calls=%async_computation.2 | async-start | bytes 2621440 | tf_op jit(solution)/shard_map/all_to_all | solution.py:25
  89.9 3.2 %fusion.67 = f32[320,1280]{1,0:T(8,128)} fusion(bf16[256,1280]{1,0:T(8,128)(2,1)S(1)} %bitcast.92, f32[256,320]{0,1:T(8,128)} %copy-done.6), kind=kOutput, calls=%fused_computation.107 | convolution fusion | flops 215040000 | bytes 2621440 | tf_op jit(solution)/shard_map/bh,bd->hd/dot_general | solution.py:21
  93.1 17.9 %all-to-all-done.2 = bf16[16,32,1280]{2,1,0:T(8,128)(2,1)S(1)} async-done(((bf16[16,32,1280]{2,1,0:T(8,128)(2,1)}), bf16[16,32,1280]{2,1,0:T(8,128)(2,1)S(1)}, u32[]{:S(2)}, u32[]{:S(2)}) %all-to-all-start.2) | async-done | bytes 1310752 | tf_op jit(solution)/shard_map/all_to_all | solution.py:25
  111.2 0.8 copy.45
  111.9 11.5 %all-to-all-start.3 = ((bf16[16,4,1280]{2,1,0:T(4,128)(2,1)}), bf16[16,4,1280]{2,1,0:T(4,128)(2,1)S(1)}, u32[]{:S(2)}, u32[]{:S(2)}) async-start(bf16[16,4,1280]{2,1,0:T(4,128)(2,1)} %copy.45), calls=%async_computation.3 | async-start | bytes 327680 | tf_op jit(solution)/shard_map/all_to_all | solution.py:25
  123.4 0.4 fusion.73
  123.9 1.0 copy-done.2
  124.9 2.9 %fusion = bf16[640,1280]{1,0:T(8,128)(2,1)} fusion(f32[320,1280]{1,0:T(8,128)S(1)} %copy-done.2, f32[320,1280]{1,0:T(8,128)S(1)} %fusion.73, bf16[640,1280]{1,0:T(8,128)(2,1)} %collective-permute-done.2), kind=kLoop, calls=%fused_computation.1 | loop fusion | flops 3276800 | bytes 6553600 | tf_op jit(solution)/shard_map/convert_element_type | solution.py:85
  127.8 3.8 %collective-permute-start.3 = (bf16[640,1280]{1,0:T(8,128)(2,1)}, bf16[640,1280]{1,0:T(8,128)(2,1)}, u32[]{:S(2)}, u32[]{:S(2)}) collective-permute-start(bf16[640,1280]{1,0:T(8,128)(2,1)} %fusion), channel_id=1, source_target_pairs={{0,0},{1,32},{32,1},{33,33},{2,2},{3,34},{34,3},{35,35},{4,4},{5,3... | collective-permute-start | bytes 4915208 | tf_op jit(solution)/shard_map/ppermute | solution.py:86
  131.6 4.0 %all-to-all-done.3 = bf16[16,4,1280]{2,1,0:T(4,128)(2,1)S(1)} async-done(((bf16[16,4,1280]{2,1,0:T(4,128)(2,1)}), bf16[16,4,1280]{2,1,0:T(4,128)(2,1)S(1)}, u32[]{:S(2)}, u32[]{:S(2)}) %all-to-all-start.3) | async-done | bytes 163872 | tf_op jit(solution)/shard_map/all_to_all | solution.py:25
  136.1 0.5 multiply_reduce_fusion.1
  137.0 19.2 %all_to_all.44 = f32[32,1,1280]{2,1,0:T(1,128)S(1)} all-to-all(f32[32,1,1280]{2,1,0:T(1,128)S(1)} %copy.49), channel_id=1, replica_groups=mesh['x'=4,'yh'=2,'yl'=2,'z'=16,'core'=2] {'x','yh','yl','core'}, dimensions={0} | all-to-all | bytes 327680 | tf_op jit(solution)/shard_map/all_to_all | solution.py:25
  156.3 0.7 broadcast_in_dim.17
  157.0 11.7 %all-to-all-start.5 = ((f32[16,1,1280]{2,1,0:T(1,128)}), f32[16,1,1280]{2,1,0:T(1,128)S(1)}, u32[]{:S(2)}, u32[]{:S(2)}) async-start(f32[16,1,1280]{2,1,0:T(1,128)} %broadcast_in_dim.17), calls=%async_computation.5 | async-start | bytes 163840 | tf_op jit(solution)/shard_map/all_to_all | solution.py:25
  168.8 0.4 fusion.59
  169.2 11.4 %all-to-all-done.5 = f32[16,1,1280]{2,1,0:T(1,128)S(1)} async-done(((f32[16,1,1280]{2,1,0:T(1,128)}), f32[16,1,1280]{2,1,0:T(1,128)S(1)}, u32[]{:S(2)}, u32[]{:S(2)}) %all-to-all-start.5) | async-done | bytes 81952 | tf_op jit(solution)/shard_map/all_to_all | solution.py:25
  180.6 0.8 broadcast_in_dim.18
  181.4 5.8 %all-to-all-start.6 = ((f32[32,1,1280]{2,1,0:T(1,128)}), f32[32,1,1280]{2,1,0:T(1,128)S(1)}, u32[]{:S(2)}, u32[]{:S(2)}) async-start(f32[32,1,1280]{2,1,0:T(1,128)} %broadcast_in_dim.18), calls=%async_computation.6 | async-start | bytes 327680 | tf_op jit(solution)/shard_map/all_to_all | solution.py:25
  187.2 1.2 fusion.4
  188.4 6.9 %all-to-all-done.6 = f32[32,1,1280]{2,1,0:T(1,128)S(1)} async-done(((f32[32,1,1280]{2,1,0:T(1,128)}), f32[32,1,1280]{2,1,0:T(1,128)S(1)}, u32[]{:S(2)}, u32[]{:S(2)}) %all-to-all-start.6) | async-done | bytes 163872 | tf_op jit(solution)/shard_map/all_to_all | solution.py:25
  195.3 0.7 copy.54
  196.0 2.7 %slice_bitcast_fusion = (bf16[1,320,1280]{2,1,0:T(8,128)(2,1)}, bf16[1,1280,320]{1,2,0:T(8,128)(2,1)}) fusion(bf16[640,1280]{1,0:T(8,128)(2,1)} %collective-permute-done.3), kind=kLoop, calls=%fused_computation.23 | loop fusion | bytes 3276800 | tf_op jit(solution)/shard_map/broadcast_in_dim | solution.py:101
  (36 shorter events, 2.0 us)
Async XLA Ops:
  0.6 1.0 copy-start
  0.6 20.8 %copy-start.3 = (bf16[1,320,1280]{2,1,0:T(8,128)(2,1)S(1)}, bf16[1,320,1280]{2,1,0:T(8,128)(2,1)}, u32[]{:S(2)}) copy-start(bf16[1,320,1280]{2,1,0:T(8,128)(2,1)} %param.8) | copy-start | bytes 2457604
  1.7 19.8 %copy-start.4 = (bf16[1,1280,320]{1,2,0:T(8,128)(2,1)S(1)}, bf16[1,1280,320]{1,2,0:T(8,128)(2,1)}, u32[]{:S(2)}) copy-start(bf16[1,1280,320]{1,2,0:T(8,128)(2,1)} %param.7) | copy-start | bytes 2457604
  5.7 28.0 %all-to-all-start = ((bf16[16,4,1280]{2,1,0:T(4,128)(2,1)}), bf16[16,4,1280]{2,1,0:T(4,128)(2,1)S(1)}, u32[]{:S(2)}, u32[]{:S(2)}) async-start(bf16[16,4,1280]{2,1,0:T(4,128)(2,1)} %copy.43), calls=%async_computation | async-start | bytes 327680 | tf_op jit(solution)/shard_map/all_to_all | solution.py:25
  22.7 23.1 %collective-permute-start = (bf16[640,1280]{1,0:T(8,128)(2,1)}, bf16[640,1280]{1,0:T(8,128)(2,1)}, u32[]{:S(2)}, u32[]{:S(2)}) collective-permute-start(bf16[640,1280]{1,0:T(8,128)(2,1)} %pad_maximum_fusion), channel_id=1, source_target_pairs={{0,0},{1,32},{32,1},{33,33},{2,2},{3,34},{34,3},{35,35},{4,4},{5,3... | collective-permute-start | bytes 4915208 | tf_op jit(solution)/shard_map/ppermute | solution.py:37
  34.9 27.3 %all-to-all-start.1 = ((bf16[16,32,1280]{2,1,0:T(8,128)(2,1)}), bf16[16,32,1280]{2,1,0:T(8,128)(2,1)S(1)}, u32[]{:S(2)}, u32[]{:S(2)}) async-start(bf16[16,32,1280]{2,1,0:T(8,128)(2,1)} %bitcast.84), calls=%async_computation.1 | async-start | bytes 2621440 | tf_op jit(solution)/shard_map/all_to_all | solution.py:25
  45.9 23.6 %collective-permute-start.1 = (bf16[640,1280]{1,0:T(8,128)(2,1)}, bf16[640,1280]{1,0:T(8,128)(2,1)}, u32[]{:S(2)}, u32[]{:S(2)}) collective-permute-start(bf16[640,1280]{1,0:T(8,128)(2,1)} %collective-permute-done), channel_id=1, source_target_pairs={{0,1},{1,0},{2,3},{3,2},{4,5},{5,4},{6,7},{7,6},{8,9},{9,8},{10,11... | collective-permute-start | bytes 4915208 | tf_op jit(solution)/shard_map/ppermute | solution.py:38
  63.8 3.4 %copy-start.6 = (f32[256,320]{0,1:T(8,128)}, f32[256,320]{0,1:T(8,128)S(1)}, u32[]{:S(2)}) copy-start(f32[256,320]{0,1:T(8,128)S(1)} %fusion.17) | copy-start | bytes 983044
  75.4 48.5 %collective-permute-start.2 = (bf16[640,1280]{1,0:T(8,128)(2,1)}, bf16[640,1280]{1,0:T(8,128)(2,1)}, u32[]{:S(2)}, u32[]{:S(2)}) collective-permute-start(bf16[640,1280]{1,0:T(8,128)(2,1)} %pad_maximum_fusion.1), channel_id=1, source_target_pairs={{0,1},{1,0},{2,3},{3,2},{4,5},{5,4},{6,7},{7,6},{8,9},{9,8},{10,11... | collective-permute-start | bytes 4915208 | tf_op jit(solution)/shard_map/ppermute | solution.py:84
  86.2 24.8 %all-to-all-start.2 = ((bf16[16,32,1280]{2,1,0:T(8,128)(2,1)}), bf16[16,32,1280]{2,1,0:T(8,128)(2,1)S(1)}, u32[]{:S(2)}, u32[]{:S(2)}) async-start(bf16[16,32,1280]{2,1,0:T(8,128)(2,1)} %pad_maximum_fusion.2), calls=%async_computation.2 | async-start | bytes 2621440 | tf_op jit(solution)/shard_map/all_to_all | solution.py:25
  111.9 23.7 %all-to-all-start.3 = ((bf16[16,4,1280]{2,1,0:T(4,128)(2,1)}), bf16[16,4,1280]{2,1,0:T(4,128)(2,1)S(1)}, u32[]{:S(2)}, u32[]{:S(2)}) async-start(bf16[16,4,1280]{2,1,0:T(4,128)(2,1)} %copy.45), calls=%async_computation.3 | async-start | bytes 327680 | tf_op jit(solution)/shard_map/all_to_all | solution.py:25
  123.4 1.4 copy-start.2
  123.8 12.0 %copy-start.1 = (bf16[1,196,1280]{2,1,0:T(8,128)(2,1)S(1)}, bf16[1,196,1280]{2,1,0:T(8,128)(2,1)}, u32[]{:S(2)}) copy-start(bf16[1,196,1280]{2,1,0:T(8,128)(2,1)} %param.9) | copy-start | bytes 1505284
  127.8 68.2 %collective-permute-start.3 = (bf16[640,1280]{1,0:T(8,128)(2,1)}, bf16[640,1280]{1,0:T(8,128)(2,1)}, u32[]{:S(2)}, u32[]{:S(2)}) collective-permute-start(bf16[640,1280]{1,0:T(8,128)(2,1)} %fusion), channel_id=1, source_target_pairs={{0,0},{1,32},{32,1},{33,33},{2,2},{3,34},{34,3},{35,35},{4,4},{5,3... | collective-permute-start | bytes 4915208 | tf_op jit(solution)/shard_map/ppermute | solution.py:86
  136.6 50.6 %copy-start.5 = (bf16[1280,32]{0,1:T(8,128)(2,1)S(1)}, bf16[1280,32]{0,1:T(8,128)(2,1)}, u32[]{:S(2)}) copy-start(bf16[1280,32]{0,1:T(8,128)(2,1)} %param.6) | copy-start | bytes 245764
  157.0 23.6 %all-to-all-start.5 = ((f32[16,1,1280]{2,1,0:T(1,128)}), f32[16,1,1280]{2,1,0:T(1,128)S(1)}, u32[]{:S(2)}, u32[]{:S(2)}) async-start(f32[16,1,1280]{2,1,0:T(1,128)} %broadcast_in_dim.17), calls=%async_computation.5 | async-start | bytes 163840 | tf_op jit(solution)/shard_map/all_to_all | solution.py:25
  181.4 13.9 %all-to-all-start.6 = ((f32[32,1,1280]{2,1,0:T(1,128)}), f32[32,1,1280]{2,1,0:T(1,128)S(1)}, u32[]{:S(2)}, u32[]{:S(2)}) async-start(f32[32,1,1280]{2,1,0:T(1,128)} %broadcast_in_dim.18), calls=%async_computation.6 | async-start | bytes 327680 | tf_op jit(solution)/shard_map/all_to_all | solution.py:25

commit v3 on v2

v3 whole, which is shorter than its diff:
```python
import jax
import jax.numpy as jnp
import numpy as np
from jax import lax
from jax.experimental import pallas as pl
from jax.experimental.pallas import tpu as pltpu
from jax.sharding import Mesh, PartitionSpec as P

BF = jnp.bfloat16
F32 = jnp.float32
PLANE = ("x", "yh", "yl")
CHIPS = ("x", "yh", "yl", "core")
TURN = [(2, 0), (0, 1), (1, 3), (3, 2)]
BACK = [(b, a) for a, b in TURN]
OTHER = [(0, 1), (1, 0)]


def dot(spec, a, b):
    return jnp.einsum(spec, a, b, preferred_element_type=F32)


def nn(a, b):
    return jnp.dot(a, b, preferred_element_type=F32)


def nt(a, b):
    return lax.dot_general(a, b, (((1,), (1,)), ((), ())), preferred_element_type=F32)


def tn(a, b):
    return lax.dot_general(a, b, (((0,), (0,)), ((), ())), preferred_element_type=F32)


def rows_of(every):
    n, both, d = every.shape
    half = both // 2
    return every[:, :half].reshape(n * half, d), every[:, half:].reshape(n * half, d)


def expert_kernel(every, mine, other, terms, hidden, g_pre):
    hid = mine.shape[0] // 2
    n, both, d = every.shape
    x, g = rows_of(every[...])
    out, back = 0.0, 0.0
    for i, block in enumerate((mine, other)):
        win, wout = block[:hid], block[hid:]
        pre = nt(x, win)
        cdf = 0.5 * (1.0 + lax.erf(pre * 0.7071067811865476))
        h = (pre * cdf).astype(BF)
        slope = cdf + pre * jnp.exp(-0.5 * pre * pre) * 0.3989422804014327
        gp = (nt(g, wout) * slope).astype(BF)
        hidden[i] = h
        g_pre[i] = gp
        out = out + nn(h, wout)
        back = back + nn(gp, win)
    terms[:, : both // 2] = out.astype(BF).reshape(n, both // 2, d)
    terms[:, both // 2 :] = back.astype(BF).reshape(n, both // 2, d)


def other_kernel(every, hidden, g_pre, grads):
    hid = grads.shape[0] // 2
    x, g = rows_of(every[...])
    grads[:hid] = tn(g_pre[1], x).astype(BF)
    grads[hid:] = tn(hidden[1], g).astype(BF)


def mine_kernel(every, hidden, g_pre, theirs, grads):
    hid = grads.shape[0] // 2
    x, g = rows_of(every[...])
    grads[:hid] = (tn(g_pre[0], x) + theirs[:hid].astype(F32)).astype(BF)
    grads[hid:] = (tn(hidden[0], g) + theirs[hid:].astype(F32)).astype(BF)


def call(kernel, outs, flops, *args):
    moved = sum(a.size * a.dtype.itemsize for a in args) + sum(o.size * o.dtype.itemsize for o in outs)
    whole = pl.BlockSpec(memory_space=pltpu.VMEM)
    return pl.pallas_call(
        kernel,
        out_shape=outs,
        in_specs=[whole] * len(args),
        out_specs=[whole] * len(outs),
        compiler_params=pltpu.CompilerParams(vmem_limit_bytes=28 * 2**20),
        cost_estimate=pl.CostEstimate(flops=flops, bytes_accessed=moved, transcendentals=0),
    )(*args)


def swap(x, axis):
    return lax.all_to_all(x, axis, split_axis=0, concat_axis=0, tiled=True)


def local(tokens, router, w_in, w_out, cotangent):
    n_z = lax.axis_size("z")
    n_plane = lax.axis_size(PLANE)
    n_chips = lax.axis_size(CHIPS)
    tok, cot = tokens[0], cotangent[0]
    d = tok.shape[1]
    hid = w_out.shape[1]

    held = jnp.concatenate([w_in[0].T, w_out[0]], axis=0)
    mine = lax.ppermute(held, ("yl", "core"), TURN)
    other = lax.ppermute(mine, "core", OTHER)

    logits = dot("td,ds->ts", tok, router)
    dispatch = jax.nn.softmax(logits, axis=0)
    combine = jax.nn.softmax(logits, axis=1)
    dispatch_bf = dispatch.astype(BF)
    combine_bf = combine.astype(BF)
    slot_in = dot("ts,td->sd", dispatch_bf, tok).astype(BF)
    g_late = dot("ts,td->sd", combine_bf, cot).astype(BF)

    rows = jnp.stack([slot_in.reshape(n_z, 2, d), g_late.reshape(n_z, 2, d)], axis=2)
    rows = swap(rows.reshape(n_z, 4, d), "z").reshape(n_z, 2, 2, d)
    rows = rows.transpose(1, 2, 0, 3).reshape(1, 2, 2 * n_z, d)
    every = jnp.broadcast_to(rows, (n_plane // 2, 2, 2 * n_z, d)).reshape(n_plane, 2 * n_z, d)
    every = swap(every, PLANE)
    n_rows = n_plane * n_z
    unit = jax.ShapeDtypeStruct((2, n_rows, hid), BF)
    block = jax.ShapeDtypeStruct(mine.shape, BF)
    work = 2 * n_rows * hid * d
    terms, hidden, g_pre = call(
        expert_kernel,
        [jax.ShapeDtypeStruct(every.shape, BF), unit, unit],
        8 * work,
        every,
        mine,
        other,
    )

    terms = swap(terms, PLANE).reshape(n_plane // 2, 2, 2, n_z, d)
    sums = jnp.sum(terms.astype(F32), axis=0).astype(BF)
    sums = sums.transpose(2, 0, 1, 3).reshape(n_z, 4, d)
    back = swap(sums, "z").reshape(n_z, 2, 2, d)
    slot_out, g_slot = back[:, :, 0].reshape(2 * n_z, d), back[:, :, 1].reshape(2 * n_z, d)

    (theirs,) = call(other_kernel, [block], 2 * work, every, hidden, g_pre)
    theirs = lax.ppermute(theirs, "core", OTHER)
    (home,) = call(mine_kernel, [block], 2 * work, every, hidden, g_pre, theirs)
    home = lax.ppermute(home, ("yl", "core"), BACK)

    g_comb = dot("td,sd->ts", cot, slot_out)
    g_clog = combine * (g_comb - jnp.sum(combine * g_comb, axis=1, keepdims=True))
    g_disp = dot("td,sd->ts", tok, g_slot)
    g_dlog = dispatch * (g_disp - jnp.sum(dispatch * g_disp, axis=0, keepdims=True))
    g_logits = (g_dlog + g_clog).astype(BF)

    term = dot("ts,td->sd", g_logits, tok)
    row = jnp.sum(swap(term, CHIPS), axis=0, keepdims=True)
    row = jnp.sum(swap(jnp.broadcast_to(row, (n_z, d)), "z"), axis=0, keepdims=True)
    row, home = lax.optimization_barrier((row, home))
    grad_w_in, grad_w_out = home[:hid].T, home[hid:]
    grad_router = swap(jnp.broadcast_to(row, (n_chips, d)), CHIPS).T

    grad_tokens = dot("ts,sd->td", dispatch_bf, g_slot) + dot("ts,ds->td", g_logits, router)
    return (grad_tokens.astype(BF)[None], grad_router, grad_w_in[None], grad_w_out[None])


def solution(mesh):
    fine = Mesh(np.asarray(mesh.devices).reshape(4, 2, 2, 16, 2), ("x", "yh", "yl", "z", "core"))
    images = P(("x", "yh", "yl", "z", "core"), None, None)
    first = P(("z", "core"), None, ("x", "yh", "yl"))
    second = P(("z", "core"), ("x", "yh", "yl"), None)
    return jax.shard_map(
        local,
        mesh=fine,
        in_specs=(images, P(), first, second, images),
        out_specs=(images, P(), first, second),
        check_vma=False,
    )
```

time: 202 us -> 177 us (0.88); the launches traced: 199 us -> 176 us
  waiting for transfers between devices: 62.5 us -> 27 us
  matrix products: 24.6 us -> 4.41 us
  blocking collectives: 19.2 us -> 38.6 us
  Pallas kernels: 0 us -> 8.06 us
  local copies, waits for them, and re-layouts: 10.2 us -> 14.3 us
  starting transfers between devices: 73.8 us -> 77.1 us
    all_to_all x6 -> x5, waiting for transfers between devices: 61.1 us -> 25.6 us  [swap(): return lax.all_to_all(x, axis, split_axis=0, concat_axis=0, tiled=True)]
    dot_general x20 -> x8, matrix products: 24.6 us -> 4.41 us  [dot(): return jnp.einsum(spec, a, b, preferred_element_type=F32)]
    all_to_all x1 -> x2, blocking collectives: 19.2 us -> 38.6 us  [swap(): return lax.all_to_all(x, axis, split_axis=0, concat_axis=0, tiled=True)]
    pallas_call x0 -> x3, Pallas kernels: none -> 8.06 us  [call(): pl.pallas_call(kernel, out_shape=outs, in_specs=[whole] * len(args), out_...]
    ppermute x1, starting transfers between devices: 2.34 us -> 9.6 us  [local(): other = lax.ppermute(mine, 'core', OTHER)]
    all_to_all x6 -> x5, starting transfers between devices: 58 us -> 51.2 us  [swap(): return lax.all_to_all(x, axis, split_axis=0, concat_axis=0, tiled=True)]
    unnamed x15 -> x21, local copies, waits for them, and re-layouts: 2.74 us -> 6.17 us
    convert_element_type x1 -> x0, other arithmetic: 2.94 us -> none  [local(): whole = (grads[0] + theirs.astype(F32)).astype(BF)]
  transfers between devices with their start and end apart: 10 -> 9, of which waited for: 7 -> 6; matrix products, arithmetic and copies ran while one was open for 14% -> 8% of each run, Pallas kernels for 0% -> 2%
where the time goes in v3:
time: 177 us; the launch traced here: 176 us
  starting transfers between devices  77.1 us (44%)
  blocking collectives  38.6 us (22%)
  waiting for transfers between devices  27 us (15%)
  local copies, waits for them, and re-layouts  14.3 us (8%)
  Pallas kernels  8.06 us (5%)
  other arithmetic  5.39 us (3%)
  matrix products  4.41 us (2%)
    all_to_all x5, starting transfers between devices, swap(): return lax.all_to_all(x, axis, split_axis=0, concat_axis=0, tiled=True)  51.2 us
    all_to_all x2, blocking collectives, swap(): return lax.all_to_all(x, axis, split_axis=0, concat_axis=0, tiled=True)  38.6 us
    all_to_all x5, waiting for transfers between devices, swap(): return lax.all_to_all(x, axis, split_axis=0, concat_axis=0, tiled=True)  25.6 us
    ppermute x1, starting transfers between devices, local(): other = lax.ppermute(mine, 'core', OTHER)  9.6 us
    pallas_call x3, Pallas kernels, call(): pl.pallas_call(kernel, out_shape=outs, in_specs=[whole] * len(args), out_...  8.06 us
    ppermute x1, starting transfers between devices, local(): theirs = lax.ppermute(theirs, 'core', OTHER)  6.54 us
    unnamed x21, local copies, waits for them, and re-layouts  6.17 us
    ppermute x1, starting transfers between devices, local(): home = lax.ppermute(home, ('yl', 'core'), BACK)  5.8 us
  transfers between devices with their start and end apart: 9, of which 6 were waited for; matrix products, arithmetic and copies ran while one was open for 8% of the time, Pallas kernels for 2%

profile of v3, /device:TPU:1, one launch (start us, length us, event | category | flops | bytes accessed | tf_op | source)
XLA Modules:
  0.0 175.8 jit_solution(17561657643845525028)
XLA Ops:
  0.7 2.8 %pad_maximum_fusion = bf16[640,1280]{1,0:T(8,128)(2,1)} fusion(bf16[320,1280]{1,0:T(8,128)(2,1)} %bitcast.63, bf16[320,1280]{1,0:T(8,128)(2,1)} %bitcast.64), kind=kLoop, calls=%fused_computation.6 | loop fusion | flops 3276800 | bytes 3276800 | tf_op jit(solution)/shard_map/concatenate | solution.py:99
  3.4 4.0 %collective-permute-start = (bf16[640,1280]{1,0:T(8,128)(2,1)}, bf16[640,1280]{1,0:T(8,128)(2,1)S(1)}, u32[]{:S(2)}, u32[]{:S(2)}) collective-permute-start(bf16[640,1280]{1,0:T(8,128)(2,1)} %pad_maximum_fusion), channel_id=1, source_target_pairs={{32,0},{0,1},{1,33},{33,32},{34,2},{2,3},{3,35},{35,34},{36,4},{4,... | collective-permute-start | bytes 4915208 | tf_op jit(solution)/shard_map/ppermute | solution.py:100
  7.5 0.4 fusion.20
  7.9 0.2 fusion.10
  8.1 0.2 convolution_convert_fusion
  8.4 0.2 convolution_convert_fusion.1
  8.7 0.8 copy.50
  9.5 14.9 %all-to-all-start = ((bf16[16,4,1280]{2,1,0:T(4,128)(2,1)}), bf16[16,4,1280]{2,1,0:T(4,128)(2,1)S(1)}, u32[]{:S(2)}, u32[]{:S(2)}) async-start(bf16[16,4,1280]{2,1,0:T(4,128)(2,1)} %copy.50), calls=%async_computation | async-start | bytes 327680 | tf_op jit(solution)/shard_map/all_to_all | solution.py:88
  24.4 1.4 collective-permute-done.mine
  25.8 9.6 %collective-permute-start.1 = (bf16[640,1280]{1,0:T(8,128)(2,1)S(1)}, bf16[640,1280]{1,0:T(8,128)(2,1)}, u32[]{:S(2)}, u32[]{:S(2)}) collective-permute-start(bf16[640,1280]{1,0:T(8,128)(2,1)S(1)} %collective-permute-done.mine), channel_id=1, source_target_pairs={{0,1},{1,0},{2,3},{3,2},{4,5},{5,4},{6,7},{7,6},{8,9},{9,8},{10,11... | collective-permute-start | bytes 4915208 | tf_op jit(solution)/shard_map/ppermute | solution.py:101
  35.4 2.4 %all-to-all-done = bf16[16,4,1280]{2,1,0:T(4,128)(2,1)S(1)} async-done(((bf16[16,4,1280]{2,1,0:T(4,128)(2,1)}), bf16[16,4,1280]{2,1,0:T(4,128)(2,1)S(1)}, u32[]{:S(2)}, u32[]{:S(2)}) %all-to-all-start) | async-done | bytes 163872 | tf_op jit(solution)/shard_map/all_to_all | solution.py:88
  37.8 0.1 broadcast_in_dim.17
  38.0 21.8 %all_to_all.44.every = bf16[16,32,1280]{2,1,0:T(8,128)(2,1)S(1)} all-to-all(bf16[16,32,1280]{2,1,0:T(8,128)(2,1)S(1)} %bitcast.62), channel_id=1, replica_groups=mesh['x'=4,'yh'=2,'yl'=2,'z'=16,'core'=2] {'x','yh','yl'}, dimensions={0} | all-to-all | bytes 2621440 | tf_op jit(solution)/shard_map/all_to_all | solution.py:88
  59.8 5.4 %shard_map.84 = (bf16[16,32,1280]{2,1,0:T(8,128)(2,1)}, bf16[2,256,320]{2,1,0:T(8,128)(2,1)S(1)}, bf16[2,256,320]{2,1,0:T(8,128)(2,1)S(1)}) custom-call(bf16[16,32,1280]{2,1,0:T(8,128)(2,1)S(1)} %all_to_all.44.every, bf16[640,1280]{1,0:T(8,128)(2,1)S(1)} %collective-permute-done.mine, bf16[640,1280]{1,0:T(8,128)(2,1)} %collective-permute-done.1.other), custom_call_target="tpu_custom_call" | custom-call | flops 1677721600 | bytes 6553600 | tf_op jit(solution)/shard_map/pallas_call | solution.py:77
  65.2 0.7 copy-done.1
  65.9 0.7 copy-done.4
  66.7 4.4 %all-to-all-start.2 = ((bf16[16,32,1280]{2,1,0:T(8,128)(2,1)}), bf16[16,32,1280]{2,1,0:T(8,128)(2,1)}, u32[]{:S(2)}, u32[]{:S(2)}) async-start(bf16[16,32,1280]{2,1,0:T(8,128)(2,1)} %get-tuple-element.9), calls=%async_computation.2 | async-start | bytes 2621440 | tf_op jit(solution)/shard_map/all_to_all | solution.py:88
  71.1 1.0 copy-done.2
  72.1 1.0 copy-done.5
  73.1 0.6 shard_map.85
  73.7 6.5 %collective-permute-start.2 = (bf16[640,1280]{1,0:T(8,128)(2,1)S(1)}, bf16[640,1280]{1,0:T(8,128)(2,1)}, u32[]{:S(2)}, u32[]{:S(2)}) collective-permute-start(bf16[640,1280]{1,0:T(8,128)(2,1)S(1)} %shard_map.85), channel_id=1, source_target_pairs={{0,1},{1,0},{2,3},{3,2},{4,5},{5,4},{6,7},{7,6},{8,9},{9,8},{10,11... | collective-permute-start | bytes 4915208 | tf_op jit(solution)/shard_map/ppermute | solution.py:136
  80.2 5.3 %all-to-all-done.2 = bf16[16,32,1280]{2,1,0:T(8,128)(2,1)} async-done(((bf16[16,32,1280]{2,1,0:T(8,128)(2,1)}), bf16[16,32,1280]{2,1,0:T(8,128)(2,1)}, u32[]{:S(2)}, u32[]{:S(2)}) %all-to-all-start.2) | async-done | bytes 1310752 | tf_op jit(solution)/shard_map/all_to_all | solution.py:88
  85.6 2.2 %reduce_sum.68 = bf16[2,2,16,1280]{3,2,1,0:T(8,128)(2,1)} reduce(bf16[8,2,2,16,1280]{4,3,2,1,0:T(8,128)(2,1)} %bitcast.10, bf16[]{:T(256)} %constant.2.clone.1), dimensions={0}, to_apply=%region_4.0 | reduce | flops 573440 | bytes 1474562 | tf_op jit(solution)/shard_map/reduce_sum | solution.py:130
  87.8 1.7 copy.52
  89.4 14.5 %all-to-all-start.3 = ((bf16[16,4,1280]{2,1,0:T(4,128)(2,1)}), bf16[16,4,1280]{2,1,0:T(4,128)(2,1)}, u32[]{:S(2)}, u32[]{:S(2)}) async-start(bf16[16,4,1280]{2,1,0:T(4,128)(2,1)} %copy.52), calls=%async_computation.3 | async-start | bytes 327680 | tf_op jit(solution)/shard_map/all_to_all | solution.py:88
  104.0 1.0 copy-done.3
  105.0 1.0 copy-done.6
  106.0 2.0 %shard_map.86 = bf16[640,1280]{1,0:T(8,128)(2,1)S(1)} custom-call(bf16[16,32,1280]{2,1,0:T(8,128)(2,1)S(1)} %all_to_all.44.every, bf16[2,256,320]{2,1,0:T(8,128)(2,1)S(1)} %copy-done.3, bf16[2,256,320]{2,1,0:T(8,128)(2,1)S(1)} %copy-done.6, bf16[640,1280]{1,0:T(8,128)(2,1)} %collective-permute-done.2.theirs), custom_call_target="tpu_custom_call" | custom-call | flops 419430400 | bytes 5242880 | tf_op jit(solution)/shard_map/pallas_call | solution.py:77
  108.0 5.8 %collective-permute-start.3 = (bf16[640,1280]{1,0:T(8,128)(2,1)S(1)}, bf16[640,1280]{1,0:T(8,128)(2,1)}, u32[]{:S(2)}, u32[]{:S(2)}) collective-permute-start(bf16[640,1280]{1,0:T(8,128)(2,1)S(1)} %shard_map.86), channel_id=1, source_target_pairs={{0,32},{1,0},{33,1},{32,33},{2,34},{3,2},{35,3},{34,35},{4,36},{5,... | collective-permute-start | bytes 4915208 | tf_op jit(solution)/shard_map/ppermute | solution.py:138
  113.8 2.4 %all-to-all-done.3 = bf16[16,4,1280]{2,1,0:T(4,128)(2,1)} async-done(((bf16[16,4,1280]{2,1,0:T(4,128)(2,1)}), bf16[16,4,1280]{2,1,0:T(4,128)(2,1)}, u32[]{:S(2)}, u32[]{:S(2)}) %all-to-all-start.3) | async-done | bytes 163872 | tf_op jit(solution)/shard_map/all_to_all | solution.py:88
  116.2 0.9 copy.53
  117.1 0.1 copy.55
  117.4 1.3 convolution_bitcast_fusion.1
  118.6 0.5 multiply_reduce_fusion.1
  119.1 0.3 convolution_bitcast_fusion
  119.3 0.2 copy.56
  119.5 16.8 %all_to_all.45 = f32[32,1,1280]{2,1,0:T(1,128)S(1)} all-to-all(f32[32,1,1280]{2,1,0:T(1,128)S(1)} %copy.56), channel_id=1, replica_groups=mesh['x'=4,'yh'=2,'yl'=2,'z'=16,'core'=2] {'x','yh','yl','core'}, dimensions={0} | all-to-all | bytes 327680 | tf_op jit(solution)/shard_map/all_to_all | solution.py:88
  136.3 0.1 reduce_sum.71
  136.4 0.7 broadcast_in_dim.19
  137.1 10.6 %all-to-all-start.5 = ((f32[16,1,1280]{2,1,0:T(1,128)}), f32[16,1,1280]{2,1,0:T(1,128)S(1)}, u32[]{:S(2)}, u32[]{:S(2)}) async-start(f32[16,1,1280]{2,1,0:T(1,128)} %broadcast_in_dim.19), calls=%async_computation.5 | async-start | bytes 163840 | tf_op jit(solution)/shard_map/all_to_all | solution.py:88
  147.7 0.4 fusion.14
  148.1 1.2 fusion.1
  149.3 10.2 %all-to-all-done.5 = f32[16,1,1280]{2,1,0:T(1,128)S(1)} async-done(((f32[16,1,1280]{2,1,0:T(1,128)}), f32[16,1,1280]{2,1,0:T(1,128)S(1)}, u32[]{:S(2)}, u32[]{:S(2)}) %all-to-all-start.5) | async-done | bytes 81952 | tf_op jit(solution)/shard_map/all_to_all | solution.py:88
  159.7 0.8 broadcast_in_dim.41
  160.4 6.7 %all-to-all-start.6 = ((f32[32,1,1280]{2,1,0:T(1,128)}), f32[32,1,1280]{2,1,0:T(1,128)S(1)}, u32[]{:S(2)}, u32[]{:S(2)}) async-start(f32[32,1,1280]{2,1,0:T(1,128)} %broadcast_in_dim.41), calls=%async_computation.6 | async-start | bytes 327680 | tf_op jit(solution)/shard_map/all_to_all | solution.py:88
  167.2 2.7 %slice_bitcast_fusion = (bf16[1,320,1280]{2,1,0:T(8,128)(2,1)}, bf16[1,1280,320]{1,2,0:T(8,128)(2,1)}) fusion(bf16[640,1280]{1,0:T(8,128)(2,1)} %collective-permute-done.3), kind=kLoop, calls=%fused_computation.9 | loop fusion | bytes 3276800 | tf_op jit(solution)/shard_map/broadcast_in_dim | solution.py:154
  169.8 5.3 %all-to-all-done.6 = f32[32,1,1280]{2,1,0:T(1,128)S(1)} async-done(((f32[32,1,1280]{2,1,0:T(1,128)}), f32[32,1,1280]{2,1,0:T(1,128)S(1)}, u32[]{:S(2)}, u32[]{:S(2)}) %all-to-all-start.6) | async-done | bytes 163872 | tf_op jit(solution)/shard_map/all_to_all | solution.py:88
  175.2 0.7 copy.61
  (30 shorter events, 0.5 us)
Async XLA Ops:
  0.6 6.8 %copy-start = (bf16[1,196,1280]{2,1,0:T(8,128)(2,1)S(1)}, bf16[1,196,1280]{2,1,0:T(8,128)(2,1)}, u32[]{:S(2)}) copy-start(bf16[1,196,1280]{2,1,0:T(8,128)(2,1)} %param.5) | copy-start | bytes 1505284
  0.6 6.8 %copy-start.8 = (bf16[1280,32]{0,1:T(8,128)(2,1)S(1)}, bf16[1280,32]{0,1:T(8,128)(2,1)}, u32[]{:S(2)}) copy-start(bf16[1280,32]{0,1:T(8,128)(2,1)} %param.6) | copy-start | bytes 245764
  0.7 7.4 %copy-start.7 = (bf16[1,196,1280]{2,1,0:T(8,128)(2,1)S(1)}, bf16[1,196,1280]{2,1,0:T(8,128)(2,1)}, u32[]{:S(2)}) copy-start(bf16[1,196,1280]{2,1,0:T(8,128)(2,1)} %param.9) | copy-start | bytes 1505284
  3.4 22.4 %collective-permute-start = (bf16[640,1280]{1,0:T(8,128)(2,1)}, bf16[640,1280]{1,0:T(8,128)(2,1)S(1)}, u32[]{:S(2)}, u32[]{:S(2)}) collective-permute-start(bf16[640,1280]{1,0:T(8,128)(2,1)} %pad_maximum_fusion), channel_id=1, source_target_pairs={{32,0},{0,1},{1,33},{33,32},{34,2},{2,3},{3,35},{35,34},{36,4},{4,... | collective-permute-start | bytes 4915208 | tf_op jit(solution)/shard_map/ppermute | solution.py:100
  9.5 28.3 %all-to-all-start = ((bf16[16,4,1280]{2,1,0:T(4,128)(2,1)}), bf16[16,4,1280]{2,1,0:T(4,128)(2,1)S(1)}, u32[]{:S(2)}, u32[]{:S(2)}) async-start(bf16[16,4,1280]{2,1,0:T(4,128)(2,1)} %copy.50), calls=%async_computation | async-start | bytes 327680 | tf_op jit(solution)/shard_map/all_to_all | solution.py:88
  25.8 34.0 %collective-permute-start.1 = (bf16[640,1280]{1,0:T(8,128)(2,1)S(1)}, bf16[640,1280]{1,0:T(8,128)(2,1)}, u32[]{:S(2)}, u32[]{:S(2)}) collective-permute-start(bf16[640,1280]{1,0:T(8,128)(2,1)S(1)} %collective-permute-done.mine), channel_id=1, source_target_pairs={{0,1},{1,0},{2,3},{3,2},{4,5},{5,4},{6,7},{7,6},{8,9},{9,8},{10,11... | collective-permute-start | bytes 4915208 | tf_op jit(solution)/shard_map/ppermute | solution.py:101
  65.2 0.7 copy-start.1
  65.9 0.7 copy-start.4
  66.7 18.9 %all-to-all-start.2 = ((bf16[16,32,1280]{2,1,0:T(8,128)(2,1)}), bf16[16,32,1280]{2,1,0:T(8,128)(2,1)}, u32[]{:S(2)}, u32[]{:S(2)}) async-start(bf16[16,32,1280]{2,1,0:T(8,128)(2,1)} %get-tuple-element.9), calls=%async_computation.2 | async-start | bytes 2621440 | tf_op jit(solution)/shard_map/all_to_all | solution.py:88
  71.1 1.0 copy-start.2
  72.1 1.0 copy-start.5
  73.7 30.2 %collective-permute-start.2 = (bf16[640,1280]{1,0:T(8,128)(2,1)S(1)}, bf16[640,1280]{1,0:T(8,128)(2,1)}, u32[]{:S(2)}, u32[]{:S(2)}) collective-permute-start(bf16[640,1280]{1,0:T(8,128)(2,1)S(1)} %shard_map.85), channel_id=1, source_target_pairs={{0,1},{1,0},{2,3},{3,2},{4,5},{5,4},{6,7},{7,6},{8,9},{9,8},{10,11... | collective-permute-start | bytes 4915208 | tf_op jit(solution)/shard_map/ppermute | solution.py:136
  89.4 26.7 %all-to-all-start.3 = ((bf16[16,4,1280]{2,1,0:T(4,128)(2,1)}), bf16[16,4,1280]{2,1,0:T(4,128)(2,1)}, u32[]{:S(2)}, u32[]{:S(2)}) async-start(bf16[16,4,1280]{2,1,0:T(4,128)(2,1)} %copy.52), calls=%async_computation.3 | async-start | bytes 327680 | tf_op jit(solution)/shard_map/all_to_all | solution.py:88
  104.0 1.0 copy-start.3
  105.0 1.0 copy-start.6
  108.0 51.6 %collective-permute-start.3 = (bf16[640,1280]{1,0:T(8,128)(2,1)S(1)}, bf16[640,1280]{1,0:T(8,128)(2,1)}, u32[]{:S(2)}, u32[]{:S(2)}) collective-permute-start(bf16[640,1280]{1,0:T(8,128)(2,1)S(1)} %shard_map.86), channel_id=1, source_target_pairs={{0,32},{1,0},{33,1},{32,33},{2,34},{3,2},{35,3},{34,35},{4,36},{5,... | collective-permute-start | bytes 4915208 | tf_op jit(solution)/shard_map/ppermute | solution.py:138
  119.1 29.1 %copy-start.9 = (bf16[1280,32]{0,1:T(8,128)(2,1)S(1)}, bf16[1280,32]{0,1:T(8,128)(2,1)}, u32[]{:S(2)}) copy-start(bf16[1280,32]{0,1:T(8,128)(2,1)} %param.6) | copy-start | bytes 245764
  137.1 22.4 %all-to-all-start.5 = ((f32[16,1,1280]{2,1,0:T(1,128)}), f32[16,1,1280]{2,1,0:T(1,128)S(1)}, u32[]{:S(2)}, u32[]{:S(2)}) async-start(f32[16,1,1280]{2,1,0:T(1,128)} %broadcast_in_dim.19), calls=%async_computation.5 | async-start | bytes 163840 | tf_op jit(solution)/shard_map/all_to_all | solution.py:88
  160.4 14.7 %all-to-all-start.6 = ((f32[32,1,1280]{2,1,0:T(1,128)}), f32[32,1,1280]{2,1,0:T(1,128)S(1)}, u32[]{:S(2)}, u32[]{:S(2)}) async-start(f32[32,1,1280]{2,1,0:T(1,128)} %broadcast_in_dim.41), calls=%async_computation.6 | async-start | bytes 327680 | tf_op jit(solution)/shard_map/all_to_all | solution.py:88

commit v4 on v3

v4 whole, which is shorter than its diff:
```python
import jax
import jax.numpy as jnp
import numpy as np
from jax import lax
from jax.experimental import pallas as pl
from jax.experimental.pallas import tpu as pltpu
from jax.sharding import Mesh, PartitionSpec as P

BF = jnp.bfloat16
F32 = jnp.float32
PLANE = ("x", "yh", "yl")
CHIPS = ("x", "yh", "yl", "core")
PAIR = ("yl", "core")
TURN = [(2, 0), (0, 1), (1, 3), (3, 2)]
BACK = [(b, a) for a, b in TURN]
OTHER = [(0, 1), (1, 0)]


def dot(spec, a, b):
    return jnp.einsum(spec, a, b, preferred_element_type=F32)


def nn(a, b):
    return jnp.dot(a, b, preferred_element_type=F32)


def nt(a, b):
    return lax.dot_general(a, b, (((1,), (1,)), ((), ())), preferred_element_type=F32)


def tn(a, b):
    return lax.dot_general(a, b, (((0,), (0,)), ((), ())), preferred_element_type=F32)


def rows_of(every):
    n, both, d = every.shape
    half = both // 2
    return every[:, :half].reshape(n * half, d), every[:, half:].reshape(n * half, d)


def expert_kernel(every, mine, in1, out1, terms, rows, hidden, g_pre, h_part, g_part, sems):
    hid = mine.shape[0] // 2
    n, both, d = every.shape
    saves = [pltpu.make_async_copy(every, rows, sems.at[0])]
    saves[0].start()
    x, g = rows_of(every[...])
    out, back = 0.0, 0.0
    for i, (win, wout) in enumerate(((mine[:hid], mine[hid:]), (in1[...], out1[...]))):
        pre = nt(x, win)
        cdf = 0.5 * (1.0 + lax.erf(pre * 0.7071067811865476))
        h = (pre * cdf).astype(BF)
        slope = cdf + pre * jnp.exp(-0.5 * pre * pre) * 0.3989422804014327
        gp = (nt(g, wout) * slope).astype(BF)
        h_part[i] = h
        g_part[i] = gp
        saves.append(pltpu.make_async_copy(h_part.at[i], hidden.at[i], sems.at[1 + 2 * i]))
        saves.append(pltpu.make_async_copy(g_part.at[i], g_pre.at[i], sems.at[2 + 2 * i]))
        saves[-2].start()
        saves[-1].start()
        out = out + nn(h, wout)
        back = back + nn(gp, win)
    terms[:, : both // 2] = out.astype(BF).reshape(n, both // 2, d)
    terms[:, both // 2 :] = back.astype(BF).reshape(n, both // 2, d)
    for save in saves:
        save.wait()


def grads_kernel(every, hidden, g_pre, kept, given):
    hid = kept.shape[0] // 2
    x, g = rows_of(every[...])
    for i, grads in enumerate((kept, given)):
        grads[:hid] = tn(g_pre[i], x).astype(BF)
        grads[hid:] = tn(hidden[i], g).astype(BF)


def add_kernel(kept, given, grads_in, grads_out):
    hid = grads_in.shape[0]
    grads_in[...] = (kept[:hid].astype(F32) + given[:hid].astype(F32)).astype(BF)
    grads_out[...] = (kept[hid:].astype(F32) + given[hid:].astype(F32)).astype(BF)


def place_kernel(a, b, a_out, b_out):
    a_out[...] = a[...]
    b_out[...] = b[...]


def sum_kernel(terms, sums):
    n, both, d = terms.shape
    n_z = both // 2
    for parity in range(2):
        for kind in range(2):
            total = 0.0
            for chip in range(parity, n, 2):
                total = total + terms[chip, kind * n_z : (kind + 1) * n_z].astype(F32)
            sums[:, parity * 2 + kind] = total.astype(BF)


def call(kernel, outs, flops, *args, saved=(), scratch=(), vmem=8):
    moved = sum(a.size * a.dtype.itemsize for a in (*args, *outs, *saved))
    whole = pl.BlockSpec(memory_space=pltpu.VMEM)
    return pl.pallas_call(
        kernel,
        out_shape=[*outs, *(pltpu.HBM(a.shape, a.dtype) for a in saved)],
        in_specs=[whole] * len(args),
        out_specs=[whole] * len(outs) + [pl.BlockSpec(memory_space=pltpu.HBM)] * len(saved),
        scratch_shapes=scratch,
        compiler_params=pltpu.CompilerParams(vmem_limit_bytes=vmem * 2**20),
        cost_estimate=pl.CostEstimate(flops=flops, bytes_accessed=moved, transcendentals=0),
    )(*args)


def swap(x, axis):
    return lax.all_to_all(x, axis, split_axis=0, concat_axis=0, tiled=True)


def local(tokens, router, w_in, w_out, cotangent):
    n_z = lax.axis_size("z")
    n_plane = lax.axis_size(PLANE)
    n_chips = lax.axis_size(CHIPS)
    tok, cot = tokens[0], cotangent[0]
    d = tok.shape[1]
    hid = w_out.shape[1]

    logits = dot("td,ds->ts", tok, router)
    dispatch = jax.nn.softmax(logits, axis=0)
    combine = jax.nn.softmax(logits, axis=1)
    dispatch_bf = dispatch.astype(BF)
    combine_bf = combine.astype(BF)
    slot_in = dot("ts,td->sd", dispatch_bf, tok).astype(BF)
    g_late = dot("ts,td->sd", combine_bf, cot).astype(BF)

    rows = jnp.stack([slot_in.reshape(n_z, 2, d), g_late.reshape(n_z, 2, d)], axis=2)
    rows = rows.reshape(n_z, 4, d)
    rows, win, wout = lax.optimization_barrier((rows, w_in[0].T, w_out[0]))
    mine = lax.ppermute(jnp.concatenate([win, wout], axis=0), PAIR, TURN)
    rows = swap(rows, "z")
    in1 = lax.ppermute(mine[:hid], "core", OTHER)
    out1 = lax.ppermute(mine[hid:], "core", OTHER)
    rows = rows.reshape(n_z, 2, 2, d)
    rows = rows.transpose(1, 2, 0, 3).reshape(1, 2, 2 * n_z, d)
    every = jnp.broadcast_to(rows, (n_plane // 2, 2, 2 * n_z, d)).reshape(n_plane, 2 * n_z, d)
    every = swap(every, PLANE)
    n_rows = n_plane * n_z
    unit = jax.ShapeDtypeStruct((2, n_rows, hid), BF)
    block = jax.ShapeDtypeStruct((2 * hid, d), BF)
    half = jax.ShapeDtypeStruct((hid, d), BF)
    work = 2 * n_rows * hid * d
    terms, rows, hidden, g_pre = call(
        expert_kernel,
        [jax.ShapeDtypeStruct(every.shape, BF)],
        8 * work,
        every,
        mine,
        in1,
        out1,
        saved=[every, unit, unit],
        scratch=[pltpu.VMEM(unit.shape, BF)] * 2 + [pltpu.SemaphoreType.DMA((5,))],
        vmem=16,
    )
    kept, given = call(grads_kernel, [block, block], 4 * work, rows, hidden, g_pre, vmem=12)
    given = lax.ppermute(given, "core", OTHER)

    terms = swap(terms, PLANE)
    (sums,) = call(sum_kernel, [jax.ShapeDtypeStruct((n_z, 4, d), BF)], terms.size, terms)
    home_in, home_out = call(add_kernel, [half, half], block.size, kept, given)
    home_in = lax.ppermute(home_in, PAIR, BACK)
    back = swap(sums, "z").reshape(n_z, 2, 2, d)
    slot_out, g_slot = back[:, :, 0].reshape(2 * n_z, d), back[:, :, 1].reshape(2 * n_z, d)

    g_comb = dot("td,sd->ts", cot, slot_out)
    g_clog = combine * (g_comb - jnp.sum(combine * g_comb, axis=1, keepdims=True))
    g_disp = dot("td,sd->ts", tok, g_slot)
    g_dlog = dispatch * (g_disp - jnp.sum(dispatch * g_disp, axis=0, keepdims=True))
    g_logits = (g_dlog + g_clog).astype(BF)

    term = dot("ts,td->sd", g_logits, tok)
    row, home_in, home_out = lax.optimization_barrier((swap(term, CHIPS), home_in, home_out))
    home_out = lax.ppermute(home_out, PAIR, BACK)
    row = jnp.sum(row, axis=0, keepdims=True)
    row = jnp.sum(swap(jnp.broadcast_to(row, (n_z, d)), "z"), axis=0, keepdims=True)
    row, home_in, home_out = lax.optimization_barrier((row, home_in, home_out))
    grad_w_in, grad_w_out = call(place_kernel, [half, half], block.size, home_in, home_out)
    grad_router = swap(jnp.broadcast_to(row, (n_chips, d)), CHIPS).T

    grad_tokens = dot("ts,sd->td", dispatch_bf, g_slot) + dot("ts,ds->td", g_logits, router)
    return (grad_tokens.astype(BF)[None], grad_router, grad_w_in.T[None], grad_w_out[None])


def solution(mesh):
    fine = Mesh(np.asarray(mesh.devices).reshape(4, 2, 2, 16, 2), ("x", "yh", "yl", "z", "core"))
    images = P(("x", "yh", "yl", "z", "core"), None, None)
    first = P(("z", "core"), None, ("x", "yh", "yl"))
    second = P(("z", "core"), ("x", "yh", "yl"), None)
    return jax.shard_map(
        local,
        mesh=fine,
        in_specs=(images, P(), first, second, images),
        out_specs=(images, P(), first, second),
        check_vma=False,
    )
```

time: 177 us -> 168 us (0.949)
  starting transfers between devices: 77.1 us -> 52.9 us
  waiting for transfers between devices: 27 us -> 34.4 us
  blocking collectives: 38.6 us -> 45.5 us
  matrix products: 4.41 us -> 8.68 us
  other arithmetic: 5.39 us -> 1.61 us
  Pallas kernels: 8.06 us -> 11.2 us
  local copies, waits for them, and re-layouts: 14.3 us -> 12 us
    all_to_all x5, starting transfers between devices: 51.2 us -> 29.3 us  [swap(): return lax.all_to_all(x, axis, split_axis=0, concat_axis=0, tiled=True)]
    all_to_all x5, waiting for transfers between devices: 25.6 us -> 34.4 us  [swap(): return lax.all_to_all(x, axis, split_axis=0, concat_axis=0, tiled=True)]
    all_to_all x2, blocking collectives: 38.6 us -> 45.5 us  [swap(): return lax.all_to_all(x, axis, split_axis=0, concat_axis=0, tiled=True)]
    dot_general x8, matrix products: 4.41 us -> 8.68 us  [dot(): return jnp.einsum(spec, a, b, preferred_element_type=F32)]
    pallas_call x3 -> x5, Pallas kernels: 8.06 us -> 11.2 us  [call(): pl.pallas_call(kernel, out_shape=[*outs, *(pltpu.HBM(a.shape, a.dtype) fo...]
    broadcast_in_dim x1 -> x0, local copies, waits for them, and re-layouts: 2.66 us -> none  [local(): grad_w_out[None]]
    reshape x2 -> x1, local copies, waits for them, and re-layouts: 2.42 us -> 0.06 us  [local(): back = swap(sums, 'z').reshape(n_z, 2, 2, d)]
    ppermute x4 -> x6, starting transfers between devices: 26 us -> 23.6 us  [the longest x1 5.92 us: local(): home_in = lax.ppermute(home_in, PAIR, BACK)]
  transfers between devices with their start and end apart: 9 -> 11, of which waited for: 6 -> 5; matrix products, arithmetic and copies ran while one was open for 8% -> 6% of each run, Pallas kernels for 2% -> 4%
where the time goes in v4:
time: 168 us; the launch traced here: 167 us
  starting transfers between devices  52.9 us (31%)
  blocking collectives  45.5 us (27%)
  waiting for transfers between devices  34.4 us (20%)
  local copies, waits for them, and re-layouts  12 us (7%)
  Pallas kernels  11.2 us (7%)
  matrix products  8.68 us (5%)
    all_to_all x2, blocking collectives, swap(): return lax.all_to_all(x, axis, split_axis=0, concat_axis=0, tiled=True)  45.5 us
    all_to_all x5, waiting for transfers between devices, swap(): return lax.all_to_all(x, axis, split_axis=0, concat_axis=0, tiled=True)  34.4 us
    all_to_all x5, starting transfers between devices, swap(): return lax.all_to_all(x, axis, split_axis=0, concat_axis=0, tiled=True)  29.3 us
    pallas_call x5, Pallas kernels, call(): pl.pallas_call(kernel, out_shape=[*outs, *(pltpu.HBM(a.shape, a.dtype) fo...  11.2 us
    dot_general x8, matrix products, dot(): return jnp.einsum(spec, a, b, preferred_element_type=F32)  8.68 us
    unnamed x18, local copies, waits for them, and re-layouts  6.75 us
    ppermute x1, starting transfers between devices, local(): home_in = lax.ppermute(home_in, PAIR, BACK)  5.92 us
    ppermute x1, starting transfers between devices, local(): out1 = lax.ppermute(mine[hid:], 'core', OTHER)  5.33 us
  transfers between devices with their start and end apart: 11, of which 5 were waited for; matrix products, arithmetic and copies ran while one was open for 6% of the time, Pallas kernels for 4%

profile of v4, /device:TPU:1, one launch (start us, length us, event | category | flops | bytes accessed | tf_op | source)
XLA Modules:
  0.0 167.3 jit_solution(6124469565679887622)
XLA Ops:
  0.7 1.0 copy-done
  1.7 1.4 fusion.20
  3.0 0.2 fusion.10
  3.2 1.2 convolution_convert_fusion
  4.6 0.2 convolution_convert_fusion.1
  4.9 1.3 pad_maximum_fusion
  6.2 4.0 %collective-permute-start = (bf16[640,1280]{1,0:T(8,128)(2,1)}, bf16[640,1280]{1,0:T(8,128)(2,1)S(1)}, u32[]{:S(2)}, u32[]{:S(2)}) collective-permute-start(bf16[640,1280]{1,0:T(8,128)(2,1)} %pad_maximum_fusion), channel_id=1, source_target_pairs={{32,0},{0,1},{1,33},{33,32},{34,2},{2,3},{3,35},{35,34},{36,4},{4,... | collective-permute-start | bytes 4915208 | tf_op jit(solution)/shard_map/ppermute | solution.py:135
  10.3 0.1 copy.35
  10.4 28.1 %all_to_all.47 = bf16[16,4,1280]{2,1,0:T(4,128)(2,1)S(1)} all-to-all(bf16[16,4,1280]{2,1,0:T(4,128)(2,1)S(1)} %copy.35), channel_id=1, replica_groups=mesh['x'=4,'yh'=2,'yl'=2,'z'=16,'core'=2] {'z'}, dimensions={0} | all-to-all | bytes 327680 | tf_op jit(solution)/shard_map/all_to_all | solution.py:113
  38.5 1.2 broadcast_in_dim.17
  39.7 6.0 %all-to-all-start.1 = ((bf16[16,32,1280]{2,1,0:T(8,128)(2,1)}), bf16[16,32,1280]{2,1,0:T(8,128)(2,1)S(1)}, u32[]{:S(2)}, u32[]{:S(2)}) async-start(bf16[16,32,1280]{2,1,0:T(8,128)(2,1)} %bitcast.54), calls=%async_computation.1 | async-start | bytes 2621440 | tf_op jit(solution)/shard_map/all_to_all | solution.py:113
  45.7 1.3 fusion.21
  46.9 5.3 %collective-permute-start.2 = (bf16[320,1280]{1,0:T(8,128)(2,1)}, bf16[320,1280]{1,0:T(8,128)(2,1)}, u32[]{:S(2)}, u32[]{:S(2)}) collective-permute-start(bf16[320,1280]{1,0:T(8,128)(2,1)} %get-tuple-element.50), channel_id=1, source_target_pairs={{0,1},{1,0},{2,3},{3,2},{4,5},{5,4},{6,7},{7,6},{8,9},{9,8},{10,11... | collective-permute-start | bytes 2457608 | tf_op jit(solution)/shard_map/ppermute | solution.py:138
  52.3 1.9 %collective-permute-start.1 = (bf16[320,1280]{1,0:T(8,128)(2,1)}, bf16[320,1280]{1,0:T(8,128)(2,1)}, u32[]{:S(2)}, u32[]{:S(2)}) collective-permute-start(bf16[320,1280]{1,0:T(8,128)(2,1)} %get-tuple-element.51), channel_id=1, source_target_pairs={{0,1},{1,0},{2,3},{3,2},{4,5},{5,4},{6,7},{7,6},{8,9},{9,8},{10,11... | collective-permute-start | bytes 2457608 | tf_op jit(solution)/shard_map/ppermute | solution.py:137
  54.2 8.2 %all-to-all-done.1.every = bf16[16,32,1280]{2,1,0:T(8,128)(2,1)S(1)} async-done(((bf16[16,32,1280]{2,1,0:T(8,128)(2,1)}), bf16[16,32,1280]{2,1,0:T(8,128)(2,1)S(1)}, u32[]{:S(2)}, u32[]{:S(2)}) %all-to-all-start.1) | async-done | bytes 1310752 | tf_op jit(solution)/shard_map/all_to_all | solution.py:113
  62.5 4.8 %shard_map.84 = (bf16[16,32,1280]{2,1,0:T(8,128)(2,1)S(1)}, bf16[16,32,1280]{2,1,0:T(8,128)(2,1)}, bf16[2,256,320]{2,1,0:T(8,128)(2,1)}, bf16[2,256,320]{2,1,0:T(8,128)(2,1)}) custom-call(bf16[16,32,1280]{2,1,0:T(8,128)(2,1)S(1)} %all-to-all-done.1.every, bf16[640,1280]{1,0:T(8,128)(2,1)S(1)} %collective-permute-done.mine, ...), custom_call_target="tpu_custom_call" | custom-call | flops 1677721600 | bytes 7864320 | tf_op jit(solution)/shard_map/pallas_call | solution.py:101
  67.3 1.1 copy-done.1
  68.4 5.8 %all-to-all-start.2 = ((bf16[16,32,1280]{2,1,0:T(8,128)(2,1)}), bf16[16,32,1280]{2,1,0:T(8,128)(2,1)S(1)}, u32[]{:S(2)}, u32[]{:S(2)}) async-start(bf16[16,32,1280]{2,1,0:T(8,128)(2,1)} %copy-done.1), calls=%async_computation.2 | async-start | bytes 2621440 | tf_op jit(solution)/shard_map/all_to_all | solution.py:113
  74.2 1.3 copy-done.3
  75.5 1.0 copy-done.4
  76.5 1.0 copy-done.5
  77.5 2.2 %shard_map.86 = (bf16[640,1280]{1,0:T(8,128)(2,1)S(1)}, bf16[640,1280]{1,0:T(8,128)(2,1)}) custom-call(bf16[16,32,1280]{2,1,0:T(8,128)(2,1)S(1)} %copy-done.3, bf16[2,256,320]{2,1,0:T(8,128)(2,1)S(1)} %copy-done.4, bf16[2,256,320]{2,1,0:T(8,128)(2,1)S(1)} %copy-done.5), custom_call_target="tpu_custom_call" | custom-call | flops 838860800 | bytes 5242880 | tf_op jit(solution)/shard_map/pallas_call | solution.py:101
  79.7 4.2 %collective-permute-start.3 = (bf16[640,1280]{1,0:T(8,128)(2,1)}, bf16[640,1280]{1,0:T(8,128)(2,1)}, u32[]{:S(2)}, u32[]{:S(2)}) collective-permute-start(bf16[640,1280]{1,0:T(8,128)(2,1)} %get-tuple-element.31), channel_id=1, source_target_pairs={{0,1},{1,0},{2,3},{3,2},{4,5},{5,4},{6,7},{7,6},{8,9},{9,8},{10,11... | collective-permute-start | bytes 4915208 | tf_op jit(solution)/shard_map/ppermute | solution.py:161
  83.9 7.9 %all-to-all-done.2.terms = bf16[16,32,1280]{2,1,0:T(8,128)(2,1)S(1)} async-done(((bf16[16,32,1280]{2,1,0:T(8,128)(2,1)}), bf16[16,32,1280]{2,1,0:T(8,128)(2,1)S(1)}, u32[]{:S(2)}, u32[]{:S(2)}) %all-to-all-start.2) | async-done | bytes 1310752 | tf_op jit(solution)/shard_map/all_to_all | solution.py:113
  91.8 0.3 shard_map.85
  92.1 0.7 copy-done.2
  92.7 7.7 %all-to-all-start.3 = ((bf16[16,4,1280]{2,1,0:T(4,128)(2,1)}), bf16[16,4,1280]{2,1,0:T(4,128)(2,1)S(1)}, u32[]{:S(2)}, u32[]{:S(2)}) async-start(bf16[16,4,1280]{2,1,0:T(4,128)(2,1)} %copy-done.2), calls=%async_computation.3 | async-start | bytes 327680 | tf_op jit(solution)/shard_map/all_to_all | solution.py:113
  100.4 2.6 %shard_map.87 = (bf16[320,1280]{1,0:T(8,128)(2,1)}, bf16[320,1280]{1,0:T(8,128)(2,1)S(1)}) custom-call(bf16[640,1280]{1,0:T(8,128)(2,1)S(1)} %get-tuple-element.30.kept, bf16[640,1280]{1,0:T(8,128)(2,1)} %collective-permute-done.3.given), custom_call_target="tpu_custom_call" | custom-call | flops 819200 | bytes 4915200 | tf_op jit(solution)/shard_map/pallas_call | solution.py:101
  103.0 5.9 %collective-permute-start.4 = (bf16[320,1280]{1,0:T(8,128)(2,1)}, bf16[320,1280]{1,0:T(8,128)(2,1)S(1)}, u32[]{:S(2)}, u32[]{:S(2)}) collective-permute-start(bf16[320,1280]{1,0:T(8,128)(2,1)} %get-tuple-element.32), channel_id=1, source_target_pairs={{0,32},{1,0},{33,1},{32,33},{2,34},{3,2},{35,3},{34,35},{4,36},{5,... | collective-permute-start | bytes 2457608 | tf_op jit(solution)/shard_map/ppermute | solution.py:166
  109.0 3.6 %all-to-all-done.3 = bf16[16,4,1280]{2,1,0:T(4,128)(2,1)S(1)} async-done(((bf16[16,4,1280]{2,1,0:T(4,128)(2,1)}), bf16[16,4,1280]{2,1,0:T(4,128)(2,1)S(1)}, u32[]{:S(2)}, u32[]{:S(2)}) %all-to-all-start.3) | async-done | bytes 163872 | tf_op jit(solution)/shard_map/all_to_all | solution.py:113
  112.6 0.1 reshape.45
  112.6 0.8 slice_reduce_fusion
  113.6 1.3 convolution_bitcast_fusion.1
  114.8 0.5 multiply_reduce_fusion.1
  115.3 0.3 convolution_bitcast_fusion
  115.5 0.2 copy.39
  115.7 17.4 %all_to_all.48 = f32[32,1,1280]{2,1,0:T(1,128)S(1)} all-to-all(f32[32,1,1280]{2,1,0:T(1,128)S(1)} %copy.39), channel_id=1, replica_groups=mesh['x'=4,'yh'=2,'yl'=2,'z'=16,'core'=2] {'x','yh','yl','core'}, dimensions={0} | all-to-all | bytes 327680 | tf_op jit(solution)/shard_map/all_to_all | solution.py:113
  133.2 2.3 %collective-permute-start.5 = (bf16[320,1280]{1,0:T(8,128)(2,1)S(1)}, bf16[320,1280]{1,0:T(8,128)(2,1)S(1)}, u32[]{:S(2)}, u32[]{:S(2)}) collective-permute-start(bf16[320,1280]{1,0:T(8,128)(2,1)S(1)} %get-tuple-element.36), channel_id=1, source_target_pairs={{0,32},{1,0},{33,1},{32,33},{2,34},{3,2},{35,3},{34,35},{4,36},{5,... | collective-permute-start | bytes 2457608 | tf_op jit(solution)/shard_map/ppermute | solution.py:178
  135.5 0.7 broadcast_in_dim.19
  136.2 3.5 %all-to-all-start.5 = ((f32[16,1,1280]{2,1,0:T(1,128)}), f32[16,1,1280]{2,1,0:T(1,128)S(1)}, u32[]{:S(2)}, u32[]{:S(2)}) async-start(f32[16,1,1280]{2,1,0:T(1,128)} %broadcast_in_dim.19), calls=%async_computation.5 | async-start | bytes 163840 | tf_op jit(solution)/shard_map/all_to_all | solution.py:113
  139.7 1.4 fusion.14
  141.1 10.4 %all-to-all-done.5 = f32[16,1,1280]{2,1,0:T(1,128)S(1)} async-done(((f32[16,1,1280]{2,1,0:T(1,128)}), f32[16,1,1280]{2,1,0:T(1,128)S(1)}, u32[]{:S(2)}, u32[]{:S(2)}) %all-to-all-start.5) | async-done | bytes 81952 | tf_op jit(solution)/shard_map/all_to_all | solution.py:113
  151.6 0.8 broadcast_in_dim.41
  152.4 6.3 %all-to-all-start.6 = ((f32[32,1,1280]{2,1,0:T(1,128)}), f32[32,1,1280]{2,1,0:T(1,128)S(1)}, u32[]{:S(2)}, u32[]{:S(2)}) async-start(f32[32,1,1280]{2,1,0:T(1,128)} %broadcast_in_dim.41), calls=%async_computation.6 | async-start | bytes 327680 | tf_op jit(solution)/shard_map/all_to_all | solution.py:113
  158.7 2.5 %fusion.1 = bf16[1,196,1280]{2,1,0:T(8,128)(2,1)} fusion(f32[196,1280]{1,0:T(8,128)} %fusion.14, bf16[1280,32]{0,1:T(8,128)(2,1)} %param.6, f32[196,32]{0,1:T(8,128)S(1)} %convolution_bitcast_fusion.1, f32[196,32]{0,1:T(8,128)S(1)} %get-tuple-element.53, f32[196]{0:T(256)S(1)} %get-tuple-element.45, f32[32]{0:T(128)S(1)} %get-tuple-element.44, ...), kind=kOutput, calls=%fused_computation.2 | convolution fusion | flops 16620800 | bytes 1665200 | tf_op jit(solution)/shard_map/ts,ds->td/dot_general | solution.py:20
  161.1 1.3 shard_map.88
  162.4 4.3 %all-to-all-done.6 = f32[32,1,1280]{2,1,0:T(1,128)S(1)} async-done(((f32[32,1,1280]{2,1,0:T(1,128)}), f32[32,1,1280]{2,1,0:T(1,128)S(1)}, u32[]{:S(2)}, u32[]{:S(2)}) %all-to-all-start.6) | async-done | bytes 163872 | tf_op jit(solution)/shard_map/all_to_all | solution.py:113
  166.7 0.7 copy.50
  (29 shorter events, 0.4 us)
Async XLA Ops:
  0.6 1.0 copy-start
  0.6 4.3 %copy-start.6 = (bf16[1,320,1280]{2,1,0:T(8,128)(2,1)S(1)}, bf16[1,320,1280]{2,1,0:T(8,128)(2,1)}, u32[]{:S(2)}) copy-start(bf16[1,320,1280]{2,1,0:T(8,128)(2,1)} %param.8) | copy-start | bytes 2457604
  1.7 3.3 %copy-start.7 = (bf16[1,1280,320]{1,2,0:T(8,128)(2,1)S(1)}, bf16[1,1280,320]{1,2,0:T(8,128)(2,1)}, u32[]{:S(2)}) copy-start(bf16[1,1280,320]{1,2,0:T(8,128)(2,1)} %param.7) | copy-start | bytes 2457604
  6.2 39.4 %collective-permute-start = (bf16[640,1280]{1,0:T(8,128)(2,1)}, bf16[640,1280]{1,0:T(8,128)(2,1)S(1)}, u32[]{:S(2)}, u32[]{:S(2)}) collective-permute-start(bf16[640,1280]{1,0:T(8,128)(2,1)} %pad_maximum_fusion), channel_id=1, source_target_pairs={{32,0},{0,1},{1,33},{33,32},{34,2},{2,3},{3,35},{35,34},{36,4},{4,... | collective-permute-start | bytes 4915208 | tf_op jit(solution)/shard_map/ppermute | solution.py:135
  39.7 22.8 %all-to-all-start.1 = ((bf16[16,32,1280]{2,1,0:T(8,128)(2,1)}), bf16[16,32,1280]{2,1,0:T(8,128)(2,1)S(1)}, u32[]{:S(2)}, u32[]{:S(2)}) async-start(bf16[16,32,1280]{2,1,0:T(8,128)(2,1)} %bitcast.54), calls=%async_computation.1 | async-start | bytes 2621440 | tf_op jit(solution)/shard_map/all_to_all | solution.py:113
  46.9 15.5 %collective-permute-start.2 = (bf16[320,1280]{1,0:T(8,128)(2,1)}, bf16[320,1280]{1,0:T(8,128)(2,1)}, u32[]{:S(2)}, u32[]{:S(2)}) collective-permute-start(bf16[320,1280]{1,0:T(8,128)(2,1)} %get-tuple-element.50), channel_id=1, source_target_pairs={{0,1},{1,0},{2,3},{3,2},{4,5},{5,4},{6,7},{7,6},{8,9},{9,8},{10,11... | collective-permute-start | bytes 2457608 | tf_op jit(solution)/shard_map/ppermute | solution.py:138
  52.3 10.2 %collective-permute-start.1 = (bf16[320,1280]{1,0:T(8,128)(2,1)}, bf16[320,1280]{1,0:T(8,128)(2,1)}, u32[]{:S(2)}, u32[]{:S(2)}) collective-permute-start(bf16[320,1280]{1,0:T(8,128)(2,1)} %get-tuple-element.51), channel_id=1, source_target_pairs={{0,1},{1,0},{2,3},{3,2},{4,5},{5,4},{6,7},{7,6},{8,9},{9,8},{10,11... | collective-permute-start | bytes 2457608 | tf_op jit(solution)/shard_map/ppermute | solution.py:137
  67.3 1.1 copy-start.1
  68.4 23.4 %all-to-all-start.2 = ((bf16[16,32,1280]{2,1,0:T(8,128)(2,1)}), bf16[16,32,1280]{2,1,0:T(8,128)(2,1)S(1)}, u32[]{:S(2)}, u32[]{:S(2)}) async-start(bf16[16,32,1280]{2,1,0:T(8,128)(2,1)} %copy-done.1), calls=%async_computation.2 | async-start | bytes 2621440 | tf_op jit(solution)/shard_map/all_to_all | solution.py:113
  74.2 1.3 copy-start.3
  75.5 1.0 copy-start.4
  76.5 1.0 copy-start.5
  79.7 20.7 %collective-permute-start.3 = (bf16[640,1280]{1,0:T(8,128)(2,1)}, bf16[640,1280]{1,0:T(8,128)(2,1)}, u32[]{:S(2)}, u32[]{:S(2)}) collective-permute-start(bf16[640,1280]{1,0:T(8,128)(2,1)} %get-tuple-element.31), channel_id=1, source_target_pairs={{0,1},{1,0},{2,3},{3,2},{4,5},{5,4},{6,7},{7,6},{8,9},{9,8},{10,11... | collective-permute-start | bytes 4915208 | tf_op jit(solution)/shard_map/ppermute | solution.py:161
  92.1 0.7 copy-start.2
  92.7 19.8 %all-to-all-start.3 = ((bf16[16,4,1280]{2,1,0:T(4,128)(2,1)}), bf16[16,4,1280]{2,1,0:T(4,128)(2,1)S(1)}, u32[]{:S(2)}, u32[]{:S(2)}) async-start(bf16[16,4,1280]{2,1,0:T(4,128)(2,1)} %copy-done.2), calls=%async_computation.3 | async-start | bytes 327680 | tf_op jit(solution)/shard_map/all_to_all | solution.py:113
  103.0 30.1 %collective-permute-start.4 = (bf16[320,1280]{1,0:T(8,128)(2,1)}, bf16[320,1280]{1,0:T(8,128)(2,1)S(1)}, u32[]{:S(2)}, u32[]{:S(2)}) collective-permute-start(bf16[320,1280]{1,0:T(8,128)(2,1)} %get-tuple-element.32), channel_id=1, source_target_pairs={{0,32},{1,0},{33,1},{32,33},{2,34},{3,2},{35,3},{34,35},{4,36},{5,... | collective-permute-start | bytes 2457608 | tf_op jit(solution)/shard_map/ppermute | solution.py:166
  133.2 18.4 %collective-permute-start.5 = (bf16[320,1280]{1,0:T(8,128)(2,1)S(1)}, bf16[320,1280]{1,0:T(8,128)(2,1)S(1)}, u32[]{:S(2)}, u32[]{:S(2)}) collective-permute-start(bf16[320,1280]{1,0:T(8,128)(2,1)S(1)} %get-tuple-element.36), channel_id=1, source_target_pairs={{0,32},{1,0},{33,1},{32,33},{2,34},{3,2},{35,3},{34,35},{4,36},{5,... | collective-permute-start | bytes 2457608 | tf_op jit(solution)/shard_map/ppermute | solution.py:178
  136.2 15.4 %all-to-all-start.5 = ((f32[16,1,1280]{2,1,0:T(1,128)}), f32[16,1,1280]{2,1,0:T(1,128)S(1)}, u32[]{:S(2)}, u32[]{:S(2)}) async-start(f32[16,1,1280]{2,1,0:T(1,128)} %broadcast_in_dim.19), calls=%async_computation.5 | async-start | bytes 163840 | tf_op jit(solution)/shard_map/all_to_all | solution.py:113
  152.4 14.3 %all-to-all-start.6 = ((f32[32,1,1280]{2,1,0:T(1,128)}), f32[32,1,1280]{2,1,0:T(1,128)S(1)}, u32[]{:S(2)}, u32[]{:S(2)}) async-start(f32[32,1,1280]{2,1,0:T(1,128)} %broadcast_in_dim.41), calls=%async_computation.6 | async-start | bytes 327680 | tf_op jit(solution)/shard_map/all_to_all | solution.py:113

commit v5 on v4

v5 whole, which is shorter than its diff:
```python
import jax
import jax.numpy as jnp
import numpy as np
from jax import lax
from jax.experimental import pallas as pl
from jax.experimental.pallas import tpu as pltpu
from jax.sharding import Mesh, PartitionSpec as P

BF = jnp.bfloat16
F32 = jnp.float32
PLANE = ("x", "yh", "yl")
CHIPS = ("x", "yh", "yl", "core")
PAIR = ("yl", "core")
TURN = [(2, 0), (0, 1), (1, 3), (3, 2)]
BACK = [(b, a) for a, b in TURN]
OTHER = [(0, 1), (1, 0)]


def nn(a, b):
    return jnp.dot(a, b, preferred_element_type=F32)


def nt(a, b):
    return lax.dot_general(a, b, (((1,), (1,)), ((), ())), preferred_element_type=F32)


def tn(a, b):
    return lax.dot_general(a, b, (((0,), (0,)), ((), ())), preferred_element_type=F32)


def dot(spec, a, b):
    return jnp.einsum(spec, a, b, preferred_element_type=F32)


def rows_of(every):
    n, both, d = every.shape
    half = both // 2
    return every[:, :half].reshape(n * half, d), every[:, half:].reshape(n * half, d)


def reorder(slots):
    n_z = slots // 2
    row = lax.broadcasted_iota(jnp.int32, (slots, slots), 0)
    column = lax.broadcasted_iota(jnp.int32, (slots, slots), 1)
    last = (row >= n_z).astype(jnp.int32)
    return (column == 2 * (row - n_z * last) + last).astype(F32).astype(BF)


def expert_kernel(every, mine, other, terms, rows, hidden, g_pre, h_part, g_part, win, wout, made, sems):
    hid = mine.shape[0] // 2
    n, both, d = every.shape
    half = both // 2
    loads = [pltpu.make_async_copy(other.at[:hid], win, sems.at[0]), pltpu.make_async_copy(other.at[hid:], wout, sems.at[1])]
    for load in loads:
        load.start()
    saves = [pltpu.make_async_copy(every, rows, sems.at[2])]
    saves[0].start()
    x, g = rows_of(every[...])
    for i in range(2):
        if i == 0:
            a, b = mine[:hid], mine[hid:]
        else:
            for load in loads:
                load.wait()
            a, b = win[...], wout[...]
        pre = nt(x, a)
        cdf = 0.5 * (1.0 + lax.erf(pre * 0.7071067811865476))
        h_part[i] = (pre * cdf).astype(BF)
        slope = cdf + pre * jnp.exp(-0.5 * pre * pre) * 0.3989422804014327
        g_part[i] = (nt(g, b) * slope).astype(BF)
        saves.append(pltpu.make_async_copy(h_part.at[i], hidden.at[i], sems.at[3 + 2 * i]))
        saves.append(pltpu.make_async_copy(g_part.at[i], g_pre.at[i], sems.at[4 + 2 * i]))
        saves[-2].start()
        saves[-1].start()
    out = nn(h_part[0], mine[hid:]) + nn(h_part[1], wout[...])
    made[:, :half] = out.astype(BF).reshape(n, half, d)
    saves.append(pltpu.make_async_copy(made.at[:, :half], terms.at[:, :half], sems.at[7]))
    saves[-1].start()
    back = nn(g_part[0], mine[:hid]) + nn(g_part[1], win[...])
    made[:, half:] = back.astype(BF).reshape(n, half, d)
    saves.append(pltpu.make_async_copy(made.at[:, half:], terms.at[:, half:], sems.at[8]))
    saves[-1].start()
    for save in saves:
        save.wait()


def grads_kernel(every, hidden, g_pre, kept, given):
    hid = kept.shape[0] // 2
    x, g = rows_of(every[...])
    for i, grads in enumerate((kept, given)):
        grads[:hid] = tn(g_pre[i], x).astype(BF)
        grads[hid:] = tn(hidden[i], g).astype(BF)


def add_kernel(kept, given, grads_in, grads_out):
    hid = grads_in.shape[0]
    grads_in[...] = (kept[:hid].astype(F32) + given[:hid].astype(F32)).astype(BF)
    grads_out[...] = (kept[hid:].astype(F32) + given[hid:].astype(F32)).astype(BF)


def place_kernel(a, b, a_out, b_out):
    a_out[...] = a[...]
    b_out[...] = b[...]


def sum_kernel(terms, sums, made, sem):
    n, both, d = terms.shape
    n_z = both // 2
    for core in range(2):
        for kind in range(2):
            total = 0.0
            for chip in range(core, n, 2):
                total = total + terms[chip, kind * n_z : (kind + 1) * n_z].astype(F32)
            made[:, core * 2 + kind] = total.astype(BF)
    send = pltpu.make_async_copy(made, sums, sem)
    send.start()
    send.wait()


def tail_kernel(back, tok, cot, dispatch, combine, term, g_logits, g_slot):
    turn = reorder(2 * back.shape[0])
    slot_out = tn(turn, jnp.concatenate([back[:, 0], back[:, 2]], axis=0)).astype(BF)
    slot_grad = tn(turn, jnp.concatenate([back[:, 1], back[:, 3]], axis=0)).astype(BF)
    com, dis = combine[...], dispatch[...]
    g_comb = nt(slot_out, cot[...])
    g_clog = com * (g_comb - jnp.sum(com * g_comb, axis=0, keepdims=True))
    g_disp = nt(slot_grad, tok[...])
    g_dlog = dis * (g_disp - jnp.sum(dis * g_disp, axis=1, keepdims=True))
    g_log = (g_dlog + g_clog).astype(BF)
    g_logits[...] = g_log
    g_slot[...] = slot_grad
    term[:, 0] = nn(g_log, tok[...])


def tokens_kernel(dispatch, g_logits, g_slot, router, grads):
    made = tn(dispatch[...].astype(BF), g_slot[...]) + tn(g_logits[...], router[...])
    grads[...] = made.astype(BF)


def total_near_kernel(parts, out):
    out[...] = jnp.broadcast_to(jnp.sum(parts[...], axis=0, keepdims=True), out.shape)


def total_kernel(parts, out, made, sem):
    total = jnp.sum(parts[...], axis=0, keepdims=True)
    made[...] = jnp.broadcast_to(total, made.shape)
    send = pltpu.make_async_copy(made, out, sem)
    send.start()
    send.wait()


def call(kernel, outs, flops, *args, saved=(), scratch=(), far=(), vmem=8):
    moved = sum(a.size * a.dtype.itemsize for a in (*args, *outs, *saved))
    whole = pl.BlockSpec(memory_space=pltpu.VMEM)
    return pl.pallas_call(
        kernel,
        out_shape=[*outs, *(pltpu.HBM(a.shape, a.dtype) for a in saved)],
        in_specs=[pl.BlockSpec(memory_space=pltpu.HBM) if i in far else whole for i in range(len(args))],
        out_specs=[whole] * len(outs) + [pl.BlockSpec(memory_space=pltpu.HBM)] * len(saved),
        scratch_shapes=scratch,
        compiler_params=pltpu.CompilerParams(vmem_limit_bytes=vmem * 2**20),
        cost_estimate=pl.CostEstimate(flops=flops, bytes_accessed=moved, transcendentals=0),
    )(*args)


def like(shape, kind=BF):
    return jax.ShapeDtypeStruct(shape, kind)


def swap(x, axis):
    return lax.all_to_all(x, axis, split_axis=0, concat_axis=0, tiled=True)


def local(tokens, router, w_in, w_out, cotangent):
    n_z = lax.axis_size("z")
    n_plane = lax.axis_size(PLANE)
    n_chips = lax.axis_size(CHIPS)
    tok, cot = tokens[0], cotangent[0]
    n_tok, d = tok.shape
    slots = 2 * n_z
    hid = w_out.shape[1]
    dma = pltpu.SemaphoreType.DMA
    one = 2 * n_tok * slots * d

    logits = dot("td,ds->ts", tok, router)
    dispatch = jax.nn.softmax(logits, axis=0)
    combine = jax.nn.softmax(logits, axis=1)
    slot_in = dot("ts,td->sd", dispatch.astype(BF), tok).astype(BF)
    g_late = dot("ts,td->sd", combine.astype(BF), cot).astype(BF)

    rows = jnp.stack([slot_in.reshape(n_z, 2, d), g_late.reshape(n_z, 2, d)], axis=2).reshape(n_z, 4, d)
    mine = lax.ppermute(jnp.concatenate([w_in[0].T, w_out[0]], axis=0), PAIR, TURN)
    rows = swap(rows, "z")
    other = lax.ppermute(mine, "core", OTHER)
    rows = rows.reshape(n_z, 2, 2, d).transpose(1, 2, 0, 3).reshape(1, 2, 2 * n_z, d)
    both = like((n_plane, 2 * n_z, d))
    every = jnp.broadcast_to(rows, (n_plane // 2, 2, 2 * n_z, d)).reshape(both.shape)
    every = swap(every, PLANE)
    n_rows = n_plane * n_z
    unit = like((2, n_rows, hid))
    block = like((2 * hid, d))
    half = like((hid, d))
    work = 2 * n_rows * hid * d
    terms, rows, hidden, g_pre = call(
        expert_kernel,
        [],
        8 * work,
        every,
        mine,
        other,
        far=(2,),
        saved=[both, both, unit, unit],
        scratch=[pltpu.VMEM(a.shape, BF) for a in (unit, unit, half, half, both)] + [dma((9,))],
        vmem=16,
    )
    kept, given = call(grads_kernel, [block, block], 4 * work, rows, hidden, g_pre, vmem=12)
    given = lax.ppermute(given, "core", OTHER)

    terms = swap(terms, PLANE)
    (sums,) = call(
        sum_kernel,
        [],
        400 * one,
        terms,
        saved=[like((n_z, 4, d))],
        scratch=[pltpu.VMEM((n_z, 4, d), BF), dma],
    )
    home_in, home_out = call(add_kernel, [half, half], block.size, kept, given)
    home_in = lax.ppermute(home_in, PAIR, BACK)
    back = swap(sums, "z")
    term, g_logits, g_slot = call(
        tail_kernel,
        [like((slots, 1, d), F32), like((slots, n_tok)), like((slots, d))],
        400 * one,
        back,
        tok,
        cot,
        dispatch.T,
        combine.T,
    )

    term = swap(term, CHIPS)
    row, home_in, home_out = lax.optimization_barrier((term, home_in, home_out))
    home_out = lax.ppermute(home_out, PAIR, BACK)
    (row,) = call(total_near_kernel, [like((n_z, 1, d), F32)], row.size, row)
    (row,) = call(
        total_kernel,
        [],
        400 * one,
        swap(row, "z"),
        saved=[like((n_chips, 1, d), F32)],
        scratch=[pltpu.VMEM((n_chips, 1, d), F32), dma],
    )
    row, home_in, home_out = lax.optimization_barrier((row, home_in, home_out))
    grad_w_in, grad_w_out = call(place_kernel, [half, half], block.size, home_in, home_out)
    grad_router = swap(row, CHIPS).reshape(n_chips, d).T
    (grad_tokens,) = call(tokens_kernel, [like((n_tok, d))], 2 * one, dispatch.T, g_logits, g_slot, router.T)
    return (grad_tokens[None], grad_router, grad_w_in.T[None], grad_w_out[None])


def solution(mesh):
    fine = Mesh(np.asarray(mesh.devices).reshape(4, 2, 2, 16, 2), ("x", "yh", "yl", "z", "core"))
    images = P(("x", "yh", "yl", "z", "core"), None, None)
    first = P(("z", "core"), None, ("x", "yh", "yl"))
    second = P(("z", "core"), ("x", "yh", "yl"), None)
    return jax.shard_map(
        local,
        mesh=fine,
        in_specs=(images, P(), first, second, images),
        out_specs=(images, P(), first, second),
        check_vma=False,
    )
```

time: 168 us -> 162 us (0.964)
  starting transfers between devices: 52.9 us -> 71 us
  waiting for transfers between devices: 34.4 us -> 24.5 us
  matrix products: 8.68 us -> 0.83 us
  blocking collectives: 45.5 us -> 38.6 us
  local copies, waits for them, and re-layouts: 12 us -> 6.43 us
  Pallas kernels: 11.2 us -> 16 us
    all_to_all x5, starting transfers between devices: 29.3 us -> 42.3 us  [swap(): return lax.all_to_all(x, axis, split_axis=0, concat_axis=0, tiled=True)]
    all_to_all x5, waiting for transfers between devices: 34.4 us -> 22.5 us  [swap(): return lax.all_to_all(x, axis, split_axis=0, concat_axis=0, tiled=True)]
    dot_general x8 -> x3, matrix products: 8.68 us -> 0.83 us  [dot(): return jnp.einsum(spec, a, b, preferred_element_type=F32)]
    all_to_all x2, blocking collectives: 45.5 us -> 38.6 us  [swap(): return lax.all_to_all(x, axis, split_axis=0, concat_axis=0, tiled=True)]
    pallas_call x5 -> x9, Pallas kernels: 11.2 us -> 16 us  [call(): pl.pallas_call(kernel, out_shape=[*outs, *(pltpu.HBM(a.shape, a.dtype) fo...]
    broadcast_in_dim x4 -> x1, local copies, waits for them, and re-layouts: 2.63 us -> 0.12 us  [local(): jnp.broadcast_to(rows, (n_plane // 2, 2, 2 * n_z, d)).reshape(both.shape)]
    ppermute x1, starting transfers between devices: 4.18 us -> 6.53 us  [local(): given = lax.ppermute(given, 'core', OTHER)]
    ppermute x3 -> x2, starting transfers between devices: 11.3 us -> 13.6 us  [the longest x1 9.6 us: local(): other = lax.ppermute(mine, 'core', OTHER)]
  transfers between devices with their start and end apart: 11 -> 10, of which waited for: 5 -> 7; matrix products, arithmetic and copies ran while one was open for 6% -> 1% of each run, Pallas kernels for 4% -> 6%
where the time goes in v5:
time: 162 us; the launch traced here: 161 us
  starting transfers between devices  71 us (44%)
  blocking collectives  38.6 us (24%)
  waiting for transfers between devices  24.5 us (15%)
  Pallas kernels  16 us (10%)
  local copies, waits for them, and re-layouts  6.43 us (4%)
  other arithmetic  3.08 us (2%)
    all_to_all x5, starting transfers between devices, swap(): return lax.all_to_all(x, axis, split_axis=0, concat_axis=0, tiled=True)  42.3 us
    all_to_all x2, blocking collectives, swap(): return lax.all_to_all(x, axis, split_axis=0, concat_axis=0, tiled=True)  38.6 us
    all_to_all x5, waiting for transfers between devices, swap(): return lax.all_to_all(x, axis, split_axis=0, concat_axis=0, tiled=True)  22.5 us
    pallas_call x9, Pallas kernels, call(): pl.pallas_call(kernel, out_shape=[*outs, *(pltpu.HBM(a.shape, a.dtype) fo...  16 us
    ppermute x1, starting transfers between devices, local(): other = lax.ppermute(mine, 'core', OTHER)  9.6 us
    ppermute x1, starting transfers between devices, local(): given = lax.ppermute(given, 'core', OTHER)  6.53 us
    ppermute x1, starting transfers between devices, local(): home_in = lax.ppermute(home_in, PAIR, BACK)  5.79 us
    unnamed x25, local copies, waits for them, and re-layouts  5.41 us
  transfers between devices with their start and end apart: 10, of which 7 were waited for; matrix products, arithmetic and copies ran while one was open for 1% of the time, Pallas kernels for 6%

profile of v5, /device:TPU:1, one launch (start us, length us, event | category | flops | bytes accessed | tf_op | source)
XLA Modules:
  0.0 161.4 jit_solution(6890545036676718282)
XLA Ops:
  0.7 0.0 copy-start.1
  0.7 2.8 %pad_maximum_fusion = bf16[640,1280]{1,0:T(8,128)(2,1)} fusion(bf16[320,1280]{1,0:T(8,128)(2,1)} %bitcast.41, bf16[320,1280]{1,0:T(8,128)(2,1)} %bitcast.42), kind=kLoop, calls=%fused_computation.2 | loop fusion | flops 3276800 | bytes 3276800 | tf_op jit(solution)/shard_map/concatenate | solution.py:192
  3.4 4.0 %collective-permute-start = (bf16[640,1280]{1,0:T(8,128)(2,1)}, bf16[640,1280]{1,0:T(8,128)(2,1)S(1)}, u32[]{:S(2)}, u32[]{:S(2)}) collective-permute-start(bf16[640,1280]{1,0:T(8,128)(2,1)} %pad_maximum_fusion), channel_id=1, source_target_pairs={{32,0},{0,1},{1,33},{33,32},{34,2},{2,3},{3,35},{35,34},{36,4},{4,... | collective-permute-start | bytes 4915208 | tf_op jit(solution)/shard_map/ppermute | solution.py:192
  7.5 0.4 fusion.14
  7.9 0.2 fusion.3
  8.1 0.5 copy-done.10
  8.6 0.2 convolution_convert_fusion.1
  8.9 0.1 stack_reshape.6
  8.9 0.2 convolution_convert_fusion
  9.2 0.8 copy.16
  10.0 14.9 %all-to-all-start = ((bf16[16,4,1280]{2,1,0:T(4,128)(2,1)}), bf16[16,4,1280]{2,1,0:T(4,128)(2,1)S(1)}, u32[]{:S(2)}, u32[]{:S(2)}) async-start(bf16[16,4,1280]{2,1,0:T(4,128)(2,1)} %copy.16), calls=%async_computation | async-start | bytes 327680 | tf_op jit(solution)/shard_map/all_to_all | solution.py:171
  24.9 0.9 collective-permute-done.mine
  25.8 9.6 %collective-permute-start.1 = (bf16[640,1280]{1,0:T(8,128)(2,1)S(1)}, bf16[640,1280]{1,0:T(8,128)(2,1)}, u32[]{:S(2)}, u32[]{:S(2)}) collective-permute-start(bf16[640,1280]{1,0:T(8,128)(2,1)S(1)} %collective-permute-done.mine), channel_id=1, source_target_pairs={{0,1},{1,0},{2,3},{3,2},{4,5},{5,4},{6,7},{7,6},{8,9},{9,8},{10,11... | collective-permute-start | bytes 4915208 | tf_op jit(solution)/shard_map/ppermute | solution.py:194
  35.4 2.9 %all-to-all-done = bf16[16,4,1280]{2,1,0:T(4,128)(2,1)S(1)} async-done(((bf16[16,4,1280]{2,1,0:T(4,128)(2,1)}), bf16[16,4,1280]{2,1,0:T(4,128)(2,1)S(1)}, u32[]{:S(2)}, u32[]{:S(2)}) %all-to-all-start) | async-done | bytes 163872 | tf_op jit(solution)/shard_map/all_to_all | solution.py:171
  38.3 0.1 broadcast_in_dim.21
  38.5 21.8 %all_to_all.35.every = bf16[16,32,1280]{2,1,0:T(8,128)(2,1)S(1)} all-to-all(bf16[16,32,1280]{2,1,0:T(8,128)(2,1)S(1)} %bitcast.40), channel_id=1, replica_groups=mesh['x'=4,'yh'=2,'yl'=2,'z'=16,'core'=2] {'x','yh','yl'}, dimensions={0} | all-to-all | bytes 2621440 | tf_op jit(solution)/shard_map/all_to_all | solution.py:171
  60.3 0.0 collective-permute-done.1.other
  60.3 5.3 %shard_map.84 = (bf16[16,32,1280]{2,1,0:T(8,128)(2,1)}, bf16[16,32,1280]{2,1,0:T(8,128)(2,1)}, bf16[2,256,320]{2,1,0:T(8,128)(2,1)}, bf16[2,256,320]{2,1,0:T(8,128)(2,1)}) custom-call(bf16[16,32,1280]{2,1,0:T(8,128)(2,1)S(1)} %all_to_all.35.every, bf16[640,1280]{1,0:T(8,128)(2,1)S(1)} %collective-permute-done.mine, ...), custom_call_target="tpu_custom_call" | custom-call | flops 1677721600 | bytes 7864320 | tf_op jit(solution)/shard_map/pallas_call | solution.py:155
  65.6 3.7 %all-to-all-start.2 = ((bf16[16,32,1280]{2,1,0:T(8,128)(2,1)}), bf16[16,32,1280]{2,1,0:T(8,128)(2,1)S(1)}, u32[]{:S(2)}, u32[]{:S(2)}) async-start(bf16[16,32,1280]{2,1,0:T(8,128)(2,1)} %get-tuple-element.23), calls=%async_computation.2 | async-start | bytes 2621440 | tf_op jit(solution)/shard_map/all_to_all | solution.py:171
  69.3 1.3 copy-done.5
  70.6 1.0 copy-done.6
  71.6 1.0 copy-done.7
  72.6 2.2 %shard_map.88 = (bf16[640,1280]{1,0:T(8,128)(2,1)S(1)}, bf16[640,1280]{1,0:T(8,128)(2,1)}) custom-call(bf16[16,32,1280]{2,1,0:T(8,128)(2,1)S(1)} %copy-done.5, bf16[2,256,320]{2,1,0:T(8,128)(2,1)S(1)} %copy-done.6, bf16[2,256,320]{2,1,0:T(8,128)(2,1)S(1)} %copy-done.7), custom_call_target="tpu_custom_call" | custom-call | flops 838860800 | bytes 5242880 | tf_op jit(solution)/shard_map/pallas_call | solution.py:155
  74.9 6.5 %collective-permute-start.2 = (bf16[640,1280]{1,0:T(8,128)(2,1)}, bf16[640,1280]{1,0:T(8,128)(2,1)}, u32[]{:S(2)}, u32[]{:S(2)}) collective-permute-start(bf16[640,1280]{1,0:T(8,128)(2,1)} %get-tuple-element.31), channel_id=1, source_target_pairs={{0,1},{1,0},{2,3},{3,2},{4,5},{5,4},{6,7},{7,6},{8,9},{9,8},{10,11... | collective-permute-start | bytes 4915208 | tf_op jit(solution)/shard_map/ppermute | solution.py:217
  81.4 2.3 %all-to-all-done.2.terms = bf16[16,32,1280]{2,1,0:T(8,128)(2,1)S(1)} async-done(((bf16[16,32,1280]{2,1,0:T(8,128)(2,1)}), bf16[16,32,1280]{2,1,0:T(8,128)(2,1)S(1)}, u32[]{:S(2)}, u32[]{:S(2)}) %all-to-all-start.2) | async-done | bytes 1310752 | tf_op jit(solution)/shard_map/all_to_all | solution.py:171
  83.7 1.0 shard_map.85
  84.7 13.9 %all-to-all-start.3 = ((bf16[16,4,1280]{2,1,0:T(4,128)(2,1)}), bf16[16,4,1280]{2,1,0:T(4,128)(2,1)S(1)}, u32[]{:S(2)}, u32[]{:S(2)}) async-start(bf16[16,4,1280]{2,1,0:T(4,128)(2,1)} %shard_map.85), calls=%async_computation.3 | async-start | bytes 327680 | tf_op jit(solution)/shard_map/all_to_all | solution.py:171
  98.6 0.0 collective-permute-done.2.given
  98.7 0.0 copy-start.2
  98.7 2.6 %shard_map.89 = (bf16[320,1280]{1,0:T(8,128)(2,1)}, bf16[320,1280]{1,0:T(8,128)(2,1)S(1)}) custom-call(bf16[640,1280]{1,0:T(8,128)(2,1)S(1)} %get-tuple-element.30.kept, bf16[640,1280]{1,0:T(8,128)(2,1)} %collective-permute-done.2.given), custom_call_target="tpu_custom_call" | custom-call | flops 819200 | bytes 4915200 | tf_op jit(solution)/shard_map/pallas_call | solution.py:155
  101.3 0.9 copy-done.4
  102.1 5.8 %collective-permute-start.3 = (bf16[320,1280]{1,0:T(8,128)(2,1)}, bf16[320,1280]{1,0:T(8,128)(2,1)S(1)}, u32[]{:S(2)}, u32[]{:S(2)}) collective-permute-start(bf16[320,1280]{1,0:T(8,128)(2,1)} %get-tuple-element.32), channel_id=1, source_target_pairs={{0,32},{1,0},{33,1},{32,33},{2,34},{3,2},{35,3},{34,35},{4,36},{5,... | collective-permute-start | bytes 2457608 | tf_op jit(solution)/shard_map/ppermute | solution.py:229
  108.0 0.1 fusion.6
  108.1 2.8 %all-to-all-done.3.back = bf16[16,4,1280]{2,1,0:T(4,128)(2,1)S(1)} async-done(((bf16[16,4,1280]{2,1,0:T(4,128)(2,1)}), bf16[16,4,1280]{2,1,0:T(4,128)(2,1)S(1)}, u32[]{:S(2)}, u32[]{:S(2)}) %all-to-all-start.3) | async-done | bytes 163872 | tf_op jit(solution)/shard_map/all_to_all | solution.py:171
  110.8 1.0 shard_map.86
  111.8 16.8 %all_to_all.36.parts = f32[32,1,1280]{2,1,0:T(1,128)S(1)} all-to-all(f32[32,1,1280]{2,1,0:T(1,128)S(1)} %get-tuple-element.26), channel_id=1, replica_groups=mesh['x'=4,'yh'=2,'yl'=2,'z'=16,'core'=2] {'x','yh','yl','core'}, dimensions={0} | all-to-all | bytes 327680 | tf_op jit(solution)/shard_map/all_to_all | solution.py:171
  128.6 0.0 collective-permute-done.3.a
  128.6 0.7 shard_map.90
  129.4 4.1 %all-to-all-start.5 = ((f32[16,1,1280]{2,1,0:T(1,128)}), f32[16,1,1280]{2,1,0:T(1,128)S(1)}, u32[]{:S(2)}, u32[]{:S(2)}) async-start(f32[16,1,1280]{2,1,0:T(1,128)} %shard_map.90), calls=%async_computation.5 | async-start | bytes 163840 | tf_op jit(solution)/shard_map/all_to_all | solution.py:171
  133.5 2.7 %collective-permute-start.4 = (bf16[320,1280]{1,0:T(8,128)(2,1)}, bf16[320,1280]{1,0:T(8,128)(2,1)S(1)}, u32[]{:S(2)}, u32[]{:S(2)}) collective-permute-start(bf16[320,1280]{1,0:T(8,128)(2,1)} %copy-done.4), channel_id=1, source_target_pairs={{0,32},{1,0},{33,1},{32,33},{2,34},{3,2},{35,3},{34,35},{4,36},{5,... | collective-permute-start | bytes 2457608 | tf_op jit(solution)/shard_map/ppermute | solution.py:244
  136.2 9.1 %all-to-all-done.5.parts = f32[16,1,1280]{2,1,0:T(1,128)S(1)} async-done(((f32[16,1,1280]{2,1,0:T(1,128)}), f32[16,1,1280]{2,1,0:T(1,128)S(1)}, u32[]{:S(2)}, u32[]{:S(2)}) %all-to-all-start.5) | async-done | bytes 81952 | tf_op jit(solution)/shard_map/all_to_all | solution.py:171
  145.3 0.7 shard_map.91
  146.0 1.0 collective-permute-done.4.b
  147.1 5.6 %all-to-all-start.6 = ((f32[32,1,1280]{2,1,0:T(1,128)}), f32[32,1,1280]{2,1,0:T(1,128)S(1)}, u32[]{:S(2)}, u32[]{:S(2)}) async-start(f32[32,1,1280]{2,1,0:T(1,128)} %shard_map.91), calls=%async_computation.6 | async-start | bytes 327680 | tf_op jit(solution)/shard_map/all_to_all | solution.py:171
  152.7 1.2 shard_map.87
  153.9 1.3 shard_map.92
  155.2 5.5 %all-to-all-done.6 = f32[32,1,1280]{2,1,0:T(1,128)S(1)} async-done(((f32[32,1,1280]{2,1,0:T(1,128)}), f32[32,1,1280]{2,1,0:T(1,128)S(1)}, u32[]{:S(2)}, u32[]{:S(2)}) %all-to-all-start.6) | async-done | bytes 163872 | tf_op jit(solution)/shard_map/all_to_all | solution.py:171
  160.7 0.7 copy.20
  (22 shorter events, 0.1 us)
Async XLA Ops:
  0.6 6.8 %copy-start = (bf16[1,196,1280]{2,1,0:T(8,128)(2,1)S(1)}, bf16[1,196,1280]{2,1,0:T(8,128)(2,1)}, u32[]{:S(2)}) copy-start(bf16[1,196,1280]{2,1,0:T(8,128)(2,1)} %param.5) | copy-start | bytes 1505284
  0.6 6.8 %copy-start.3 = (bf16[1280,32]{0,1:T(8,128)(2,1)S(1)}, bf16[1280,32]{0,1:T(8,128)(2,1)}, u32[]{:S(2)}) copy-start(bf16[1280,32]{0,1:T(8,128)(2,1)} %param.6) | copy-start | bytes 245764
  0.7 8.3 %copy-start.1 = (bf16[1,196,1280]{2,1,0:T(8,128)(2,1)S(1)}, bf16[1,196,1280]{2,1,0:T(8,128)(2,1)}, u32[]{:S(2)}) copy-start(bf16[1,196,1280]{2,1,0:T(8,128)(2,1)} %param.9) | copy-start | bytes 1505284
  3.4 22.4 %collective-permute-start = (bf16[640,1280]{1,0:T(8,128)(2,1)}, bf16[640,1280]{1,0:T(8,128)(2,1)S(1)}, u32[]{:S(2)}, u32[]{:S(2)}) collective-permute-start(bf16[640,1280]{1,0:T(8,128)(2,1)} %pad_maximum_fusion), channel_id=1, source_target_pairs={{32,0},{0,1},{1,33},{33,32},{34,2},{2,3},{3,35},{35,34},{36,4},{4,... | collective-permute-start | bytes 4915208 | tf_op jit(solution)/shard_map/ppermute | solution.py:192
  7.9 30.6 %copy-start.8 = (f32[196,32]{0,1:T(8,128)}, f32[196,32]{0,1:T(8,128)S(1)}, u32[]{:S(2)}) copy-start(f32[196,32]{0,1:T(8,128)S(1)} %get-tuple-element.48) | copy-start | bytes 75268
  8.1 0.5 copy-start.10
  10.0 28.3 %all-to-all-start = ((bf16[16,4,1280]{2,1,0:T(4,128)(2,1)}), bf16[16,4,1280]{2,1,0:T(4,128)(2,1)S(1)}, u32[]{:S(2)}, u32[]{:S(2)}) async-start(bf16[16,4,1280]{2,1,0:T(4,128)(2,1)} %copy.16), calls=%async_computation | async-start | bytes 327680 | tf_op jit(solution)/shard_map/all_to_all | solution.py:171
  25.8 34.5 %collective-permute-start.1 = (bf16[640,1280]{1,0:T(8,128)(2,1)S(1)}, bf16[640,1280]{1,0:T(8,128)(2,1)}, u32[]{:S(2)}, u32[]{:S(2)}) collective-permute-start(bf16[640,1280]{1,0:T(8,128)(2,1)S(1)} %collective-permute-done.mine), channel_id=1, source_target_pairs={{0,1},{1,0},{2,3},{3,2},{4,5},{5,4},{6,7},{7,6},{8,9},{9,8},{10,11... | collective-permute-start | bytes 4915208 | tf_op jit(solution)/shard_map/ppermute | solution.py:194
  65.6 18.1 %all-to-all-start.2 = ((bf16[16,32,1280]{2,1,0:T(8,128)(2,1)}), bf16[16,32,1280]{2,1,0:T(8,128)(2,1)S(1)}, u32[]{:S(2)}, u32[]{:S(2)}) async-start(bf16[16,32,1280]{2,1,0:T(8,128)(2,1)} %get-tuple-element.23), calls=%async_computation.2 | async-start | bytes 2621440 | tf_op jit(solution)/shard_map/all_to_all | solution.py:171
  69.3 1.3 copy-start.5
  70.6 1.0 copy-start.6
  71.6 1.0 copy-start.7
  74.9 23.8 %collective-permute-start.2 = (bf16[640,1280]{1,0:T(8,128)(2,1)}, bf16[640,1280]{1,0:T(8,128)(2,1)}, u32[]{:S(2)}, u32[]{:S(2)}) collective-permute-start(bf16[640,1280]{1,0:T(8,128)(2,1)} %get-tuple-element.31), channel_id=1, source_target_pairs={{0,1},{1,0},{2,3},{3,2},{4,5},{5,4},{6,7},{7,6},{8,9},{9,8},{10,11... | collective-permute-start | bytes 4915208 | tf_op jit(solution)/shard_map/ppermute | solution.py:217
  84.7 26.1 %all-to-all-start.3 = ((bf16[16,4,1280]{2,1,0:T(4,128)(2,1)}), bf16[16,4,1280]{2,1,0:T(4,128)(2,1)S(1)}, u32[]{:S(2)}, u32[]{:S(2)}) async-start(bf16[16,4,1280]{2,1,0:T(4,128)(2,1)} %shard_map.85), calls=%async_computation.3 | async-start | bytes 327680 | tf_op jit(solution)/shard_map/all_to_all | solution.py:171
  98.7 9.3 %copy-start.9 = (f32[196,32]{0,1:T(8,128)S(1)}, f32[196,32]{0,1:T(8,128)}, u32[]{:S(2)}) copy-start(f32[196,32]{0,1:T(8,128)} %copy-done.8) | copy-start | bytes 75268
  98.7 9.3 %copy-start.11 = (f32[32]{0:T(128)S(1)}, f32[32]{0:T(128)}, u32[]{:S(2)}) copy-start(f32[32]{0:T(128)} %copy-done.10) | copy-start | bytes 388
  98.7 12.1 %copy-start.2 = (bf16[1,196,1280]{2,1,0:T(8,128)(2,1)S(1)}, bf16[1,196,1280]{2,1,0:T(8,128)(2,1)}, u32[]{:S(2)}) copy-start(bf16[1,196,1280]{2,1,0:T(8,128)(2,1)} %param.9) | copy-start | bytes 1505284
  101.3 0.9 copy-start.4
  102.1 26.5 %collective-permute-start.3 = (bf16[320,1280]{1,0:T(8,128)(2,1)}, bf16[320,1280]{1,0:T(8,128)(2,1)S(1)}, u32[]{:S(2)}, u32[]{:S(2)}) collective-permute-start(bf16[320,1280]{1,0:T(8,128)(2,1)} %get-tuple-element.32), channel_id=1, source_target_pairs={{0,32},{1,0},{33,1},{32,33},{2,34},{3,2},{35,3},{34,35},{4,36},{5,... | collective-permute-start | bytes 2457608 | tf_op jit(solution)/shard_map/ppermute | solution.py:229
  129.4 15.9 %all-to-all-start.5 = ((f32[16,1,1280]{2,1,0:T(1,128)}), f32[16,1,1280]{2,1,0:T(1,128)S(1)}, u32[]{:S(2)}, u32[]{:S(2)}) async-start(f32[16,1,1280]{2,1,0:T(1,128)} %shard_map.90), calls=%async_computation.5 | async-start | bytes 163840 | tf_op jit(solution)/shard_map/all_to_all | solution.py:171
  133.5 13.6 %collective-permute-start.4 = (bf16[320,1280]{1,0:T(8,128)(2,1)}, bf16[320,1280]{1,0:T(8,128)(2,1)S(1)}, u32[]{:S(2)}, u32[]{:S(2)}) collective-permute-start(bf16[320,1280]{1,0:T(8,128)(2,1)} %copy-done.4), channel_id=1, source_target_pairs={{0,32},{1,0},{33,1},{32,33},{2,34},{3,2},{35,3},{34,35},{4,36},{5,... | collective-permute-start | bytes 2457608 | tf_op jit(solution)/shard_map/ppermute | solution.py:244
  147.1 13.6 %all-to-all-start.6 = ((f32[32,1,1280]{2,1,0:T(1,128)}), f32[32,1,1280]{2,1,0:T(1,128)S(1)}, u32[]{:S(2)}, u32[]{:S(2)}) async-start(f32[32,1,1280]{2,1,0:T(1,128)} %shard_map.91), calls=%async_computation.6 | async-start | bytes 327680 | tf_op jit(solution)/shard_map/all_to_all | solution.py:171

commit v6 on v5

--- a/solution.py
+++ b/solution.py
@@ -53,8 +53,7 @@
     loads = [pltpu.make_async_copy(other.at[:hid], win, sems.at[0]), pltpu.make_async_copy(other.at[hid:], wout, sems.at[1])]
     for load in loads:
         load.start()
-    saves = [pltpu.make_async_copy(every, rows, sems.at[2])]
-    saves[0].start()
+    saves = []
     x, g = rows_of(every[...])
     for i in range(2):
         if i == 0:
@@ -62,6 +61,8 @@
         else:
             for load in loads:
                 load.wait()
+            saves.append(pltpu.make_async_copy(every, rows, sems.at[2]))
+            saves[-1].start()
             a, b = win[...], wout[...]
         pre = nt(x, a)
         cdf = 0.5 * (1.0 + lax.erf(pre * 0.7071067811865476))
@@ -129,7 +130,10 @@
     g_log = (g_dlog + g_clog).astype(BF)
     g_logits[...] = g_log
     g_slot[...] = slot_grad
-    term[:, 0] = nn(g_log, tok[...])
+    made = nn(g_log, tok[...]).astype(BF)
+    wide = term.shape[2]
+    for i in range(2):
+        term[:, i] = made[:, i * wide : (i + 1) * wide]
 
 
 def tokens_kernel(dispatch, g_logits, g_slot, router, grads):
@@ -137,16 +141,18 @@
     grads[...] = made.astype(BF)
 
 
-def total_near_kernel(parts, out):
-    out[...] = jnp.broadcast_to(jnp.sum(parts[...], axis=0, keepdims=True), out.shape)
-
-
 def total_kernel(parts, out, made, sem):
-    total = jnp.sum(parts[...], axis=0, keepdims=True)
-    made[...] = jnp.broadcast_to(total, made.shape)
+    total = jnp.sum(parts[...].astype(F32), axis=0, keepdims=True)
+    made[...] = jnp.broadcast_to(total, made.shape).astype(BF)
     send = pltpu.make_async_copy(made, out, sem)
     send.start()
     send.wait()
+
+
+def router_kernel(parts, grads):
+    wide = parts.shape[2]
+    for i in range(2):
+        grads[:, i * wide : (i + 1) * wide] = parts[:, i].astype(F32)
 
 
 def call(kernel, outs, flops, *args, saved=(), scratch=(), far=(), vmem=8):
@@ -230,7 +236,7 @@
     back = swap(sums, "z")
     term, g_logits, g_slot = call(
         tail_kernel,
-        [like((slots, 1, d), F32), like((slots, n_tok)), like((slots, d))],
+        [like((slots, 2, d // 2)), like((slots, n_tok)), like((slots, d))],
         400 * one,
         back,
         tok,
@@ -242,20 +248,16 @@
     term = swap(term, CHIPS)
     row, home_in, home_out = lax.optimization_barrier((term, home_in, home_out))
     home_out = lax.ppermute(home_out, PAIR, BACK)
-    (row,) = call(total_near_kernel, [like((n_z, 1, d), F32)], row.size, row)
+    few, many = like((n_z, 2, d // 2)), like((n_chips, 2, d // 2))
+    (row,) = call(total_kernel, [], row.size, row, saved=[few], scratch=[pltpu.VMEM(few.shape, BF), dma])
     (row,) = call(
-        total_kernel,
-        [],
-        400 * one,
-        swap(row, "z"),
-        saved=[like((n_chips, 1, d), F32)],
-        scratch=[pltpu.VMEM((n_chips, 1, d), F32), dma],
+        total_kernel, [], 1200 * one, swap(row, "z"), saved=[many], scratch=[pltpu.VMEM(many.shape, BF), dma]
     )
     row, home_in, home_out = lax.optimization_barrier((row, home_in, home_out))
     grad_w_in, grad_w_out = call(place_kernel, [half, half], block.size, home_in, home_out)
-    grad_router = swap(row, CHIPS).reshape(n_chips, d).T
+    (grad_router,) = call(router_kernel, [like((slots, d), F32)], row.size, swap(row, CHIPS))
     (grad_tokens,) = call(tokens_kernel, [like((n_tok, d))], 2 * one, dispatch.T, g_logits, g_slot, router.T)
-    return (grad_tokens[None], grad_router, grad_w_in.T[None], grad_w_out[None])
+    return (grad_tokens[None], grad_router.T, grad_w_in.T[None], grad_w_out[None])
 
 
 def solution(mesh):

time: 162 us -> 160 us (0.988)
    unnamed x25 -> x24, local copies, waits for them, and re-layouts: 5.41 us -> 4.73 us
    pallas_call x9 -> x10, Pallas kernels: 16 us -> 16.1 us  [call(): pl.pallas_call(kernel, out_shape=[*outs, *(pltpu.HBM(a.shape, a.dtype) fo...]
where the time goes in v6:
time: 160 us; the launch traced here: 159 us
  starting transfers between devices  70.4 us (44%)
  blocking collectives  38 us (24%)
  waiting for transfers between devices  23.8 us (15%)
  Pallas kernels  16.1 us (10%)
  local copies, waits for them, and re-layouts  5.75 us (4%)
  other arithmetic  3.08 us (2%)
    all_to_all x5, starting transfers between devices, swap(): return lax.all_to_all(x, axis, split_axis=0, concat_axis=0, tiled=True)  41.9 us
    all_to_all x2, blocking collectives, swap(): return lax.all_to_all(x, axis, split_axis=0, concat_axis=0, tiled=True)  38 us
    all_to_all x5, waiting for transfers between devices, swap(): return lax.all_to_all(x, axis, split_axis=0, concat_axis=0, tiled=True)  21.8 us
    pallas_call x10, Pallas kernels, call(): pl.pallas_call(kernel, out_shape=[*outs, *(pltpu.HBM(a.shape, a.dtype) fo...  16.1 us
    ppermute x1, starting transfers between devices, local(): other = lax.ppermute(mine, 'core', OTHER)  9.6 us
    ppermute x1, starting transfers between devices, local(): given = lax.ppermute(given, 'core', OTHER)  6.53 us
    ppermute x1, starting transfers between devices, local(): home_in = lax.ppermute(home_in, PAIR, BACK)  5.79 us
    unnamed x24, local copies, waits for them, and re-layouts  4.73 us
  transfers between devices with their start and end apart: 10, of which 7 were waited for; matrix products, arithmetic and copies ran while one was open for 1% of the time, Pallas kernels for 6%

profile of v6, /device:TPU:1, one launch (start us, length us, event | category | flops | bytes accessed | tf_op | source)
XLA Modules:
  0.0 158.9 jit_solution(8682821382186181597)
XLA Ops:
  0.7 0.0 copy-start.1
  0.7 2.8 %pad_maximum_fusion = bf16[640,1280]{1,0:T(8,128)(2,1)} fusion(bf16[320,1280]{1,0:T(8,128)(2,1)} %bitcast.37, bf16[320,1280]{1,0:T(8,128)(2,1)} %bitcast.38), kind=kLoop, calls=%fused_computation.2 | loop fusion | flops 3276800 | bytes 3276800 | tf_op jit(solution)/shard_map/concatenate | solution.py:198
  3.4 4.0 %collective-permute-start = (bf16[640,1280]{1,0:T(8,128)(2,1)}, bf16[640,1280]{1,0:T(8,128)(2,1)S(1)}, u32[]{:S(2)}, u32[]{:S(2)}) collective-permute-start(bf16[640,1280]{1,0:T(8,128)(2,1)} %pad_maximum_fusion), channel_id=1, source_target_pairs={{32,0},{0,1},{1,33},{33,32},{34,2},{2,3},{3,35},{35,34},{36,4},{4,... | collective-permute-start | bytes 4915208 | tf_op jit(solution)/shard_map/ppermute | solution.py:198
  7.5 0.4 fusion.14
  7.9 0.2 fusion.3
  8.1 0.5 copy-done.10
  8.6 0.2 convolution_convert_fusion.1
  8.9 0.1 stack_reshape.6
  8.9 0.2 convolution_convert_fusion
  9.2 0.8 copy.16
  10.0 14.9 %all-to-all-start = ((bf16[16,4,1280]{2,1,0:T(4,128)(2,1)}), bf16[16,4,1280]{2,1,0:T(4,128)(2,1)S(1)}, u32[]{:S(2)}, u32[]{:S(2)}) async-start(bf16[16,4,1280]{2,1,0:T(4,128)(2,1)} %copy.16), calls=%async_computation | async-start | bytes 327680 | tf_op jit(solution)/shard_map/all_to_all | solution.py:177
  24.9 0.9 collective-permute-done.mine
  25.8 9.6 %collective-permute-start.1 = (bf16[640,1280]{1,0:T(8,128)(2,1)S(1)}, bf16[640,1280]{1,0:T(8,128)(2,1)}, u32[]{:S(2)}, u32[]{:S(2)}) collective-permute-start(bf16[640,1280]{1,0:T(8,128)(2,1)S(1)} %collective-permute-done.mine), channel_id=1, source_target_pairs={{0,1},{1,0},{2,3},{3,2},{4,5},{5,4},{6,7},{7,6},{8,9},{9,8},{10,11... | collective-permute-start | bytes 4915208 | tf_op jit(solution)/shard_map/ppermute | solution.py:200
  35.4 2.9 %all-to-all-done = bf16[16,4,1280]{2,1,0:T(4,128)(2,1)S(1)} async-done(((bf16[16,4,1280]{2,1,0:T(4,128)(2,1)}), bf16[16,4,1280]{2,1,0:T(4,128)(2,1)S(1)}, u32[]{:S(2)}, u32[]{:S(2)}) %all-to-all-start) | async-done | bytes 163872 | tf_op jit(solution)/shard_map/all_to_all | solution.py:177
  38.3 0.1 broadcast_in_dim.21
  38.5 21.8 %all_to_all.35.every = bf16[16,32,1280]{2,1,0:T(8,128)(2,1)S(1)} all-to-all(bf16[16,32,1280]{2,1,0:T(8,128)(2,1)S(1)} %bitcast.36), channel_id=1, replica_groups=mesh['x'=4,'yh'=2,'yl'=2,'z'=16,'core'=2] {'x','yh','yl'}, dimensions={0} | all-to-all | bytes 2621440 | tf_op jit(solution)/shard_map/all_to_all | solution.py:177
  60.3 0.0 collective-permute-done.1.other
  60.3 4.7 %shard_map.84 = (bf16[16,32,1280]{2,1,0:T(8,128)(2,1)}, bf16[16,32,1280]{2,1,0:T(8,128)(2,1)}, bf16[2,256,320]{2,1,0:T(8,128)(2,1)}, bf16[2,256,320]{2,1,0:T(8,128)(2,1)}) custom-call(bf16[16,32,1280]{2,1,0:T(8,128)(2,1)S(1)} %all_to_all.35.every, bf16[640,1280]{1,0:T(8,128)(2,1)S(1)} %collective-permute-done.mine, ...), custom_call_target="tpu_custom_call" | custom-call | flops 1677721600 | bytes 7864320 | tf_op jit(solution)/shard_map/pallas_call | solution.py:161
  65.0 3.7 %all-to-all-start.2 = ((bf16[16,32,1280]{2,1,0:T(8,128)(2,1)}), bf16[16,32,1280]{2,1,0:T(8,128)(2,1)S(1)}, u32[]{:S(2)}, u32[]{:S(2)}) async-start(bf16[16,32,1280]{2,1,0:T(8,128)(2,1)} %get-tuple-element.23), calls=%async_computation.2 | async-start | bytes 2621440 | tf_op jit(solution)/shard_map/all_to_all | solution.py:177
  68.7 1.3 copy-done.5
  70.0 1.0 copy-done.6
  71.0 1.0 copy-done.7
  72.0 2.2 %shard_map.88 = (bf16[640,1280]{1,0:T(8,128)(2,1)S(1)}, bf16[640,1280]{1,0:T(8,128)(2,1)}) custom-call(bf16[16,32,1280]{2,1,0:T(8,128)(2,1)S(1)} %copy-done.5, bf16[2,256,320]{2,1,0:T(8,128)(2,1)S(1)} %copy-done.6, bf16[2,256,320]{2,1,0:T(8,128)(2,1)S(1)} %copy-done.7), custom_call_target="tpu_custom_call" | custom-call | flops 838860800 | bytes 5242880 | tf_op jit(solution)/shard_map/pallas_call | solution.py:161
  74.3 6.5 %collective-permute-start.2 = (bf16[640,1280]{1,0:T(8,128)(2,1)}, bf16[640,1280]{1,0:T(8,128)(2,1)}, u32[]{:S(2)}, u32[]{:S(2)}) collective-permute-start(bf16[640,1280]{1,0:T(8,128)(2,1)} %get-tuple-element.31), channel_id=1, source_target_pairs={{0,1},{1,0},{2,3},{3,2},{4,5},{5,4},{6,7},{7,6},{8,9},{9,8},{10,11... | collective-permute-start | bytes 4915208 | tf_op jit(solution)/shard_map/ppermute | solution.py:223
  80.8 2.3 %all-to-all-done.2.terms = bf16[16,32,1280]{2,1,0:T(8,128)(2,1)S(1)} async-done(((bf16[16,32,1280]{2,1,0:T(8,128)(2,1)}), bf16[16,32,1280]{2,1,0:T(8,128)(2,1)S(1)}, u32[]{:S(2)}, u32[]{:S(2)}) %all-to-all-start.2) | async-done | bytes 1310752 | tf_op jit(solution)/shard_map/all_to_all | solution.py:177
  83.1 1.0 shard_map.85
  84.1 13.9 %all-to-all-start.3 = ((bf16[16,4,1280]{2,1,0:T(4,128)(2,1)}), bf16[16,4,1280]{2,1,0:T(4,128)(2,1)S(1)}, u32[]{:S(2)}, u32[]{:S(2)}) async-start(bf16[16,4,1280]{2,1,0:T(4,128)(2,1)} %shard_map.85), calls=%async_computation.3 | async-start | bytes 327680 | tf_op jit(solution)/shard_map/all_to_all | solution.py:177
  98.0 0.0 collective-permute-done.2.given
  98.1 0.0 copy-start.2
  98.1 2.6 %shard_map.89 = (bf16[320,1280]{1,0:T(8,128)(2,1)}, bf16[320,1280]{1,0:T(8,128)(2,1)S(1)}) custom-call(bf16[640,1280]{1,0:T(8,128)(2,1)S(1)} %get-tuple-element.30.kept, bf16[640,1280]{1,0:T(8,128)(2,1)} %collective-permute-done.2.given), custom_call_target="tpu_custom_call" | custom-call | flops 819200 | bytes 4915200 | tf_op jit(solution)/shard_map/pallas_call | solution.py:161
  100.6 0.9 copy-done.4
  101.5 5.8 %collective-permute-start.3 = (bf16[320,1280]{1,0:T(8,128)(2,1)}, bf16[320,1280]{1,0:T(8,128)(2,1)S(1)}, u32[]{:S(2)}, u32[]{:S(2)}) collective-permute-start(bf16[320,1280]{1,0:T(8,128)(2,1)} %get-tuple-element.32), channel_id=1, source_target_pairs={{0,32},{1,0},{33,1},{32,33},{2,34},{3,2},{35,3},{34,35},{4,36},{5,... | collective-permute-start | bytes 2457608 | tf_op jit(solution)/shard_map/ppermute | solution.py:235
  107.3 0.1 fusion.6
  107.4 2.8 %all-to-all-done.3.back = bf16[16,4,1280]{2,1,0:T(4,128)(2,1)S(1)} async-done(((bf16[16,4,1280]{2,1,0:T(4,128)(2,1)}), bf16[16,4,1280]{2,1,0:T(4,128)(2,1)S(1)}, u32[]{:S(2)}, u32[]{:S(2)}) %all-to-all-start.3) | async-done | bytes 163872 | tf_op jit(solution)/shard_map/all_to_all | solution.py:177
  110.2 1.0 shard_map.86
  111.2 16.2 %all_to_all.36.parts = bf16[32,2,640]{2,1,0:T(2,128)(2,1)S(1)} all-to-all(bf16[32,2,640]{2,1,0:T(2,128)(2,1)S(1)} %get-tuple-element.26), channel_id=1, replica_groups=mesh['x'=4,'yh'=2,'yl'=2,'z'=16,'core'=2] {'x','yh','yl','core'}, dimensions={0} | all-to-all | bytes 163840 | tf_op jit(solution)/shard_map/all_to_all | solution.py:177
  127.4 0.0 collective-permute-done.3.a
  127.4 0.7 shard_map.90
  128.1 4.1 %all-to-all-start.5 = ((bf16[16,2,640]{2,1,0:T(2,128)(2,1)}), bf16[16,2,640]{2,1,0:T(2,128)(2,1)S(1)}, u32[]{:S(2)}, u32[]{:S(2)}) async-start(bf16[16,2,640]{2,1,0:T(2,128)(2,1)} %shard_map.90), calls=%async_computation.5 | async-start | bytes 81920 | tf_op jit(solution)/shard_map/all_to_all | solution.py:177
  132.3 2.6 %collective-permute-start.4 = (bf16[320,1280]{1,0:T(8,128)(2,1)}, bf16[320,1280]{1,0:T(8,128)(2,1)S(1)}, u32[]{:S(2)}, u32[]{:S(2)}) collective-permute-start(bf16[320,1280]{1,0:T(8,128)(2,1)} %copy-done.4), channel_id=1, source_target_pairs={{0,32},{1,0},{33,1},{32,33},{2,34},{3,2},{35,3},{34,35},{4,36},{5,... | collective-permute-start | bytes 2457608 | tf_op jit(solution)/shard_map/ppermute | solution.py:250
  134.9 8.9 %all-to-all-done.5.parts = bf16[16,2,640]{2,1,0:T(2,128)(2,1)S(1)} async-done(((bf16[16,2,640]{2,1,0:T(2,128)(2,1)}), bf16[16,2,640]{2,1,0:T(2,128)(2,1)S(1)}, u32[]{:S(2)}, u32[]{:S(2)}) %all-to-all-start.5) | async-done | bytes 40992 | tf_op jit(solution)/shard_map/all_to_all | solution.py:177
  143.8 0.7 shard_map.91
  144.5 1.1 collective-permute-done.4.b
  145.6 5.2 %all-to-all-start.6 = ((bf16[32,2,640]{2,1,0:T(2,128)(2,1)}), bf16[32,2,640]{2,1,0:T(2,128)(2,1)S(1)}, u32[]{:S(2)}, u32[]{:S(2)}) async-start(bf16[32,2,640]{2,1,0:T(2,128)(2,1)} %shard_map.91), calls=%async_computation.6 | async-start | bytes 163840 | tf_op jit(solution)/shard_map/all_to_all | solution.py:177
  150.7 1.2 shard_map.87
  152.0 1.3 shard_map.93
  153.3 4.9 %all-to-all-done.6.parts = bf16[32,2,640]{2,1,0:T(2,128)(2,1)S(1)} async-done(((bf16[32,2,640]{2,1,0:T(2,128)(2,1)}), bf16[32,2,640]{2,1,0:T(2,128)(2,1)S(1)}, u32[]{:S(2)}, u32[]{:S(2)}) %all-to-all-start.6) | async-done | bytes 81952 | tf_op jit(solution)/shard_map/all_to_all | solution.py:177
  158.2 0.7 shard_map.92
  (22 shorter events, 0.1 us)
Async XLA Ops:
  0.6 6.8 %copy-start = (bf16[1,196,1280]{2,1,0:T(8,128)(2,1)S(1)}, bf16[1,196,1280]{2,1,0:T(8,128)(2,1)}, u32[]{:S(2)}) copy-start(bf16[1,196,1280]{2,1,0:T(8,128)(2,1)} %param.5) | copy-start | bytes 1505284
  0.6 6.8 %copy-start.3 = (bf16[1280,32]{0,1:T(8,128)(2,1)S(1)}, bf16[1280,32]{0,1:T(8,128)(2,1)}, u32[]{:S(2)}) copy-start(bf16[1280,32]{0,1:T(8,128)(2,1)} %param.6) | copy-start | bytes 245764
  0.7 8.3 %copy-start.1 = (bf16[1,196,1280]{2,1,0:T(8,128)(2,1)S(1)}, bf16[1,196,1280]{2,1,0:T(8,128)(2,1)}, u32[]{:S(2)}) copy-start(bf16[1,196,1280]{2,1,0:T(8,128)(2,1)} %param.9) | copy-start | bytes 1505284
  3.4 22.4 %collective-permute-start = (bf16[640,1280]{1,0:T(8,128)(2,1)}, bf16[640,1280]{1,0:T(8,128)(2,1)S(1)}, u32[]{:S(2)}, u32[]{:S(2)}) collective-permute-start(bf16[640,1280]{1,0:T(8,128)(2,1)} %pad_maximum_fusion), channel_id=1, source_target_pairs={{32,0},{0,1},{1,33},{33,32},{34,2},{2,3},{3,35},{35,34},{36,4},{4,... | collective-permute-start | bytes 4915208 | tf_op jit(solution)/shard_map/ppermute | solution.py:198
  7.9 30.6 %copy-start.8 = (f32[196,32]{0,1:T(8,128)}, f32[196,32]{0,1:T(8,128)S(1)}, u32[]{:S(2)}) copy-start(f32[196,32]{0,1:T(8,128)S(1)} %get-tuple-element.48) | copy-start | bytes 75268
  8.1 0.5 copy-start.10
  10.0 28.3 %all-to-all-start = ((bf16[16,4,1280]{2,1,0:T(4,128)(2,1)}), bf16[16,4,1280]{2,1,0:T(4,128)(2,1)S(1)}, u32[]{:S(2)}, u32[]{:S(2)}) async-start(bf16[16,4,1280]{2,1,0:T(4,128)(2,1)} %copy.16), calls=%async_computation | async-start | bytes 327680 | tf_op jit(solution)/shard_map/all_to_all | solution.py:177
  25.8 34.5 %collective-permute-start.1 = (bf16[640,1280]{1,0:T(8,128)(2,1)S(1)}, bf16[640,1280]{1,0:T(8,128)(2,1)}, u32[]{:S(2)}, u32[]{:S(2)}) collective-permute-start(bf16[640,1280]{1,0:T(8,128)(2,1)S(1)} %collective-permute-done.mine), channel_id=1, source_target_pairs={{0,1},{1,0},{2,3},{3,2},{4,5},{5,4},{6,7},{7,6},{8,9},{9,8},{10,11... | collective-permute-start | bytes 4915208 | tf_op jit(solution)/shard_map/ppermute | solution.py:200
  65.0 18.1 %all-to-all-start.2 = ((bf16[16,32,1280]{2,1,0:T(8,128)(2,1)}), bf16[16,32,1280]{2,1,0:T(8,128)(2,1)S(1)}, u32[]{:S(2)}, u32[]{:S(2)}) async-start(bf16[16,32,1280]{2,1,0:T(8,128)(2,1)} %get-tuple-element.23), calls=%async_computation.2 | async-start | bytes 2621440 | tf_op jit(solution)/shard_map/all_to_all | solution.py:177
  68.7 1.3 copy-start.5
  70.0 1.0 copy-start.6
  71.0 1.0 copy-start.7
  74.3 23.8 %collective-permute-start.2 = (bf16[640,1280]{1,0:T(8,128)(2,1)}, bf16[640,1280]{1,0:T(8,128)(2,1)}, u32[]{:S(2)}, u32[]{:S(2)}) collective-permute-start(bf16[640,1280]{1,0:T(8,128)(2,1)} %get-tuple-element.31), channel_id=1, source_target_pairs={{0,1},{1,0},{2,3},{3,2},{4,5},{5,4},{6,7},{7,6},{8,9},{9,8},{10,11... | collective-permute-start | bytes 4915208 | tf_op jit(solution)/shard_map/ppermute | solution.py:223
  84.1 26.1 %all-to-all-start.3 = ((bf16[16,4,1280]{2,1,0:T(4,128)(2,1)}), bf16[16,4,1280]{2,1,0:T(4,128)(2,1)S(1)}, u32[]{:S(2)}, u32[]{:S(2)}) async-start(bf16[16,4,1280]{2,1,0:T(4,128)(2,1)} %shard_map.85), calls=%async_computation.3 | async-start | bytes 327680 | tf_op jit(solution)/shard_map/all_to_all | solution.py:177
  98.0 9.3 %copy-start.9 = (f32[196,32]{0,1:T(8,128)S(1)}, f32[196,32]{0,1:T(8,128)}, u32[]{:S(2)}) copy-start(f32[196,32]{0,1:T(8,128)} %copy-done.8) | copy-start | bytes 75268
  98.1 9.3 %copy-start.11 = (f32[32]{0:T(128)S(1)}, f32[32]{0:T(128)}, u32[]{:S(2)}) copy-start(f32[32]{0:T(128)} %copy-done.10) | copy-start | bytes 388
  98.1 12.1 %copy-start.2 = (bf16[1,196,1280]{2,1,0:T(8,128)(2,1)S(1)}, bf16[1,196,1280]{2,1,0:T(8,128)(2,1)}, u32[]{:S(2)}) copy-start(bf16[1,196,1280]{2,1,0:T(8,128)(2,1)} %param.9) | copy-start | bytes 1505284
  100.6 0.9 copy-start.4
  101.5 25.9 %collective-permute-start.3 = (bf16[320,1280]{1,0:T(8,128)(2,1)}, bf16[320,1280]{1,0:T(8,128)(2,1)S(1)}, u32[]{:S(2)}, u32[]{:S(2)}) collective-permute-start(bf16[320,1280]{1,0:T(8,128)(2,1)} %get-tuple-element.32), channel_id=1, source_target_pairs={{0,32},{1,0},{33,1},{32,33},{2,34},{3,2},{35,3},{34,35},{4,36},{5,... | collective-permute-start | bytes 2457608 | tf_op jit(solution)/shard_map/ppermute | solution.py:235
  128.1 15.7 %all-to-all-start.5 = ((bf16[16,2,640]{2,1,0:T(2,128)(2,1)}), bf16[16,2,640]{2,1,0:T(2,128)(2,1)S(1)}, u32[]{:S(2)}, u32[]{:S(2)}) async-start(bf16[16,2,640]{2,1,0:T(2,128)(2,1)} %shard_map.90), calls=%async_computation.5 | async-start | bytes 81920 | tf_op jit(solution)/shard_map/all_to_all | solution.py:177
  132.3 13.3 %collective-permute-start.4 = (bf16[320,1280]{1,0:T(8,128)(2,1)}, bf16[320,1280]{1,0:T(8,128)(2,1)S(1)}, u32[]{:S(2)}, u32[]{:S(2)}) collective-permute-start(bf16[320,1280]{1,0:T(8,128)(2,1)} %copy-done.4), channel_id=1, source_target_pairs={{0,32},{1,0},{33,1},{32,33},{2,34},{3,2},{35,3},{34,35},{4,36},{5,... | collective-permute-start | bytes 2457608 | tf_op jit(solution)/shard_map/ppermute | solution.py:250
  145.6 12.6 %all-to-all-start.6 = ((bf16[32,2,640]{2,1,0:T(2,128)(2,1)}), bf16[32,2,640]{2,1,0:T(2,128)(2,1)S(1)}, u32[]{:S(2)}, u32[]{:S(2)}) async-start(bf16[32,2,640]{2,1,0:T(2,128)(2,1)} %shard_map.91), calls=%async_computation.6 | async-start | bytes 163840 | tf_op jit(solution)/shard_map/all_to_all | solution.py:177

commit v7 on v6

--- a/solution.py
+++ b/solution.py
@@ -9,7 +9,7 @@
 BF = jnp.bfloat16
 F32 = jnp.float32
 PLANE = ("x", "yh", "yl")
-CHIPS = ("x", "yh", "yl", "core")
+CHIPS = ("core", "x", "yh", "yl")
 PAIR = ("yl", "core")
 TURN = [(2, 0), (0, 1), (1, 3), (3, 2)]
 BACK = [(b, a) for a, b in TURN]

time: 160 us -> 160 us (level)
  no operation moved by 1% of the time
where the time goes in v7:
time: 160 us; the launch traced here: 159 us
  starting transfers between devices  70.7 us (44%)
  blocking collectives  37.8 us (24%)
  waiting for transfers between devices  23.5 us (15%)
  Pallas kernels  16.1 us (10%)
  local copies, waits for them, and re-layouts  5.75 us (4%)
  other arithmetic  3.08 us (2%)
    all_to_all x5, starting transfers between devices, swap(): return lax.all_to_all(x, axis, split_axis=0, concat_axis=0, tiled=True)  42 us
    all_to_all x2, blocking collectives, swap(): return lax.all_to_all(x, axis, split_axis=0, concat_axis=0, tiled=True)  37.8 us
    all_to_all x5, waiting for transfers between devices, swap(): return lax.all_to_all(x, axis, split_axis=0, concat_axis=0, tiled=True)  21.5 us
    pallas_call x10, Pallas kernels, call(): pl.pallas_call(kernel, out_shape=[*outs, *(pltpu.HBM(a.shape, a.dtype) fo...  16.1 us
    ppermute x1, starting transfers between devices, local(): other = lax.ppermute(mine, 'core', OTHER)  9.6 us
    ppermute x1, starting transfers between devices, local(): given = lax.ppermute(given, 'core', OTHER)  6.53 us
    ppermute x1, starting transfers between devices, local(): home_in = lax.ppermute(home_in, PAIR, BACK)  5.79 us
    unnamed x24, local copies, waits for them, and re-layouts  4.73 us
  transfers between devices with their start and end apart: 10, of which 7 were waited for; matrix products, arithmetic and copies ran while one was open for 1% of the time, Pallas kernels for 6%

profile of v7, /device:TPU:1, one launch (start us, length us, event | category | flops | bytes accessed | tf_op | source)
XLA Modules:
  0.0 158.7 jit_solution(14563768731158480657)
XLA Ops:
  0.7 0.0 copy-start.1
  0.7 2.8 %pad_maximum_fusion = bf16[640,1280]{1,0:T(8,128)(2,1)} fusion(bf16[320,1280]{1,0:T(8,128)(2,1)} %bitcast.37, bf16[320,1280]{1,0:T(8,128)(2,1)} %bitcast.38), kind=kLoop, calls=%fused_computation.2 | loop fusion | flops 3276800 | bytes 3276800 | tf_op jit(solution)/shard_map/concatenate | solution.py:198
  3.4 4.0 %collective-permute-start = (bf16[640,1280]{1,0:T(8,128)(2,1)}, bf16[640,1280]{1,0:T(8,128)(2,1)S(1)}, u32[]{:S(2)}, u32[]{:S(2)}) collective-permute-start(bf16[640,1280]{1,0:T(8,128)(2,1)} %pad_maximum_fusion), channel_id=1, source_target_pairs={{32,0},{0,1},{1,33},{33,32},{34,2},{2,3},{3,35},{35,34},{36,4},{4,... | collective-permute-start | bytes 4915208 | tf_op jit(solution)/shard_map/ppermute | solution.py:198
  7.5 0.4 fusion.14
  7.9 0.2 fusion.3
  8.1 0.5 copy-done.10
  8.6 0.2 convolution_convert_fusion.1
  8.9 0.1 stack_reshape.6
  8.9 0.2 convolution_convert_fusion
  9.2 0.8 copy.16
  10.0 14.9 %all-to-all-start = ((bf16[16,4,1280]{2,1,0:T(4,128)(2,1)}), bf16[16,4,1280]{2,1,0:T(4,128)(2,1)S(1)}, u32[]{:S(2)}, u32[]{:S(2)}) async-start(bf16[16,4,1280]{2,1,0:T(4,128)(2,1)} %copy.16), calls=%async_computation | async-start | bytes 327680 | tf_op jit(solution)/shard_map/all_to_all | solution.py:177
  24.9 0.9 collective-permute-done.mine
  25.8 9.6 %collective-permute-start.1 = (bf16[640,1280]{1,0:T(8,128)(2,1)S(1)}, bf16[640,1280]{1,0:T(8,128)(2,1)}, u32[]{:S(2)}, u32[]{:S(2)}) collective-permute-start(bf16[640,1280]{1,0:T(8,128)(2,1)S(1)} %collective-permute-done.mine), channel_id=1, source_target_pairs={{0,1},{1,0},{2,3},{3,2},{4,5},{5,4},{6,7},{7,6},{8,9},{9,8},{10,11... | collective-permute-start | bytes 4915208 | tf_op jit(solution)/shard_map/ppermute | solution.py:200
  35.4 2.9 %all-to-all-done = bf16[16,4,1280]{2,1,0:T(4,128)(2,1)S(1)} async-done(((bf16[16,4,1280]{2,1,0:T(4,128)(2,1)}), bf16[16,4,1280]{2,1,0:T(4,128)(2,1)S(1)}, u32[]{:S(2)}, u32[]{:S(2)}) %all-to-all-start) | async-done | bytes 163872 | tf_op jit(solution)/shard_map/all_to_all | solution.py:177
  38.3 0.1 broadcast_in_dim.21
  38.5 21.8 %all_to_all.35.every = bf16[16,32,1280]{2,1,0:T(8,128)(2,1)S(1)} all-to-all(bf16[16,32,1280]{2,1,0:T(8,128)(2,1)S(1)} %bitcast.36), channel_id=1, replica_groups=mesh['x'=4,'yh'=2,'yl'=2,'z'=16,'core'=2] {'x','yh','yl'}, dimensions={0} | all-to-all | bytes 2621440 | tf_op jit(solution)/shard_map/all_to_all | solution.py:177
  60.3 0.0 collective-permute-done.1.other
  60.3 4.7 %shard_map.84 = (bf16[16,32,1280]{2,1,0:T(8,128)(2,1)}, bf16[16,32,1280]{2,1,0:T(8,128)(2,1)}, bf16[2,256,320]{2,1,0:T(8,128)(2,1)}, bf16[2,256,320]{2,1,0:T(8,128)(2,1)}) custom-call(bf16[16,32,1280]{2,1,0:T(8,128)(2,1)S(1)} %all_to_all.35.every, bf16[640,1280]{1,0:T(8,128)(2,1)S(1)} %collective-permute-done.mine, ...), custom_call_target="tpu_custom_call" | custom-call | flops 1677721600 | bytes 7864320 | tf_op jit(solution)/shard_map/pallas_call | solution.py:161
  65.0 3.7 %all-to-all-start.2 = ((bf16[16,32,1280]{2,1,0:T(8,128)(2,1)}), bf16[16,32,1280]{2,1,0:T(8,128)(2,1)S(1)}, u32[]{:S(2)}, u32[]{:S(2)}) async-start(bf16[16,32,1280]{2,1,0:T(8,128)(2,1)} %get-tuple-element.23), calls=%async_computation.2 | async-start | bytes 2621440 | tf_op jit(solution)/shard_map/all_to_all | solution.py:177
  68.7 1.3 copy-done.5
  70.0 1.0 copy-done.6
  71.0 1.0 copy-done.7
  72.0 2.2 %shard_map.88 = (bf16[640,1280]{1,0:T(8,128)(2,1)S(1)}, bf16[640,1280]{1,0:T(8,128)(2,1)}) custom-call(bf16[16,32,1280]{2,1,0:T(8,128)(2,1)S(1)} %copy-done.5, bf16[2,256,320]{2,1,0:T(8,128)(2,1)S(1)} %copy-done.6, bf16[2,256,320]{2,1,0:T(8,128)(2,1)S(1)} %copy-done.7), custom_call_target="tpu_custom_call" | custom-call | flops 838860800 | bytes 5242880 | tf_op jit(solution)/shard_map/pallas_call | solution.py:161
  74.3 6.5 %collective-permute-start.2 = (bf16[640,1280]{1,0:T(8,128)(2,1)}, bf16[640,1280]{1,0:T(8,128)(2,1)}, u32[]{:S(2)}, u32[]{:S(2)}) collective-permute-start(bf16[640,1280]{1,0:T(8,128)(2,1)} %get-tuple-element.31), channel_id=1, source_target_pairs={{0,1},{1,0},{2,3},{3,2},{4,5},{5,4},{6,7},{7,6},{8,9},{9,8},{10,11... | collective-permute-start | bytes 4915208 | tf_op jit(solution)/shard_map/ppermute | solution.py:223
  80.8 2.3 %all-to-all-done.2.terms = bf16[16,32,1280]{2,1,0:T(8,128)(2,1)S(1)} async-done(((bf16[16,32,1280]{2,1,0:T(8,128)(2,1)}), bf16[16,32,1280]{2,1,0:T(8,128)(2,1)S(1)}, u32[]{:S(2)}, u32[]{:S(2)}) %all-to-all-start.2) | async-done | bytes 1310752 | tf_op jit(solution)/shard_map/all_to_all | solution.py:177
  83.1 1.0 shard_map.85
  84.1 13.9 %all-to-all-start.3 = ((bf16[16,4,1280]{2,1,0:T(4,128)(2,1)}), bf16[16,4,1280]{2,1,0:T(4,128)(2,1)S(1)}, u32[]{:S(2)}, u32[]{:S(2)}) async-start(bf16[16,4,1280]{2,1,0:T(4,128)(2,1)} %shard_map.85), calls=%async_computation.3 | async-start | bytes 327680 | tf_op jit(solution)/shard_map/all_to_all | solution.py:177
  98.0 0.0 collective-permute-done.2.given
  98.1 0.0 copy-start.2
  98.1 2.6 %shard_map.89 = (bf16[320,1280]{1,0:T(8,128)(2,1)}, bf16[320,1280]{1,0:T(8,128)(2,1)S(1)}) custom-call(bf16[640,1280]{1,0:T(8,128)(2,1)S(1)} %get-tuple-element.30.kept, bf16[640,1280]{1,0:T(8,128)(2,1)} %collective-permute-done.2.given), custom_call_target="tpu_custom_call" | custom-call | flops 819200 | bytes 4915200 | tf_op jit(solution)/shard_map/pallas_call | solution.py:161
  100.6 0.9 copy-done.4
  101.5 5.8 %collective-permute-start.3 = (bf16[320,1280]{1,0:T(8,128)(2,1)}, bf16[320,1280]{1,0:T(8,128)(2,1)S(1)}, u32[]{:S(2)}, u32[]{:S(2)}) collective-permute-start(bf16[320,1280]{1,0:T(8,128)(2,1)} %get-tuple-element.32), channel_id=1, source_target_pairs={{0,32},{1,0},{33,1},{32,33},{2,34},{3,2},{35,3},{34,35},{4,36},{5,... | collective-permute-start | bytes 2457608 | tf_op jit(solution)/shard_map/ppermute | solution.py:235
  107.3 0.1 fusion.6
  107.4 2.8 %all-to-all-done.3.back = bf16[16,4,1280]{2,1,0:T(4,128)(2,1)S(1)} async-done(((bf16[16,4,1280]{2,1,0:T(4,128)(2,1)}), bf16[16,4,1280]{2,1,0:T(4,128)(2,1)S(1)}, u32[]{:S(2)}, u32[]{:S(2)}) %all-to-all-start.3) | async-done | bytes 163872 | tf_op jit(solution)/shard_map/all_to_all | solution.py:177
  110.2 1.0 shard_map.86
  111.2 16.0 %all_to_all.36.parts = bf16[32,2,640]{2,1,0:T(2,128)(2,1)S(1)} all-to-all(bf16[32,2,640]{2,1,0:T(2,128)(2,1)S(1)} %get-tuple-element.26), channel_id=1, replica_groups=mesh['x'=4,'yh'=2,'yl'=2,'z'=16,'core'=2] {'core','x','yh','yl'}, dimensions={0} | all-to-all | bytes 163840 | tf_op jit(solution)/shard_map/all_to_all | solution.py:177
  127.2 0.0 collective-permute-done.3.a
  127.2 0.7 shard_map.90
  127.9 4.2 %all-to-all-start.5 = ((bf16[16,2,640]{2,1,0:T(2,128)(2,1)}), bf16[16,2,640]{2,1,0:T(2,128)(2,1)S(1)}, u32[]{:S(2)}, u32[]{:S(2)}) async-start(bf16[16,2,640]{2,1,0:T(2,128)(2,1)} %shard_map.90), calls=%async_computation.5 | async-start | bytes 81920 | tf_op jit(solution)/shard_map/all_to_all | solution.py:177
  132.2 2.7 %collective-permute-start.4 = (bf16[320,1280]{1,0:T(8,128)(2,1)}, bf16[320,1280]{1,0:T(8,128)(2,1)S(1)}, u32[]{:S(2)}, u32[]{:S(2)}) collective-permute-start(bf16[320,1280]{1,0:T(8,128)(2,1)} %copy-done.4), channel_id=1, source_target_pairs={{0,32},{1,0},{33,1},{32,33},{2,34},{3,2},{35,3},{34,35},{4,36},{5,... | collective-permute-start | bytes 2457608 | tf_op jit(solution)/shard_map/ppermute | solution.py:250
  134.9 8.8 %all-to-all-done.5.parts = bf16[16,2,640]{2,1,0:T(2,128)(2,1)S(1)} async-done(((bf16[16,2,640]{2,1,0:T(2,128)(2,1)}), bf16[16,2,640]{2,1,0:T(2,128)(2,1)S(1)}, u32[]{:S(2)}, u32[]{:S(2)}) %all-to-all-start.5) | async-done | bytes 40992 | tf_op jit(solution)/shard_map/all_to_all | solution.py:177
  143.7 0.7 shard_map.91
  144.4 1.1 collective-permute-done.4.b
  145.5 5.2 %all-to-all-start.6 = ((bf16[32,2,640]{2,1,0:T(2,128)(2,1)}), bf16[32,2,640]{2,1,0:T(2,128)(2,1)S(1)}, u32[]{:S(2)}, u32[]{:S(2)}) async-start(bf16[32,2,640]{2,1,0:T(2,128)(2,1)} %shard_map.91), calls=%async_computation.6 | async-start | bytes 163840 | tf_op jit(solution)/shard_map/all_to_all | solution.py:177
  150.7 1.2 shard_map.87
  152.0 1.3 shard_map.93
  153.2 4.7 %all-to-all-done.6.parts = bf16[32,2,640]{2,1,0:T(2,128)(2,1)S(1)} async-done(((bf16[32,2,640]{2,1,0:T(2,128)(2,1)}), bf16[32,2,640]{2,1,0:T(2,128)(2,1)S(1)}, u32[]{:S(2)}, u32[]{:S(2)}) %all-to-all-start.6) | async-done | bytes 81952 | tf_op jit(solution)/shard_map/all_to_all | solution.py:177
  157.9 0.7 shard_map.92
  (22 shorter events, 0.1 us)
Async XLA Ops:
  0.6 6.8 %copy-start = (bf16[1,196,1280]{2,1,0:T(8,128)(2,1)S(1)}, bf16[1,196,1280]{2,1,0:T(8,128)(2,1)}, u32[]{:S(2)}) copy-start(bf16[1,196,1280]{2,1,0:T(8,128)(2,1)} %param.5) | copy-start | bytes 1505284
  0.6 6.8 %copy-start.3 = (bf16[1280,32]{0,1:T(8,128)(2,1)S(1)}, bf16[1280,32]{0,1:T(8,128)(2,1)}, u32[]{:S(2)}) copy-start(bf16[1280,32]{0,1:T(8,128)(2,1)} %param.6) | copy-start | bytes 245764
  0.7 8.3 %copy-start.1 = (bf16[1,196,1280]{2,1,0:T(8,128)(2,1)S(1)}, bf16[1,196,1280]{2,1,0:T(8,128)(2,1)}, u32[]{:S(2)}) copy-start(bf16[1,196,1280]{2,1,0:T(8,128)(2,1)} %param.9) | copy-start | bytes 1505284
  3.4 22.4 %collective-permute-start = (bf16[640,1280]{1,0:T(8,128)(2,1)}, bf16[640,1280]{1,0:T(8,128)(2,1)S(1)}, u32[]{:S(2)}, u32[]{:S(2)}) collective-permute-start(bf16[640,1280]{1,0:T(8,128)(2,1)} %pad_maximum_fusion), channel_id=1, source_target_pairs={{32,0},{0,1},{1,33},{33,32},{34,2},{2,3},{3,35},{35,34},{36,4},{4,... | collective-permute-start | bytes 4915208 | tf_op jit(solution)/shard_map/ppermute | solution.py:198
  7.9 30.6 %copy-start.8 = (f32[196,32]{0,1:T(8,128)}, f32[196,32]{0,1:T(8,128)S(1)}, u32[]{:S(2)}) copy-start(f32[196,32]{0,1:T(8,128)S(1)} %get-tuple-element.48) | copy-start | bytes 75268
  8.1 0.5 copy-start.10
  10.0 28.3 %all-to-all-start = ((bf16[16,4,1280]{2,1,0:T(4,128)(2,1)}), bf16[16,4,1280]{2,1,0:T(4,128)(2,1)S(1)}, u32[]{:S(2)}, u32[]{:S(2)}) async-start(bf16[16,4,1280]{2,1,0:T(4,128)(2,1)} %copy.16), calls=%async_computation | async-start | bytes 327680 | tf_op jit(solution)/shard_map/all_to_all | solution.py:177
  25.8 34.5 %collective-permute-start.1 = (bf16[640,1280]{1,0:T(8,128)(2,1)S(1)}, bf16[640,1280]{1,0:T(8,128)(2,1)}, u32[]{:S(2)}, u32[]{:S(2)}) collective-permute-start(bf16[640,1280]{1,0:T(8,128)(2,1)S(1)} %collective-permute-done.mine), channel_id=1, source_target_pairs={{0,1},{1,0},{2,3},{3,2},{4,5},{5,4},{6,7},{7,6},{8,9},{9,8},{10,11... | collective-permute-start | bytes 4915208 | tf_op jit(solution)/shard_map/ppermute | solution.py:200
  65.0 18.1 %all-to-all-start.2 = ((bf16[16,32,1280]{2,1,0:T(8,128)(2,1)}), bf16[16,32,1280]{2,1,0:T(8,128)(2,1)S(1)}, u32[]{:S(2)}, u32[]{:S(2)}) async-start(bf16[16,32,1280]{2,1,0:T(8,128)(2,1)} %get-tuple-element.23), calls=%async_computation.2 | async-start | bytes 2621440 | tf_op jit(solution)/shard_map/all_to_all | solution.py:177
  68.7 1.3 copy-start.5
  70.0 1.0 copy-start.6
  71.0 1.0 copy-start.7
  74.3 23.8 %collective-permute-start.2 = (bf16[640,1280]{1,0:T(8,128)(2,1)}, bf16[640,1280]{1,0:T(8,128)(2,1)}, u32[]{:S(2)}, u32[]{:S(2)}) collective-permute-start(bf16[640,1280]{1,0:T(8,128)(2,1)} %get-tuple-element.31), channel_id=1, source_target_pairs={{0,1},{1,0},{2,3},{3,2},{4,5},{5,4},{6,7},{7,6},{8,9},{9,8},{10,11... | collective-permute-start | bytes 4915208 | tf_op jit(solution)/shard_map/ppermute | solution.py:223
  84.1 26.1 %all-to-all-start.3 = ((bf16[16,4,1280]{2,1,0:T(4,128)(2,1)}), bf16[16,4,1280]{2,1,0:T(4,128)(2,1)S(1)}, u32[]{:S(2)}, u32[]{:S(2)}) async-start(bf16[16,4,1280]{2,1,0:T(4,128)(2,1)} %shard_map.85), calls=%async_computation.3 | async-start | bytes 327680 | tf_op jit(solution)/shard_map/all_to_all | solution.py:177
  98.0 9.3 %copy-start.9 = (f32[196,32]{0,1:T(8,128)S(1)}, f32[196,32]{0,1:T(8,128)}, u32[]{:S(2)}) copy-start(f32[196,32]{0,1:T(8,128)} %copy-done.8) | copy-start | bytes 75268
  98.1 9.3 %copy-start.11 = (f32[32]{0:T(128)S(1)}, f32[32]{0:T(128)}, u32[]{:S(2)}) copy-start(f32[32]{0:T(128)} %copy-done.10) | copy-start | bytes 388
  98.1 12.1 %copy-start.2 = (bf16[1,196,1280]{2,1,0:T(8,128)(2,1)S(1)}, bf16[1,196,1280]{2,1,0:T(8,128)(2,1)}, u32[]{:S(2)}) copy-start(bf16[1,196,1280]{2,1,0:T(8,128)(2,1)} %param.9) | copy-start | bytes 1505284
  100.6 0.9 copy-start.4
  101.5 25.7 %collective-permute-start.3 = (bf16[320,1280]{1,0:T(8,128)(2,1)}, bf16[320,1280]{1,0:T(8,128)(2,1)S(1)}, u32[]{:S(2)}, u32[]{:S(2)}) collective-permute-start(bf16[320,1280]{1,0:T(8,128)(2,1)} %get-tuple-element.32), channel_id=1, source_target_pairs={{0,32},{1,0},{33,1},{32,33},{2,34},{3,2},{35,3},{34,35},{4,36},{5,... | collective-permute-start | bytes 2457608 | tf_op jit(solution)/shard_map/ppermute | solution.py:235
  127.9 15.8 %all-to-all-start.5 = ((bf16[16,2,640]{2,1,0:T(2,128)(2,1)}), bf16[16,2,640]{2,1,0:T(2,128)(2,1)S(1)}, u32[]{:S(2)}, u32[]{:S(2)}) async-start(bf16[16,2,640]{2,1,0:T(2,128)(2,1)} %shard_map.90), calls=%async_computation.5 | async-start | bytes 81920 | tf_op jit(solution)/shard_map/all_to_all | solution.py:177
  132.2 13.3 %collective-permute-start.4 = (bf16[320,1280]{1,0:T(8,128)(2,1)}, bf16[320,1280]{1,0:T(8,128)(2,1)S(1)}, u32[]{:S(2)}, u32[]{:S(2)}) collective-permute-start(bf16[320,1280]{1,0:T(8,128)(2,1)} %copy-done.4), channel_id=1, source_target_pairs={{0,32},{1,0},{33,1},{32,33},{2,34},{3,2},{35,3},{34,35},{4,36},{5,... | collective-permute-start | bytes 2457608 | tf_op jit(solution)/shard_map/ppermute | solution.py:250
  145.5 12.4 %all-to-all-start.6 = ((bf16[32,2,640]{2,1,0:T(2,128)(2,1)}), bf16[32,2,640]{2,1,0:T(2,128)(2,1)S(1)}, u32[]{:S(2)}, u32[]{:S(2)}) async-start(bf16[32,2,640]{2,1,0:T(2,128)(2,1)} %shard_map.91), calls=%async_computation.6 | async-start | bytes 163840 | tf_op jit(solution)/shard_map/all_to_all | solution.py:177

commit v8 on v7

--- a/solution.py
+++ b/solution.py
@@ -59,15 +59,17 @@
         if i == 0:
             a, b = mine[:hid], mine[hid:]
         else:
-            for load in loads:
-                load.wait()
-            saves.append(pltpu.make_async_copy(every, rows, sems.at[2]))
-            saves[-1].start()
-            a, b = win[...], wout[...]
+            loads[0].wait()
+            a = win[...]
         pre = nt(x, a)
         cdf = 0.5 * (1.0 + lax.erf(pre * 0.7071067811865476))
         h_part[i] = (pre * cdf).astype(BF)
         slope = cdf + pre * jnp.exp(-0.5 * pre * pre) * 0.3989422804014327
+        if i == 1:
+            loads[1].wait()
+            saves.append(pltpu.make_async_copy(every, rows, sems.at[2]))
+            saves[-1].start()
+            b = wout[...]
         g_part[i] = (nt(g, b) * slope).astype(BF)
         saves.append(pltpu.make_async_copy(h_part.at[i], hidden.at[i], sems.at[3 + 2 * i]))
         saves.append(pltpu.make_async_copy(g_part.at[i], g_pre.at[i], sems.at[4 + 2 * i]))

time: 160 us -> 160 us (level)
  no operation moved by 1% of the time
where the time goes in v8:
time: 160 us; the launch traced here: 159 us
  starting transfers between devices  70.6 us (44%)
  blocking collectives  37.8 us (24%)
  waiting for transfers between devices  23.5 us (15%)
  Pallas kernels  16.1 us (10%)
  local copies, waits for them, and re-layouts  5.75 us (4%)
  other arithmetic  3.08 us (2%)
    all_to_all x5, starting transfers between devices, swap(): return lax.all_to_all(x, axis, split_axis=0, concat_axis=0, tiled=True)  42 us
    all_to_all x2, blocking collectives, swap(): return lax.all_to_all(x, axis, split_axis=0, concat_axis=0, tiled=True)  37.8 us
    all_to_all x5, waiting for transfers between devices, swap(): return lax.all_to_all(x, axis, split_axis=0, concat_axis=0, tiled=True)  21.5 us
    pallas_call x10, Pallas kernels, call(): pl.pallas_call(kernel, out_shape=[*outs, *(pltpu.HBM(a.shape, a.dtype) fo...  16.1 us
    ppermute x1, starting transfers between devices, local(): other = lax.ppermute(mine, 'core', OTHER)  9.6 us
    ppermute x1, starting transfers between devices, local(): given = lax.ppermute(given, 'core', OTHER)  6.52 us
    ppermute x1, starting transfers between devices, local(): home_in = lax.ppermute(home_in, PAIR, BACK)  5.79 us
    unnamed x24, local copies, waits for them, and re-layouts  4.73 us
  transfers between devices with their start and end apart: 10, of which 7 were waited for; matrix products, arithmetic and copies ran while one was open for 1% of the time, Pallas kernels for 6%

profile of v8, /device:TPU:1, one launch (start us, length us, event | category | flops | bytes accessed | tf_op | source)
XLA Modules:
  0.0 158.7 jit_solution(10047450973923850712)
XLA Ops:
  0.7 0.0 copy-start.1
  0.7 2.8 %pad_maximum_fusion = bf16[640,1280]{1,0:T(8,128)(2,1)} fusion(bf16[320,1280]{1,0:T(8,128)(2,1)} %bitcast.37, bf16[320,1280]{1,0:T(8,128)(2,1)} %bitcast.38), kind=kLoop, calls=%fused_computation.2 | loop fusion | flops 3276800 | bytes 3276800 | tf_op jit(solution)/shard_map/concatenate | solution.py:200
  3.4 4.0 %collective-permute-start = (bf16[640,1280]{1,0:T(8,128)(2,1)}, bf16[640,1280]{1,0:T(8,128)(2,1)S(1)}, u32[]{:S(2)}, u32[]{:S(2)}) collective-permute-start(bf16[640,1280]{1,0:T(8,128)(2,1)} %pad_maximum_fusion), channel_id=1, source_target_pairs={{32,0},{0,1},{1,33},{33,32},{34,2},{2,3},{3,35},{35,34},{36,4},{4,... | collective-permute-start | bytes 4915208 | tf_op jit(solution)/shard_map/ppermute | solution.py:200
  7.5 0.4 fusion.14
  7.9 0.2 fusion.3
  8.1 0.5 copy-done.10
  8.6 0.2 convolution_convert_fusion.1
  8.9 0.1 stack_reshape.6
  8.9 0.2 convolution_convert_fusion
  9.2 0.8 copy.16
  10.0 14.9 %all-to-all-start = ((bf16[16,4,1280]{2,1,0:T(4,128)(2,1)}), bf16[16,4,1280]{2,1,0:T(4,128)(2,1)S(1)}, u32[]{:S(2)}, u32[]{:S(2)}) async-start(bf16[16,4,1280]{2,1,0:T(4,128)(2,1)} %copy.16), calls=%async_computation | async-start | bytes 327680 | tf_op jit(solution)/shard_map/all_to_all | solution.py:179
  24.9 0.9 collective-permute-done.mine
  25.8 9.6 %collective-permute-start.1 = (bf16[640,1280]{1,0:T(8,128)(2,1)S(1)}, bf16[640,1280]{1,0:T(8,128)(2,1)}, u32[]{:S(2)}, u32[]{:S(2)}) collective-permute-start(bf16[640,1280]{1,0:T(8,128)(2,1)S(1)} %collective-permute-done.mine), channel_id=1, source_target_pairs={{0,1},{1,0},{2,3},{3,2},{4,5},{5,4},{6,7},{7,6},{8,9},{9,8},{10,11... | collective-permute-start | bytes 4915208 | tf_op jit(solution)/shard_map/ppermute | solution.py:202
  35.4 2.9 %all-to-all-done = bf16[16,4,1280]{2,1,0:T(4,128)(2,1)S(1)} async-done(((bf16[16,4,1280]{2,1,0:T(4,128)(2,1)}), bf16[16,4,1280]{2,1,0:T(4,128)(2,1)S(1)}, u32[]{:S(2)}, u32[]{:S(2)}) %all-to-all-start) | async-done | bytes 163872 | tf_op jit(solution)/shard_map/all_to_all | solution.py:179
  38.3 0.1 broadcast_in_dim.21
  38.5 21.8 %all_to_all.35.every = bf16[16,32,1280]{2,1,0:T(8,128)(2,1)S(1)} all-to-all(bf16[16,32,1280]{2,1,0:T(8,128)(2,1)S(1)} %bitcast.36), channel_id=1, replica_groups=mesh['x'=4,'yh'=2,'yl'=2,'z'=16,'core'=2] {'x','yh','yl'}, dimensions={0} | all-to-all | bytes 2621440 | tf_op jit(solution)/shard_map/all_to_all | solution.py:179
  60.3 0.0 collective-permute-done.1.other
  60.3 4.7 %shard_map.84 = (bf16[16,32,1280]{2,1,0:T(8,128)(2,1)}, bf16[16,32,1280]{2,1,0:T(8,128)(2,1)}, bf16[2,256,320]{2,1,0:T(8,128)(2,1)}, bf16[2,256,320]{2,1,0:T(8,128)(2,1)}) custom-call(bf16[16,32,1280]{2,1,0:T(8,128)(2,1)S(1)} %all_to_all.35.every, bf16[640,1280]{1,0:T(8,128)(2,1)S(1)} %collective-permute-done.mine, ...), custom_call_target="tpu_custom_call" | custom-call | flops 1677721600 | bytes 7864320 | tf_op jit(solution)/shard_map/pallas_call | solution.py:163
  65.0 3.7 %all-to-all-start.2 = ((bf16[16,32,1280]{2,1,0:T(8,128)(2,1)}), bf16[16,32,1280]{2,1,0:T(8,128)(2,1)S(1)}, u32[]{:S(2)}, u32[]{:S(2)}) async-start(bf16[16,32,1280]{2,1,0:T(8,128)(2,1)} %get-tuple-element.23), calls=%async_computation.2 | async-start | bytes 2621440 | tf_op jit(solution)/shard_map/all_to_all | solution.py:179
  68.7 1.3 copy-done.5
  70.0 1.0 copy-done.6
  71.0 1.0 copy-done.7
  72.0 2.2 %shard_map.88 = (bf16[640,1280]{1,0:T(8,128)(2,1)S(1)}, bf16[640,1280]{1,0:T(8,128)(2,1)}) custom-call(bf16[16,32,1280]{2,1,0:T(8,128)(2,1)S(1)} %copy-done.5, bf16[2,256,320]{2,1,0:T(8,128)(2,1)S(1)} %copy-done.6, bf16[2,256,320]{2,1,0:T(8,128)(2,1)S(1)} %copy-done.7), custom_call_target="tpu_custom_call" | custom-call | flops 838860800 | bytes 5242880 | tf_op jit(solution)/shard_map/pallas_call | solution.py:163
  74.3 6.5 %collective-permute-start.2 = (bf16[640,1280]{1,0:T(8,128)(2,1)}, bf16[640,1280]{1,0:T(8,128)(2,1)}, u32[]{:S(2)}, u32[]{:S(2)}) collective-permute-start(bf16[640,1280]{1,0:T(8,128)(2,1)} %get-tuple-element.31), channel_id=1, source_target_pairs={{0,1},{1,0},{2,3},{3,2},{4,5},{5,4},{6,7},{7,6},{8,9},{9,8},{10,11... | collective-permute-start | bytes 4915208 | tf_op jit(solution)/shard_map/ppermute | solution.py:225
  80.8 2.3 %all-to-all-done.2.terms = bf16[16,32,1280]{2,1,0:T(8,128)(2,1)S(1)} async-done(((bf16[16,32,1280]{2,1,0:T(8,128)(2,1)}), bf16[16,32,1280]{2,1,0:T(8,128)(2,1)S(1)}, u32[]{:S(2)}, u32[]{:S(2)}) %all-to-all-start.2) | async-done | bytes 1310752 | tf_op jit(solution)/shard_map/all_to_all | solution.py:179
  83.1 1.0 shard_map.85
  84.1 13.9 %all-to-all-start.3 = ((bf16[16,4,1280]{2,1,0:T(4,128)(2,1)}), bf16[16,4,1280]{2,1,0:T(4,128)(2,1)S(1)}, u32[]{:S(2)}, u32[]{:S(2)}) async-start(bf16[16,4,1280]{2,1,0:T(4,128)(2,1)} %shard_map.85), calls=%async_computation.3 | async-start | bytes 327680 | tf_op jit(solution)/shard_map/all_to_all | solution.py:179
  98.0 0.0 collective-permute-done.2.given
  98.1 0.0 copy-start.2
  98.1 2.6 %shard_map.89 = (bf16[320,1280]{1,0:T(8,128)(2,1)}, bf16[320,1280]{1,0:T(8,128)(2,1)S(1)}) custom-call(bf16[640,1280]{1,0:T(8,128)(2,1)S(1)} %get-tuple-element.30.kept, bf16[640,1280]{1,0:T(8,128)(2,1)} %collective-permute-done.2.given), custom_call_target="tpu_custom_call" | custom-call | flops 819200 | bytes 4915200 | tf_op jit(solution)/shard_map/pallas_call | solution.py:163
  100.6 0.9 copy-done.4
  101.5 5.8 %collective-permute-start.3 = (bf16[320,1280]{1,0:T(8,128)(2,1)}, bf16[320,1280]{1,0:T(8,128)(2,1)S(1)}, u32[]{:S(2)}, u32[]{:S(2)}) collective-permute-start(bf16[320,1280]{1,0:T(8,128)(2,1)} %get-tuple-element.32), channel_id=1, source_target_pairs={{0,32},{1,0},{33,1},{32,33},{2,34},{3,2},{35,3},{34,35},{4,36},{5,... | collective-permute-start | bytes 2457608 | tf_op jit(solution)/shard_map/ppermute | solution.py:237
  107.3 0.1 fusion.6
  107.4 2.7 %all-to-all-done.3.back = bf16[16,4,1280]{2,1,0:T(4,128)(2,1)S(1)} async-done(((bf16[16,4,1280]{2,1,0:T(4,128)(2,1)}), bf16[16,4,1280]{2,1,0:T(4,128)(2,1)S(1)}, u32[]{:S(2)}, u32[]{:S(2)}) %all-to-all-start.3) | async-done | bytes 163872 | tf_op jit(solution)/shard_map/all_to_all | solution.py:179
  110.2 1.0 shard_map.86
  111.2 16.0 %all_to_all.36.parts = bf16[32,2,640]{2,1,0:T(2,128)(2,1)S(1)} all-to-all(bf16[32,2,640]{2,1,0:T(2,128)(2,1)S(1)} %get-tuple-element.26), channel_id=1, replica_groups=mesh['x'=4,'yh'=2,'yl'=2,'z'=16,'core'=2] {'core','x','yh','yl'}, dimensions={0} | all-to-all | bytes 163840 | tf_op jit(solution)/shard_map/all_to_all | solution.py:179
  127.2 0.0 collective-permute-done.3.a
  127.2 0.7 shard_map.90
  127.9 4.2 %all-to-all-start.5 = ((bf16[16,2,640]{2,1,0:T(2,128)(2,1)}), bf16[16,2,640]{2,1,0:T(2,128)(2,1)S(1)}, u32[]{:S(2)}, u32[]{:S(2)}) async-start(bf16[16,2,640]{2,1,0:T(2,128)(2,1)} %shard_map.90), calls=%async_computation.5 | async-start | bytes 81920 | tf_op jit(solution)/shard_map/all_to_all | solution.py:179
  132.2 2.7 %collective-permute-start.4 = (bf16[320,1280]{1,0:T(8,128)(2,1)}, bf16[320,1280]{1,0:T(8,128)(2,1)S(1)}, u32[]{:S(2)}, u32[]{:S(2)}) collective-permute-start(bf16[320,1280]{1,0:T(8,128)(2,1)} %copy-done.4), channel_id=1, source_target_pairs={{0,32},{1,0},{33,1},{32,33},{2,34},{3,2},{35,3},{34,35},{4,36},{5,... | collective-permute-start | bytes 2457608 | tf_op jit(solution)/shard_map/ppermute | solution.py:252
  134.9 8.8 %all-to-all-done.5.parts = bf16[16,2,640]{2,1,0:T(2,128)(2,1)S(1)} async-done(((bf16[16,2,640]{2,1,0:T(2,128)(2,1)}), bf16[16,2,640]{2,1,0:T(2,128)(2,1)S(1)}, u32[]{:S(2)}, u32[]{:S(2)}) %all-to-all-start.5) | async-done | bytes 40992 | tf_op jit(solution)/shard_map/all_to_all | solution.py:179
  143.7 0.7 shard_map.91
  144.4 1.1 collective-permute-done.4.b
  145.5 5.2 %all-to-all-start.6 = ((bf16[32,2,640]{2,1,0:T(2,128)(2,1)}), bf16[32,2,640]{2,1,0:T(2,128)(2,1)S(1)}, u32[]{:S(2)}, u32[]{:S(2)}) async-start(bf16[32,2,640]{2,1,0:T(2,128)(2,1)} %shard_map.91), calls=%async_computation.6 | async-start | bytes 163840 | tf_op jit(solution)/shard_map/all_to_all | solution.py:179
  150.7 1.2 shard_map.87
  152.0 1.3 shard_map.93
  153.2 4.7 %all-to-all-done.6.parts = bf16[32,2,640]{2,1,0:T(2,128)(2,1)S(1)} async-done(((bf16[32,2,640]{2,1,0:T(2,128)(2,1)}), bf16[32,2,640]{2,1,0:T(2,128)(2,1)S(1)}, u32[]{:S(2)}, u32[]{:S(2)}) %all-to-all-start.6) | async-done | bytes 81952 | tf_op jit(solution)/shard_map/all_to_all | solution.py:179
  157.9 0.7 shard_map.92
  (22 shorter events, 0.1 us)
Async XLA Ops:
  0.6 6.8 %copy-start = (bf16[1,196,1280]{2,1,0:T(8,128)(2,1)S(1)}, bf16[1,196,1280]{2,1,0:T(8,128)(2,1)}, u32[]{:S(2)}) copy-start(bf16[1,196,1280]{2,1,0:T(8,128)(2,1)} %param.5) | copy-start | bytes 1505284
  0.6 6.8 %copy-start.3 = (bf16[1280,32]{0,1:T(8,128)(2,1)S(1)}, bf16[1280,32]{0,1:T(8,128)(2,1)}, u32[]{:S(2)}) copy-start(bf16[1280,32]{0,1:T(8,128)(2,1)} %param.6) | copy-start | bytes 245764
  0.7 8.3 %copy-start.1 = (bf16[1,196,1280]{2,1,0:T(8,128)(2,1)S(1)}, bf16[1,196,1280]{2,1,0:T(8,128)(2,1)}, u32[]{:S(2)}) copy-start(bf16[1,196,1280]{2,1,0:T(8,128)(2,1)} %param.9) | copy-start | bytes 1505284
  3.4 22.4 %collective-permute-start = (bf16[640,1280]{1,0:T(8,128)(2,1)}, bf16[640,1280]{1,0:T(8,128)(2,1)S(1)}, u32[]{:S(2)}, u32[]{:S(2)}) collective-permute-start(bf16[640,1280]{1,0:T(8,128)(2,1)} %pad_maximum_fusion), channel_id=1, source_target_pairs={{32,0},{0,1},{1,33},{33,32},{34,2},{2,3},{3,35},{35,34},{36,4},{4,... | collective-permute-start | bytes 4915208 | tf_op jit(solution)/shard_map/ppermute | solution.py:200
  7.9 30.6 %copy-start.8 = (f32[196,32]{0,1:T(8,128)}, f32[196,32]{0,1:T(8,128)S(1)}, u32[]{:S(2)}) copy-start(f32[196,32]{0,1:T(8,128)S(1)} %get-tuple-element.48) | copy-start | bytes 75268
  8.1 0.5 copy-start.10
  10.0 28.3 %all-to-all-start = ((bf16[16,4,1280]{2,1,0:T(4,128)(2,1)}), bf16[16,4,1280]{2,1,0:T(4,128)(2,1)S(1)}, u32[]{:S(2)}, u32[]{:S(2)}) async-start(bf16[16,4,1280]{2,1,0:T(4,128)(2,1)} %copy.16), calls=%async_computation | async-start | bytes 327680 | tf_op jit(solution)/shard_map/all_to_all | solution.py:179
  25.8 34.5 %collective-permute-start.1 = (bf16[640,1280]{1,0:T(8,128)(2,1)S(1)}, bf16[640,1280]{1,0:T(8,128)(2,1)}, u32[]{:S(2)}, u32[]{:S(2)}) collective-permute-start(bf16[640,1280]{1,0:T(8,128)(2,1)S(1)} %collective-permute-done.mine), channel_id=1, source_target_pairs={{0,1},{1,0},{2,3},{3,2},{4,5},{5,4},{6,7},{7,6},{8,9},{9,8},{10,11... | collective-permute-start | bytes 4915208 | tf_op jit(solution)/shard_map/ppermute | solution.py:202
  65.0 18.1 %all-to-all-start.2 = ((bf16[16,32,1280]{2,1,0:T(8,128)(2,1)}), bf16[16,32,1280]{2,1,0:T(8,128)(2,1)S(1)}, u32[]{:S(2)}, u32[]{:S(2)}) async-start(bf16[16,32,1280]{2,1,0:T(8,128)(2,1)} %get-tuple-element.23), calls=%async_computation.2 | async-start | bytes 2621440 | tf_op jit(solution)/shard_map/all_to_all | solution.py:179
  68.7 1.3 copy-start.5
  70.0 1.0 copy-start.6
  71.0 1.0 copy-start.7
  74.3 23.8 %collective-permute-start.2 = (bf16[640,1280]{1,0:T(8,128)(2,1)}, bf16[640,1280]{1,0:T(8,128)(2,1)}, u32[]{:S(2)}, u32[]{:S(2)}) collective-permute-start(bf16[640,1280]{1,0:T(8,128)(2,1)} %get-tuple-element.31), channel_id=1, source_target_pairs={{0,1},{1,0},{2,3},{3,2},{4,5},{5,4},{6,7},{7,6},{8,9},{9,8},{10,11... | collective-permute-start | bytes 4915208 | tf_op jit(solution)/shard_map/ppermute | solution.py:225
  84.1 26.1 %all-to-all-start.3 = ((bf16[16,4,1280]{2,1,0:T(4,128)(2,1)}), bf16[16,4,1280]{2,1,0:T(4,128)(2,1)S(1)}, u32[]{:S(2)}, u32[]{:S(2)}) async-start(bf16[16,4,1280]{2,1,0:T(4,128)(2,1)} %shard_map.85), calls=%async_computation.3 | async-start | bytes 327680 | tf_op jit(solution)/shard_map/all_to_all | solution.py:179
  98.0 9.3 %copy-start.9 = (f32[196,32]{0,1:T(8,128)S(1)}, f32[196,32]{0,1:T(8,128)}, u32[]{:S(2)}) copy-start(f32[196,32]{0,1:T(8,128)} %copy-done.8) | copy-start | bytes 75268
  98.0 9.3 %copy-start.11 = (f32[32]{0:T(128)S(1)}, f32[32]{0:T(128)}, u32[]{:S(2)}) copy-start(f32[32]{0:T(128)} %copy-done.10) | copy-start | bytes 388
  98.1 12.1 %copy-start.2 = (bf16[1,196,1280]{2,1,0:T(8,128)(2,1)S(1)}, bf16[1,196,1280]{2,1,0:T(8,128)(2,1)}, u32[]{:S(2)}) copy-start(bf16[1,196,1280]{2,1,0:T(8,128)(2,1)} %param.9) | copy-start | bytes 1505284
  100.6 0.9 copy-start.4
  101.5 25.7 %collective-permute-start.3 = (bf16[320,1280]{1,0:T(8,128)(2,1)}, bf16[320,1280]{1,0:T(8,128)(2,1)S(1)}, u32[]{:S(2)}, u32[]{:S(2)}) collective-permute-start(bf16[320,1280]{1,0:T(8,128)(2,1)} %get-tuple-element.32), channel_id=1, source_target_pairs={{0,32},{1,0},{33,1},{32,33},{2,34},{3,2},{35,3},{34,35},{4,36},{5,... | collective-permute-start | bytes 2457608 | tf_op jit(solution)/shard_map/ppermute | solution.py:237
  127.9 15.8 %all-to-all-start.5 = ((bf16[16,2,640]{2,1,0:T(2,128)(2,1)}), bf16[16,2,640]{2,1,0:T(2,128)(2,1)S(1)}, u32[]{:S(2)}, u32[]{:S(2)}) async-start(bf16[16,2,640]{2,1,0:T(2,128)(2,1)} %shard_map.90), calls=%async_computation.5 | async-start | bytes 81920 | tf_op jit(solution)/shard_map/all_to_all | solution.py:179
  132.2 13.3 %collective-permute-start.4 = (bf16[320,1280]{1,0:T(8,128)(2,1)}, bf16[320,1280]{1,0:T(8,128)(2,1)S(1)}, u32[]{:S(2)}, u32[]{:S(2)}) collective-permute-start(bf16[320,1280]{1,0:T(8,128)(2,1)} %copy-done.4), channel_id=1, source_target_pairs={{0,32},{1,0},{33,1},{32,33},{2,34},{3,2},{35,3},{34,35},{4,36},{5,... | collective-permute-start | bytes 2457608 | tf_op jit(solution)/shard_map/ppermute | solution.py:252
  145.5 12.4 %all-to-all-start.6 = ((bf16[32,2,640]{2,1,0:T(2,128)(2,1)}), bf16[32,2,640]{2,1,0:T(2,128)(2,1)S(1)}, u32[]{:S(2)}, u32[]{:S(2)}) async-start(bf16[32,2,640]{2,1,0:T(2,128)(2,1)} %shard_map.91), calls=%async_computation.6 | async-start | bytes 163840 | tf_op jit(solution)/shard_map/all_to_all | solution.py:179
